TPU v7x, 32 devices: a whole 2x2x4 slice. The times are simulated.
32 devices in a mesh: dp: 8 (over z, y), mp: 4 (over x, core).
Axes of the slice: x: 2, y: 2, z: 4, core: 2. Of those that a mesh axis runs over, the one named last changes fastest.
Arguments:
- stream_in: bfloat16 [8192, 768], P('dp'), may hold values from -12 to 12
- features: bfloat16 [128, 257, 1408], P('dp'), may hold values from -6 to 6
- image_index: int32 [8, 16], P('dp'), may hold values from 0 to 15, each once within a row
- text_segment: int32 [32, 128], P('dp'), may hold values from 0 to 3, never falling along the last dimension, each value on 1 to 64 neighbouring positions
- text_valid: int32 [32, 128], P('dp'), may hold values 0 or 1
- self_qkv: bfloat16 [3, 768, 768], P(None, 'dp', 'mp'), may hold values from -0.21875 to 0.21875
- self_out: bfloat16 [768, 768], P('mp', 'dp'), may hold values from -1.25 to 1.25
- cross_q: bfloat16 [768, 768], P('dp', 'mp'), may hold values from -0.21875 to 0.21875
- cross_kv: bfloat16 [2, 1408, 768], P(None, 'dp', 'mp'), may hold values from -0.15625 to 0.15625
- cross_out: bfloat16 [768, 768], P('mp', 'dp'), may hold values from -1.75 to 1.75
- ffn_in: bfloat16 [2, 768, 3072], P(None, 'dp', 'mp'), may hold values from -0.21875 to 0.21875
- ffn_out: bfloat16 [2, 3072, 768], P(None, 'mp', 'dp'), may hold values from -0.109375 to 0.109375
- vectors: bfloat16 [10, 768], P(None, 'dp'), may hold values from -1.5 to 1.5
- head_bias: bfloat16 [4, 768], P(None, 'mp'), may hold values from -3 to 3
- ffn_bias: bfloat16 [2, 3072], P(None, 'mp'), may hold values from -3 to 3
- out_grad: bfloat16 [8192, 768], P('dp'), may hold values from -6 to 6
Outputs:
- out_stream: bfloat16 [8192, 768], P('dp')
- stream_grad: float32 [8192, 768], P('dp')
- grad_self_qkv: float32 [3, 768, 768], P(None, 'dp', 'mp')
- grad_self_out: float32 [768, 768], P('mp', 'dp')
- grad_cross_q: float32 [768, 768], P('dp', 'mp')
- grad_cross_kv: float32 [2, 1408, 768], P(None, 'dp', 'mp')
- grad_cross_out: float32 [768, 768], P('mp', 'dp')
- grad_ffn_in: float32 [2, 768, 3072], P(None, 'dp', 'mp')
- grad_ffn_out: float32 [2, 3072, 768], P(None, 'mp', 'dp')
- grad_vectors: float32 [10, 768], P(None, 'dp')
- grad_head_bias: float32 [4, 768], P(None, 'mp')
- grad_ffn_bias: float32 [2, 3072], P(None, 'mp')
- stream_rms: float32 [4], replicated
Inputs may be any that keep to these rules, and one draw needn't show every extreme that they name: `image_index`: each dp shard's row names each of its 16 images once. `text_segment`: never falls along a row; every slot 0 to 3 appears in every row.
All inputs are finite; a program needn't handle non-finite values. No bound on the sum of `text_valid` on one device may be relied on, other than what follows from the above.
Results may differ from a plain program's by a relative error of at most 0.014.
Values may be sent and summed in bfloat16 or wider, within the bound.
A program may use at most 192 MiB of HBM per device.

v0:
```python
import jax
import jax.numpy as jnp
from jax import lax
from jax.sharding import PartitionSpec as P

HEAD = 64
KEYS = 257
QUERIES = 32
SLOTS = 4
ROW_LEN = 256


EPSILON = 1e-06
MASKED = -1e30


def layer_norm(values, gain_row, shift_row):
    row_mean = jnp.mean(values, axis=-1, keepdims=True)
    centred = values - row_mean
    row_var = jnp.mean(centred * centred, axis=-1, keepdims=True)
    return centred * lax.rsqrt(row_var + EPSILON) * gain_row + shift_row


def norm_back(values, gain_row, shift_row, grad_normed):
    pull_back = jax.vjp(layer_norm, values, gain_row, shift_row)[1]
    return pull_back(grad_normed)


def gelu_exact(values):
    return jax.nn.gelu(values, approximate=False)


def round_low(values):
    return values.astype(jnp.bfloat16)


def matmul(left_side, right_side):
    return jnp.dot(left_side, right_side, preferred_element_type=jnp.float32)


def matmul_left(left_side, right_side):
    return lax.dot_general(
        left_side, right_side, (((0,), (0,)), ((), ())), preferred_element_type=jnp.float32
    )


def matmul_right(left_side, right_side):
    return lax.dot_general(
        left_side, right_side, (((1,), (1,)), ((), ())), preferred_element_type=jnp.float32
    )


def column_sum(values):
    return jnp.sum(values.astype(jnp.float32), axis=0)


def attn_scores(queries, keys_in, key_mask):
    score_scale = queries.shape[-1] ** (-0.5)
    scores = (
        jnp.einsum("bqhe,bkhe->bhqk", queries, keys_in, preferred_element_type=jnp.float32)
        * score_scale
    )
    if key_mask is None:
        return scores
    return jnp.where(key_mask[:, None], scores, MASKED)


def attend(queries, keys_in, values_in, key_mask):
    scores = attn_scores(queries, keys_in, key_mask)
    row_max = jnp.max(scores, axis=-1, keepdims=True)
    exponent = jnp.exp(scores - row_max)
    row_total = jnp.sum(exponent, axis=-1, keepdims=True)
    attn_probs = round_low(exponent / row_total)
    mixed_out = jnp.einsum(
        "bhqk,bkhe->bqhe", attn_probs, values_in, preferred_element_type=jnp.float32
    )
    return (round_low(mixed_out), row_max + jnp.log(row_total))


def attend_back(queries, keys_in, values_in, key_mask, log_total, grad_mixed):
    score_scale = queries.shape[-1] ** (-0.5)
    attn_probs = jnp.exp(attn_scores(queries, keys_in, key_mask) - log_total)
    grad_values = jnp.einsum(
        "bhqk,bqhe->bkhe", round_low(attn_probs), grad_mixed, preferred_element_type=jnp.float32
    )
    grad_probs = jnp.einsum(
        "bqhe,bkhe->bhqk", grad_mixed, values_in, preferred_element_type=jnp.float32
    )
    row_delta = jnp.sum(attn_probs * grad_probs, axis=-1, keepdims=True)
    grad_scores = round_low(attn_probs * (grad_probs - row_delta))
    grad_queries = (
        jnp.einsum("bhqk,bkhe->bqhe", grad_scores, keys_in, preferred_element_type=jnp.float32)
        * score_scale
    )
    grad_keys = (
        jnp.einsum("bhqk,bqhe->bkhe", grad_scores, queries, preferred_element_type=jnp.float32)
        * score_scale
    )
    return (round_low(grad_queries), round_low(grad_keys), round_low(grad_values))


def heads_total(partial_terms):
    return lax.psum(partial_terms, "mp")


def inputs_total(partial_terms):
    return lax.psum(partial_terms, "mp")


def ffn_forward(normed_low, weight_up, bias_up, weight_down):
    up_value = matmul(normed_low, weight_up) + bias_up
    hidden = round_low(gelu_exact(up_value))
    return (up_value, hidden, matmul(hidden, weight_down))


def ffn_back(normed_low, up_value, hidden, weight_up, weight_down, grad_low):
    grad_down = matmul_left(hidden, grad_low)
    grad_hidden = matmul_right(grad_low, weight_down)
    grad_up = round_low(jax.vjp(gelu_exact, up_value)[1](grad_hidden)[0])
    grad_in = matmul_left(normed_low, grad_up)
    return (grad_in, grad_down, column_sum(grad_up), matmul_right(grad_up, weight_up))


def body(
    stream_in,
    features,
    image_index,
    text_segment,
    text_valid,
    self_qkv,
    self_out,
    cross_q,
    cross_kv,
    cross_out,
    ffn_in,
    ffn_out,
    vectors,
    head_bias,
    ffn_bias,
    out_grad,
):
    gathered = (
        lax.all_gather(self_qkv, "dp", axis=1, tiled=True),
        lax.all_gather(self_out, "dp", axis=1, tiled=True),
        lax.all_gather(cross_q, "dp", axis=0, tiled=True),
        lax.all_gather(cross_kv, "dp", axis=1, tiled=True),
        lax.all_gather(cross_out, "dp", axis=1, tiled=True),
        lax.all_gather(ffn_in, "dp", axis=1, tiled=True),
        lax.all_gather(ffn_out, "dp", axis=2, tiled=True),
        lax.all_gather(vectors, "dp", axis=1, tiled=True),
    )
    qkv_w, proj_w, cq_w, ckv_w, cproj_w, up_w, down_w, vector_low = gathered
    vecs = vector_low.astype(jnp.float32)
    bias_heads = head_bias.astype(jnp.float32)
    bias_hidden = ffn_bias.astype(jnp.float32)
    stream = stream_in.astype(jnp.float32)
    tokens, model_width = stream.shape
    row_count = tokens // ROW_LEN
    query_count = SLOTS * QUERIES
    text_len = ROW_LEN - query_count
    local_width = qkv_w.shape[2]
    local_heads = local_width // HEAD
    query_segment = jnp.arange(query_count, dtype=jnp.int32) // QUERIES
    segment = jnp.concatenate(
        [jnp.broadcast_to(query_segment, (row_count, query_count)), text_segment], axis=1
    )
    valid = (
        jnp.concatenate([jnp.ones((row_count, query_count), jnp.int32), text_valid], axis=1) == 1
    )
    key_mask = (segment[:, :, None] == segment[:, None, :]) & valid[:, None, :]
    heads_shape = (row_count, ROW_LEN, local_heads, HEAD)
    normed_low = round_low(layer_norm(stream, vecs[0], vecs[1]))
    self_query = round_low(matmul(normed_low, qkv_w[0]) + bias_heads[0]).reshape(heads_shape)
    self_key = round_low(matmul(normed_low, qkv_w[1])).reshape(heads_shape)
    self_value = round_low(matmul(normed_low, qkv_w[2]) + bias_heads[1]).reshape(heads_shape)
    self_mixed, self_total = attend(self_query, self_key, self_value, key_mask)
    self_mixed = self_mixed.reshape(tokens, local_width)
    self_term = matmul(self_mixed, proj_w).reshape(row_count, ROW_LEN, model_width)
    after_self = stream + heads_total(self_term.reshape(tokens, model_width)) + vecs[6]
    self_rows = after_self.reshape(row_count, ROW_LEN, model_width)
    query_part = self_rows[:, :query_count].reshape(-1, model_width)
    cross_normed = round_low(layer_norm(query_part, vecs[2], vecs[3]))
    slot_count = row_count * SLOTS
    cross_query = round_low(matmul(cross_normed, cq_w) + bias_heads[2]).reshape(
        slot_count, QUERIES, local_heads, HEAD
    )
    image_order = image_index.reshape(-1)
    pick_table = (image_order[:, None] == jnp.arange(image_order.shape[0])[None, :]).astype(
        jnp.bfloat16
    )
    keys_all = round_low(
        jnp.einsum("nkf,fc->nkc", features, ckv_w[0], preferred_element_type=jnp.float32)
    )
    values_all = round_low(
        jnp.einsum("nkf,fc->nkc", features, ckv_w[1], preferred_element_type=jnp.float32)
        + bias_heads[3]
    )
    cross_keys = round_low(
        jnp.einsum("ij,jkc->ikc", pick_table, keys_all, preferred_element_type=jnp.float32)
    )
    cross_values = round_low(
        jnp.einsum("ij,jkc->ikc", pick_table, values_all, preferred_element_type=jnp.float32)
    )
    cross_keys = cross_keys.reshape(slot_count, KEYS, local_heads, HEAD)
    cross_values = cross_values.reshape(slot_count, KEYS, local_heads, HEAD)
    cross_mixed, cross_total = attend(cross_query, cross_keys, cross_values, None)
    cross_mixed = cross_mixed.reshape(-1, local_width)
    cross_term = matmul(cross_mixed, cproj_w).reshape(row_count, query_count, model_width)
    after_query = query_part + heads_total(cross_term.reshape(-1, model_width)) + vecs[7]
    after_cross = jnp.concatenate(
        [after_query.reshape(row_count, query_count, model_width), self_rows[:, query_count:]],
        axis=1,
    ).reshape(tokens, model_width)
    ffn_normed = round_low(layer_norm(after_cross, vecs[4], vecs[5])).reshape(
        row_count, ROW_LEN, model_width
    )
    ffn_query = ffn_normed[:, :query_count].reshape(-1, model_width)
    ffn_text = ffn_normed[:, query_count:].reshape(-1, model_width)
    up_query, hidden_query, part_query = ffn_forward(ffn_query, up_w[0], bias_hidden[0], down_w[0])
    up_text, hidden_text, part_text = ffn_forward(ffn_text, up_w[1], bias_hidden[1], down_w[1])
    ffn_terms = jnp.concatenate(
        [
            part_query.reshape(row_count, query_count, model_width),
            part_text.reshape(row_count, text_len, model_width),
        ],
        axis=1,
    )
    query_flag = jnp.arange(ROW_LEN) < query_count
    bias_rows = jnp.where(query_flag[:, None], vecs[8], vecs[9])
    ffn_sum = heads_total(ffn_terms.reshape(tokens, model_width)).reshape(
        row_count, ROW_LEN, model_width
    )
    after_ffn = after_cross + (ffn_sum + bias_rows).reshape(tokens, model_width)
    token_weight = valid.reshape(-1).astype(jnp.float32)
    stream_stats = jnp.stack(
        [
            jnp.sum(token_weight * jnp.sum(section * section, axis=1))
            for section in (stream, after_self, after_cross, after_ffn)
        ]
        + [jnp.sum(token_weight)]
    )
    out_low = round_low(after_ffn)
    regathered = (
        lax.all_gather(self_qkv, "dp", axis=1, tiled=True),
        lax.all_gather(self_out, "dp", axis=1, tiled=True),
        lax.all_gather(cross_q, "dp", axis=0, tiled=True),
        lax.all_gather(cross_kv, "dp", axis=1, tiled=True),
        lax.all_gather(cross_out, "dp", axis=1, tiled=True),
        lax.all_gather(ffn_in, "dp", axis=1, tiled=True),
        lax.all_gather(ffn_out, "dp", axis=2, tiled=True),
        lax.all_gather(vectors, "dp", axis=1, tiled=True),
    )
    qkv_w, proj_w, cq_w, ckv_w, cproj_w, up_w, down_w, vector_low = regathered
    vecs = vector_low.astype(jnp.float32)
    grad_out = out_grad.astype(jnp.float32)
    grad_out_rows = grad_out.reshape(row_count, ROW_LEN, model_width)
    grad_low = round_low(grad_out_rows)
    grad_low_query = grad_low[:, :query_count].reshape(-1, model_width)
    grad_low_text = grad_low[:, query_count:].reshape(-1, model_width)
    in_query, down_query, hidden_bias_query, normed_grad_query = ffn_back(
        ffn_query, up_query, hidden_query, up_w[0], down_w[0], grad_low_query
    )
    in_text, down_text, hidden_bias_text, normed_grad_text = ffn_back(
        ffn_text, up_text, hidden_text, up_w[1], down_w[1], grad_low_text
    )
    normed_grad_q = normed_grad_query.reshape(row_count, query_count, model_width)
    normed_grad_t = normed_grad_text.reshape(row_count, text_len, model_width)
    normed_grad = jnp.concatenate([normed_grad_q, normed_grad_t], axis=1)
    normed_grad = inputs_total(normed_grad.reshape(tokens, model_width))
    cross_back, gain_three, shift_three = norm_back(after_cross, vecs[4], vecs[5], normed_grad)
    grad_cross = grad_out + cross_back
    grad_cross_rows = grad_cross.reshape(row_count, ROW_LEN, model_width)
    grad_branch_cross = round_low(grad_cross_rows[:, :query_count].reshape(-1, model_width))
    grad_cproj = matmul_left(cross_mixed, grad_branch_cross)
    grad_cross_mixed = round_low(matmul_right(grad_branch_cross, cproj_w)).reshape(
        cross_query.shape
    )
    grad_cq_part, grad_ck_part, grad_cv_part = attend_back(
        cross_query, cross_keys, cross_values, None, cross_total, grad_cross_mixed
    )
    grad_cq_part = grad_cq_part.reshape(-1, local_width)
    grad_ck_all = round_low(
        jnp.einsum(
            "ij,ikc->jkc",
            pick_table,
            grad_ck_part.reshape(-1, KEYS, local_width),
            preferred_element_type=jnp.float32,
        )
    )
    grad_cv_all = round_low(
        jnp.einsum(
            "ij,ikc->jkc",
            pick_table,
            grad_cv_part.reshape(-1, KEYS, local_width),
            preferred_element_type=jnp.float32,
        )
    )
    grad_ckv = jnp.stack(
        [
            jnp.einsum("nkf,nkc->fc", features, grad_ck_all, preferred_element_type=jnp.float32),
            jnp.einsum("nkf,nkc->fc", features, grad_cv_all, preferred_element_type=jnp.float32),
        ]
    )
    grad_cq = matmul_left(cross_normed, grad_cq_part)
    cross_grad_term = matmul_right(grad_cq_part, cq_w)
    cross_normed_grad = inputs_total(cross_grad_term)
    query_back, gain_two, shift_two = norm_back(query_part, vecs[2], vecs[3], cross_normed_grad)
    grad_self = jnp.concatenate(
        [
            grad_cross_rows[:, :query_count]
            + query_back.reshape(row_count, query_count, model_width),
            grad_cross_rows[:, query_count:],
        ],
        axis=1,
    ).reshape(tokens, model_width)
    grad_branch_self = round_low(grad_self)
    grad_proj = matmul_left(self_mixed, grad_branch_self)
    grad_self_mixed = round_low(matmul_right(grad_branch_self, proj_w)).reshape(heads_shape)
    grad_sq, grad_sk, grad_sv = attend_back(
        self_query, self_key, self_value, key_mask, self_total, grad_self_mixed
    )
    grad_sq = grad_sq.reshape(tokens, local_width)
    grad_sk = grad_sk.reshape(tokens, local_width)
    grad_sv = grad_sv.reshape(tokens, local_width)
    grad_qkv = jnp.stack(
        [
            matmul_left(normed_low, grad_sq),
            matmul_left(normed_low, grad_sk),
            matmul_left(normed_low, grad_sv),
        ]
    )
    self_grad_term = (
        matmul_right(grad_sq, qkv_w[0])
        + matmul_right(grad_sk, qkv_w[1])
        + matmul_right(grad_sv, qkv_w[2])
    )
    normed_grad_self = inputs_total(self_grad_term)
    stream_back, gain_one, shift_one = norm_back(stream, vecs[0], vecs[1], normed_grad_self)
    stream_grad = grad_self + stream_back
    norm_rows = jnp.stack([gain_one, shift_one, gain_two, shift_two, gain_three, shift_three])
    grad_vectors = jnp.concatenate(
        [
            norm_rows,
            jnp.stack(
                [
                    column_sum(grad_branch_self),
                    column_sum(grad_branch_cross),
                    column_sum(grad_low_query),
                    column_sum(grad_low_text),
                ]
            ),
        ]
    )
    grad_up = jnp.stack([in_query, in_text])
    grad_down = jnp.stack([down_query, down_text])
    owned = (
        lax.psum_scatter(grad_qkv, "dp", scatter_dimension=1, tiled=True),
        lax.psum_scatter(grad_proj, "dp", scatter_dimension=1, tiled=True),
        lax.psum_scatter(grad_cq, "dp", scatter_dimension=0, tiled=True),
        lax.psum_scatter(grad_ckv, "dp", scatter_dimension=1, tiled=True),
        lax.psum_scatter(grad_cproj, "dp", scatter_dimension=1, tiled=True),
        lax.psum_scatter(grad_up, "dp", scatter_dimension=1, tiled=True),
        lax.psum_scatter(grad_down, "dp", scatter_dimension=2, tiled=True),
        lax.psum_scatter(grad_vectors, "dp", scatter_dimension=1, tiled=True),
    )
    grad_heads = jnp.stack(
        [
            column_sum(grad_sq),
            column_sum(grad_sv),
            column_sum(grad_cq_part),
            jnp.sum(grad_cv_part.astype(jnp.float32), axis=(0, 1)).reshape(-1),
        ]
    )
    grad_hidden_bias = jnp.stack([hidden_bias_query, hidden_bias_text])
    grad_heads, grad_hidden_bias, stream_stats = lax.psum(
        (grad_heads, grad_hidden_bias, stream_stats), "dp"
    )
    stream_rms = jnp.sqrt(stream_stats[:4] / (stream_stats[4] * model_width))
    return (
        out_low,
        stream_grad,
        owned[0],
        owned[1],
        owned[2],
        owned[3],
        owned[4],
        owned[5],
        owned[6],
        owned[7],
        grad_heads,
        grad_hidden_bias,
        stream_rms,
    )


def solution(mesh):
    in_specs = (
        P("dp", None),
        P("dp", None, None),
        P("dp", None),
        P("dp", None),
        P("dp", None),
        P(None, "dp", "mp"),
        P("mp", "dp"),
        P("dp", "mp"),
        P(None, "dp", "mp"),
        P("mp", "dp"),
        P(None, "dp", "mp"),
        P(None, "mp", "dp"),
        P(None, "dp"),
        P(None, "mp"),
        P(None, "mp"),
        P("dp", None),
    )
    out_specs = (
        P("dp", None),
        P("dp", None),
        P(None, "dp", "mp"),
        P("mp", "dp"),
        P("dp", "mp"),
        P(None, "dp", "mp"),
        P("mp", "dp"),
        P(None, "dp", "mp"),
        P(None, "mp", "dp"),
        P(None, "dp"),
        P(None, "mp"),
        P(None, "mp"),
        P(),
    )
    return jax.shard_map(body, mesh=mesh, in_specs=in_specs, out_specs=out_specs, check_vma=False)
```

profile of v0, /device:TPU:0, one launch (start us, length us, event | category | flops | bytes accessed | tf_op | source)
XLA Modules:
  0.0 1318.1 jit_solution(14410185451355210869)
XLA Ops:
  8.6 32.3 %all-gather = bf16[8,96,10]{1,2,0:T(8,128)(2,1)S(1)} all-gather(bf16[1,96,10]{1,2,0:T(8,128)(2,1)} %bitcast.369), channel_id=1, replica_groups=mesh['dp'=8,'mp'=4] {'dp'}, dimensions={0}, use_global_device_ids=true | all-gather | bytes 17280 | tf_op jit(solution)/shard_map/all_gather | solution.py:150
  44.1 33.9 %all_gather.32 = bf16[3,768,192]{2,1,0:T(8,128)(2,1)S(1)} all-gather(bf16[3,96,192]{2,1,0:T(8,128)(2,1)S(1)} %copy-done.62), channel_id=1, replica_groups=mesh['dp'=8,'mp'=4] {'dp'}, dimensions={1}, use_global_device_ids=true | all-gather | bytes 995328 | tf_op jit(solution)/shard_map/all_gather | solution.py:143
  98.0 31.2 %all_gather.33 = bf16[192,768]{0,1:T(8,128)(2,1)S(1)} all-gather(bf16[192,96]{0,1:T(8,128)(2,1)S(1)} %copy.184), channel_id=1, replica_groups=mesh['dp'=8,'mp'=4] {'dp'}, dimensions={1}, use_global_device_ids=true | all-gather | bytes 331776 | tf_op jit(solution)/shard_map/all_gather | solution.py:144
  134.1 31.6 %all_gather.35 = bf16[768,192]{1,0:T(8,128)(2,1)S(1)} all-gather(bf16[96,192]{1,0:T(8,128)(2,1)S(1)} %copy-done.71), channel_id=1, replica_groups=mesh['dp'=8,'mp'=4] {'dp'}, dimensions={0}, use_global_device_ids=true | all-gather | bytes 331776 | tf_op jit(solution)/shard_map/all_gather | solution.py:145
  165.9 31.8 %all_gather.36 = bf16[192,768]{0,1:T(8,128)(2,1)S(1)} all-gather(bf16[192,96]{0,1:T(8,128)(2,1)S(1)} %copy.195), channel_id=1, replica_groups=mesh['dp'=8,'mp'=4] {'dp'}, dimensions={1}, use_global_device_ids=true | all-gather | bytes 331776 | tf_op jit(solution)/shard_map/all_gather | solution.py:147
  218.2 8.2 fusion.31
  257.4 37.5 %all-reduce.15.cloned.1.call-done = f32[512,768]{1,0:T(8,128)} async-done(((f32[512,768]{1,0:T(8,128)}), f32[512,768]{1,0:T(8,128)}) %all-reduce.15.cloned.1.call-update) | async-done | bytes 1572880 | tf_op jit(solution)/shard_map/psum | solution.py:103
  307.0 8.7 fusion.145
  328.7 30.7 %all-gather.7.cloned.1.call-done = bf16[2,768,768]{2,1,0:T(8,128)(2,1)} async-done(((bf16[2,96,768]{2,1,0:T(8,128)(2,1)}), bf16[2,768,768]{2,1,0:T(8,128)(2,1)}) %all-gather.7.cloned.1.call-update) | async-done | bytes 2359312 | tf_op jit(solution)/shard_map/all_gather | solution.py:148
  359.4 11.8 multiply_convert_fusion.4
  373.3 10.2 multiply_convert_fusion.3
  396.4 116.1 %all-reduce.23.cloned.1.call-done = (f32[1024,768]{1,0:T(8,128)}, f32[1024,768]{1,0:T(8,128)}) async-done(((f32[1024,768]{1,0:T(8,128)}, f32[1024,768]{1,0:T(8,128)}), (f32[1024,768]{1,0:T(8,128)}, f32[1024,768]{1,0:T(8,128)})) %all-reduce.23.cloned.1.call-update) | async-done | bytes 6291472 | tf_op jit(solution)/shard_map/psum | solution.py:103
  539.3 41.9 %all-reduce.17.cloned.1.call-done = f32[512,768]{1,0:T(8,128)} async-done(((f32[512,768]{1,0:T(8,128)}), f32[512,768]{1,0:T(8,128)}) %all-reduce.17.cloned.1.call-update) | async-done | bytes 1572880 | tf_op jit(solution)/shard_map/psum | solution.py:107
  614.1 8.2 copy.218
  632.7 9.4 convolution_bitcast_fusion
  659.0 17.0 %all-reduce.19.cloned.1.call-done = f32[1024,768]{1,0:T(8,128)} async-done(((f32[1024,768]{1,0:T(8,128)}), f32[1024,768]{1,0:T(8,128)}) %all-reduce.19.cloned.1.call-update) | async-done | bytes 3145744 | tf_op jit(solution)/shard_map/psum | solution.py:107
  691.9 9.3 convolution_bitcast_fusion.1
  721.9 38.7 %reduce-scatter.21.cloned.1.call-done = f32[96,192]{1,0:T(8,128)} async-done(((f32[768,192]{1,0:T(8,128)}), f32[96,192]{1,0:T(8,128)}) %reduce-scatter.21.cloned.1.call-update) | async-done | bytes 73744
  766.2 35.2 %all-reduce.3 = (f32[4,192]{1,0:T(4,128)}, f32[2,768]{1,0:T(2,128)}, f32[5]{0:T(128)S(1)}) all-reduce(f32[4,192]{1,0:T(4,128)S(1)} %pad_maximum_fusion.9, f32[2,768]{1,0:T(2,128)S(1)} %pad_maximum_fusion.8, f32[5]{0:T(128)S(1)} %stack.125), channel_id=1, replica_groups=mesh['dp'=8,'mp'=4] {'dp'}, use_global_device_ids=true, to_apply=%region_46.47 | all-reduce | flops 2309 | bytes 18472 | tf_op jit(solution)/shard_map/psum | solution.py:375
  807.8 16.7 %reduce-scatter.25.cloned.1.call-done = f32[96,10]{1,0:T(8,128)} async-done(((f32[768,10]{1,0:T(8,128)}), f32[96,10]{1,0:T(8,128)}) %reduce-scatter.25.cloned.1.call-update) | async-done | bytes 3856
  826.0 67.8 %reduce-scatter.19.cloned.1.call-done = f32[96,576]{1,0:T(8,128)} async-done(((f32[768,576]{1,0:T(8,128)}), f32[96,576]{1,0:T(8,128)}) %reduce-scatter.19.cloned.1.call-update) | async-done | bytes 221200
  895.7 250.7 %all-reduce.21.cloned.1.call-done = (f32[2,1408,192]{2,0,1:T(2,128)}, f32[2,768,768]{1,0,2:T(2,128)}) async-done(((f32[2,1408,192]{2,0,1:T(2,128)}, f32[2,768,768]{1,0,2:T(2,128)}), (f32[2,1408,192]{2,0,1:T(2,128)}, f32[2,768,768]{1,0,2:T(2,128)})) %all-reduce.21.cloned.1.call-update) | async-done | bytes 6881296
  1150.3 61.9 %reduce-scatter.15.cloned.1.call-done = f32[96,192]{1,0:T(8,128)} async-done(((f32[768,192]{1,0:T(8,128)}), f32[96,192]{1,0:T(8,128)}) %reduce-scatter.15.cloned.1.call-update) | async-done | bytes 73744 | tf_op jit(solution)/shard_map/reduce_scatter | solution.py:359
  1212.2 98.5 %reduce-scatter.17.cloned.1.call-done = f32[2,96,768]{2,1,0:T(8,128)} async-done(((f32[2,768,768]{2,1,0:T(8,128)}), f32[2,96,768]{2,1,0:T(8,128)}) %reduce-scatter.17.cloned.1.call-update) | async-done | bytes 589840 | tf_op jit(solution)/shard_map/reduce_scatter | solution.py:362
  (465 shorter events, 259.4 us)
Async XLA Ops:
  8.0 35.4 %copy-start.2 = (bf16[1024,768]{1,0:T(8,128)(2,1)S(1)}, bf16[1024,768]{1,0:T(8,128)(2,1)}, u32[]{:S(2)}) copy-start(bf16[1024,768]{1,0:T(8,128)(2,1)} %param.16) | copy-start | bytes 4718596
  8.0 193.4 %all-reduce.13.cloned.1.call-start = ((), (), s32[]{:S(2)}) async-start(), calls=%async_computation.6 | async-start | bytes 6291456 | tf_op jit(solution)/shard_map/psum | solution.py:103
  41.7 37.0 %copy-start.63 = (f32[768]{0:T(1024)}, f32[768]{0:T(1024)S(1)}, u32[]{:S(2)}) copy-start(f32[768]{0:T(1024)S(1)} %get-tuple-element.103) | copy-start | bytes 9220
  41.7 165.3 %copy-start.65 = (f32[768]{0:T(1024)}, f32[768]{0:T(1024)S(1)}, u32[]{:S(2)}) copy-start(f32[768]{0:T(1024)S(1)} %get-tuple-element.100) | copy-start | bytes 9220
  43.4 35.9 %copy-start.60 = (f32[1024]{0:T(1024)}, f32[1024]{0:T(1024)S(1)}, u32[]{:S(2)}) copy-start(f32[1024]{0:T(1024)S(1)} %broadcast_multiply_fusion.1) | copy-start | bytes 12292
  132.3 69.1 %copy-start.85 = (f32[768]{0:T(1024)S(1)}, f32[768]{0:T(1024)}, u32[]{:S(2)}) copy-start(f32[768]{0:T(1024)} %get-tuple-element.101) | copy-start | bytes 9220
  132.4 78.5 %all-gather.5.cloned.1.call-start = ((), (), s32[]{:S(2)}) async-start(), calls=%async_computation.7 | async-start | bytes 1622016 | tf_op jit(solution)/shard_map/all_gather | solution.py:146
  134.1 160.9 %all-reduce.15.cloned.1.call-start = ((), (), s32[]{:S(2)}) async-start(), calls=%async_computation.8 | async-start | bytes 3145728 | tf_op jit(solution)/shard_map/psum | solution.py:103
  165.8 42.7 %copy-start.28 = (bf16[768,192]{1,0:T(8,128)(2,1)}, bf16[768,192]{1,0:T(8,128)(2,1)S(1)}, u32[]{:S(2)}) copy-start(bf16[768,192]{1,0:T(8,128)(2,1)S(1)} %all_gather.35) | copy-start | bytes 884740
  251.8 55.1 %all-gather.9.cloned.1.call-start = ((), (), s32[]{:S(2)}) async-start(), calls=%async_computation.10 | async-start | bytes 2654208 | tf_op jit(solution)/shard_map/all_gather | solution.py:149
  253.9 105.5 %all-gather.7.cloned.1.call-start = ((), (), s32[]{:S(2)}) async-start(), calls=%async_computation.9 | async-start | bytes 2654208 | tf_op jit(solution)/shard_map/all_gather | solution.py:148
  254.5 258.1 %all-reduce.23.cloned.1.call-start = ((), (), s32[]{:S(2)}) async-start(), calls=%async_computation.20 | async-start | bytes 12582912 | tf_op jit(solution)/shard_map/psum | solution.py:103
  254.7 40.2 %copy-start.94 = (f32[768]{0:T(1024)S(1)}, f32[768]{0:T(1024)}, u32[]{:S(2)}) copy-start(f32[768]{0:T(1024)} %get-tuple-element.98) | copy-start | bytes 9220
  394.1 187.1 %all-reduce.17.cloned.1.call-start = ((), (), s32[]{:S(2)}) async-start(), calls=%async_computation.11 | async-start | bytes 3145728 | tf_op jit(solution)/shard_map/psum | solution.py:107
  538.0 138.0 %all-reduce.19.cloned.1.call-start = ((), (), s32[]{:S(2)}) async-start(), calls=%async_computation.12 | async-start | bytes 6291456 | tf_op jit(solution)/shard_map/psum | solution.py:107
  607.4 112.9 %reduce-scatter.23.cloned.1.call-start = ((), (), s32[]{:S(2)}) async-start(), calls=%async_computation.17 | async-start | bytes 884736
  632.6 128.0 %reduce-scatter.21.cloned.1.call-start = ((), (), s32[]{:S(2)}) async-start(), calls=%async_computation.16 | async-start | bytes 884736
  657.4 167.1 %reduce-scatter.25.cloned.1.call-start = ((), (), s32[]{:S(2)}) async-start(), calls=%async_computation.18 | async-start | bytes 442368
  682.2 211.6 %reduce-scatter.19.cloned.1.call-start = ((), (), s32[]{:S(2)}) async-start(), calls=%async_computation.15 | async-start | bytes 2211840
  691.3 455.2 %all-reduce.21.cloned.1.call-start = ((), (), s32[]{:S(2)}) async-start(), calls=%async_computation.19 | async-start | bytes 15204352
  709.3 502.9 %reduce-scatter.15.cloned.1.call-start = ((), (), s32[]{:S(2)}) async-start(), calls=%async_computation.13 | async-start | bytes 884736 | tf_op jit(solution)/shard_map/reduce_scatter | solution.py:359
  711.8 598.9 %reduce-scatter.17.cloned.1.call-start = ((), (), s32[]{:S(2)}) async-start(), calls=%async_computation.14 | async-start | bytes 5308416 | tf_op jit(solution)/shard_map/reduce_scatter | solution.py:362
  717.3 44.9 %copy-start.93 = (f32[4,256]{1,0:T(4,128)S(1)}, f32[4,256]{1,0:T(4,128)}, u32[]{:S(2)}) copy-start(f32[4,256]{1,0:T(4,128)} %get-tuple-element.86) | copy-start | bytes 12292
  717.3 44.9 %copy-start.105 = (s32[4,128]{1,0:T(4,128)S(1)}, s32[4,128]{1,0:T(4,128)}, u32[]{:S(2)}) copy-start(s32[4,128]{1,0:T(4,128)} %param.20) | copy-start | bytes 6148
  (115 other events, 585.4 us)
Sparse Core Ops, SparseCore 0:
  132.5 68.9 all-reduce.12
  251.9 42.9 all-reduce.14
  394.2 118.2 all-reduce.22
  538.1 43.0 all-reduce.16
  607.5 68.4 all-reduce.18
Sparse Core Ops, SparseCore 1:
  135.6 44.6 all-gather.4
  255.1 51.8 all-gather.8
  309.0 50.3 all-gather.6
  632.6 62.7 reduce-scatter.22
  699.1 61.5 reduce-scatter.20
  763.9 60.6 reduce-scatter.24
  827.9 65.9 reduce-scatter.18
  898.4 248.0 all-reduce.20
  1150.5 61.6 reduce-scatter.14
  1216.4 94.2 reduce-scatter.16
where the time goes:
time: 1330 us; the launch traced here: 1320 us
  waiting for transfers between devices  787 us (59%)
  blocking collectives  196 us (15%)
  local copies, waits for them, and re-layouts  135 us (10%)
  matrix products  115 us (9%)
  other arithmetic  64.6 us (5%)
  between operations  19 us (1%)
    unnamed x20, waiting for transfers between devices  375 us
    psum x3, waiting for transfers between devices, heads_total(): return lax.psum(partial_terms, 'mp')  157 us
    reduce_scatter x1, waiting for transfers between devices, body(): lax.psum_scatter(grad_up, 'dp', scatter_dimension=1, tiled=True)  98.5 us
    reduce_scatter x1, waiting for transfers between devices, body(): lax.psum_scatter(grad_cq, 'dp', scatter_dimension=0, tiled=True)  61.9 us
    unnamed x275, local copies, waits for them, and re-layouts  59.9 us
    psum x2, waiting for transfers between devices, inputs_total(): return lax.psum(partial_terms, 'mp')  59 us
    psum x1, blocking collectives, body(): lax.psum((grad_heads, grad_hidden_bias, stream_stats), 'dp')  35.2 us
    all_gather x1, blocking collectives, body(): lax.all_gather(self_qkv, 'dp', axis=1, tiled=True)  33.9 us
  transfers between devices with their start and end apart: 15, of which 13 were waited for; matrix products, arithmetic and copies ran while one was open for 12% of the time, Pallas kernels for 0%

commit v1 on v0

--- a/solution.py
+++ b/solution.py
@@ -1,6 +1,10 @@
+import functools
+
 import jax
 import jax.numpy as jnp
 from jax import lax
+from jax.experimental import pallas as pl
+from jax.experimental.pallas import tpu as pltpu
 from jax.sharding import PartitionSpec as P
 
 HEAD = 64
@@ -12,6 +16,282 @@
 
 EPSILON = 1e-06
 MASKED = -1e30
+MESH = pl.DeviceIdType.MESH
+VMEM_LIMIT = 56 * 2**20
+
+
+def dp_place(count):
+    index = lax.axis_index("dp")
+    return index // 2, lax.rem(index, 2), lax.axis_index("mp"), count // 2
+
+
+def dp_barrier(line, side, rank, lines):
+    barrier = pltpu.get_barrier_semaphore()
+    for step in range(1, lines):
+        other = lax.rem(line + step, lines)
+        pl.semaphore_signal(
+            barrier, inc=1, device_id=(other * 2 + side, rank), device_id_type=MESH
+        )
+    pl.semaphore_signal(
+        barrier, inc=1, device_id=(line * 2 + 1 - side, rank), device_id_type=MESH
+    )
+    pl.semaphore_wait(barrier, lines)
+
+
+def gather_kernel(count, pieces, *refs):
+    shards, wholes = refs[:pieces], refs[pieces : 2 * pieces]
+    own_sem, line_send, line_recv, side_send, side_recv = refs[2 * pieces :]
+    line, side, rank, lines = dp_place(count)
+    index = line * 2 + side
+    beside = (line * 2 + 1 - side, rank)
+    dp_barrier(line, side, rank, lines)
+
+    def to_side(piece, step, source, origin):
+        return pltpu.make_async_remote_copy(
+            src_ref=source,
+            dst_ref=wholes[piece].at[origin],
+            send_sem=side_send.at[piece, step],
+            recv_sem=side_recv.at[piece, step],
+            device_id=beside,
+            device_id_type=MESH,
+        )
+
+    def along(piece, step):
+        return pltpu.make_async_remote_copy(
+            src_ref=shards[piece],
+            dst_ref=wholes[piece].at[index],
+            send_sem=line_send.at[piece, step],
+            recv_sem=line_recv.at[piece, step],
+            device_id=(lax.rem(line + step, lines) * 2 + side, rank),
+            device_id_type=MESH,
+        )
+
+    for piece in range(pieces):
+        pltpu.make_async_copy(shards[piece], wholes[piece].at[index], own_sem.at[piece]).start()
+        for step in range(1, lines):
+            along(piece, step).start()
+        to_side(piece, 0, shards[piece], index).start()
+    for piece in range(pieces):
+        for step in range(1, lines):
+            along(piece, step).wait_recv()
+            origin = lax.rem(line - step + lines, lines) * 2 + side
+            to_side(piece, step, wholes[piece].at[origin], origin).start()
+    for piece in range(pieces):
+        pltpu.make_async_copy(shards[piece], wholes[piece].at[index], own_sem.at[piece]).wait()
+        for step in range(1, lines):
+            along(piece, step).wait_send()
+        for step in range(lines):
+            to_side(piece, step, shards[piece], index).wait()
+
+
+def gather_dp(shards, count):
+    pieces = len(shards)
+    lines = count // 2
+    anywhere = pl.BlockSpec(memory_space=pl.ANY)
+    return pl.pallas_call(
+        functools.partial(gather_kernel, count, pieces),
+        out_shape=[jax.ShapeDtypeStruct((count, *item.shape), item.dtype) for item in shards],
+        in_specs=[anywhere] * pieces,
+        out_specs=[anywhere] * pieces,
+        scratch_shapes=[pltpu.SemaphoreType.DMA((pieces,))]
+        + [pltpu.SemaphoreType.DMA((pieces, lines))] * 4,
+        compiler_params=pltpu.CompilerParams(collective_id=0, has_side_effects=True),
+    )(*shards)
+
+
+def scatter_kernel(count, pieces, *refs):
+    terms, owned = refs[:pieces], refs[pieces : 2 * pieces]
+    side_in, pair, line_in = (
+        refs[2 * pieces : 3 * pieces],
+        refs[3 * pieces : 4 * pieces],
+        refs[4 * pieces : 5 * pieces],
+    )
+    line_send, line_recv, side_send, side_recv = refs[5 * pieces :]
+    line, side, rank, lines = dp_place(count)
+    beside = (line * 2 + 1 - side, rank)
+    dp_barrier(line, side, rank, lines)
+
+    def to_side(piece, step):
+        other = lax.rem(line + step, lines)
+        return pltpu.make_async_remote_copy(
+            src_ref=terms[piece].at[other * 2 + 1 - side],
+            dst_ref=side_in[piece].at[step],
+            send_sem=side_send.at[piece, step],
+            recv_sem=side_recv.at[piece, step],
+            device_id=beside,
+            device_id_type=MESH,
+        )
+
+    def along(piece, step):
+        return pltpu.make_async_remote_copy(
+            src_ref=pair[piece].at[step],
+            dst_ref=line_in[piece].at[step],
+            send_sem=line_send.at[piece, step],
+            recv_sem=line_recv.at[piece, step],
+            device_id=(lax.rem(line + step, lines) * 2 + side, rank),
+            device_id_type=MESH,
+        )
+
+    order = [*range(1, lines), 0]
+    for piece in range(pieces):
+        for step in order:
+            to_side(piece, step).start()
+    for piece in range(pieces):
+        for step in order:
+            to_side(piece, step).wait_recv()
+            other = lax.rem(line + step, lines)
+            total = terms[piece][other * 2 + side].astype(jnp.float32) + side_in[piece][
+                step
+            ].astype(jnp.float32)
+            if step == 0:
+                owned[piece][...] = total
+            else:
+                pair[piece][step] = total.astype(jnp.bfloat16)
+                along(piece, step).start()
+    for piece in range(pieces):
+        for step in range(1, lines):
+            along(piece, step).wait_recv()
+            owned[piece][...] += line_in[piece][step].astype(jnp.float32)
+    for piece in range(pieces):
+        for step in range(1, lines):
+            along(piece, step).wait_send()
+        for step in range(lines):
+            to_side(piece, step).wait_send()
+
+
+def scatter_dp(terms, count):
+    pieces = len(terms)
+    lines = count // 2
+    inside = pl.BlockSpec(memory_space=pltpu.VMEM)
+    blocks = [item.shape[1:] for item in terms]
+    slots = [pltpu.VMEM((lines, *block), jnp.bfloat16) for block in blocks]
+    return pl.pallas_call(
+        functools.partial(scatter_kernel, count, pieces),
+        out_shape=[jax.ShapeDtypeStruct(block, jnp.float32) for block in blocks],
+        in_specs=[inside] * pieces,
+        out_specs=[inside] * pieces,
+        scratch_shapes=slots * 3 + [pltpu.SemaphoreType.DMA((pieces, lines))] * 4,
+        compiler_params=pltpu.CompilerParams(
+            collective_id=1, has_side_effects=True, vmem_limit_bytes=VMEM_LIMIT
+        ),
+    )(*terms)
+
+
+def total_kernel(part_ref, total_ref, pair_in, half, far_in, whole, send_sem, recv_sem):
+    place, rank = lax.axis_index("dp"), lax.axis_index("mp")
+    chip, core = rank // 2, lax.rem(rank, 2)
+    beside, far = chip * 2 + 1 - core, (1 - chip) * 2 + core
+    barrier = pltpu.get_barrier_semaphore()
+    for other in (beside, far):
+        pl.semaphore_signal(barrier, inc=1, device_id=(place, other), device_id_type=MESH)
+    pl.semaphore_wait(barrier, 2)
+
+    def copy(source, target, slot, other):
+        return pltpu.make_async_remote_copy(
+            src_ref=source,
+            dst_ref=target,
+            send_sem=send_sem.at[slot],
+            recv_sem=recv_sem.at[slot],
+            device_id=(place, other),
+            device_id_type=MESH,
+        )
+
+    diagonal = (1 - chip) * 2 + 1 - core
+    pair_far = copy(part_ref.at[diagonal], pair_in.at[1], 1, beside)
+    pair_near = copy(part_ref.at[beside], pair_in.at[0], 0, beside)
+    pair_far.start()
+    pair_near.start()
+    pair_far.wait_recv()
+    half[...] = (
+        part_ref[far].astype(jnp.float32) + pair_in[1].astype(jnp.float32)
+    ).astype(jnp.bfloat16)
+    across = copy(half, far_in, 2, far)
+    across.start()
+    pair_near.wait_recv()
+    near_sum = part_ref[rank].astype(jnp.float32) + pair_in[0].astype(jnp.float32)
+    across.wait_recv()
+    whole[rank] = (near_sum + far_in[...].astype(jnp.float32)).astype(jnp.bfloat16)
+    back_far = copy(whole.at[rank], whole.at[rank], 3, far)
+    back_near = copy(whole.at[rank], whole.at[rank], 4, beside)
+    back_far.start()
+    back_near.start()
+    total_ref[rank] = whole[rank].astype(jnp.float32)
+    back_far.wait_recv()
+    back_diagonal = copy(whole.at[far], whole.at[far], 5, beside)
+    back_diagonal.start()
+    total_ref[far] = whole[far].astype(jnp.float32)
+    back_near.wait_recv()
+    total_ref[beside] = whole[beside].astype(jnp.float32)
+    back_diagonal.wait_recv()
+    total_ref[diagonal] = whole[diagonal].astype(jnp.float32)
+    for item in (pair_far, pair_near, across, back_far, back_near, back_diagonal):
+        item.wait_send()
+
+
+def total_mp(partial_terms, collective):
+    ranks = lax.axis_size("mp")
+    tokens, width = partial_terms.shape
+    if ranks != 4 or tokens % 64:
+        return lax.psum(partial_terms, "mp")
+    block = (tokens // ranks, width)
+    inside = pl.BlockSpec(memory_space=pltpu.VMEM)
+    low = partial_terms.astype(jnp.bfloat16).reshape(ranks, *block)
+    return pl.pallas_call(
+        total_kernel,
+        out_shape=jax.ShapeDtypeStruct((ranks, *block), jnp.float32),
+        in_specs=[inside],
+        out_specs=inside,
+        scratch_shapes=[
+            pltpu.VMEM((2, *block), jnp.bfloat16),
+            pltpu.VMEM(block, jnp.bfloat16),
+            pltpu.VMEM(block, jnp.bfloat16),
+            pltpu.VMEM((ranks, *block), jnp.bfloat16),
+            pltpu.SemaphoreType.DMA((6,)),
+            pltpu.SemaphoreType.DMA((6,)),
+        ],
+        compiler_params=pltpu.CompilerParams(
+            collective_id=2 + collective, has_side_effects=True, vmem_limit_bytes=VMEM_LIMIT
+        ),
+    )(low).reshape(tokens, width)
+
+
+def pack_weights(self_qkv, self_out, cross_q, cross_kv, cross_out, ffn_in, ffn_out, vectors):
+    fan, wide = ffn_in.shape[1], ffn_in.shape[2]
+    return (
+        jnp.pad(vectors, ((0, 6), (0, -vectors.shape[1] % 128))),
+        jnp.concatenate([self_qkv[0], self_qkv[1], self_qkv[2], self_out.T], axis=1),
+        jnp.concatenate([cross_kv[0], cross_kv[1]], axis=1),
+        jnp.concatenate([cross_q, cross_out.T], axis=1),
+        jnp.concatenate([ffn_in, ffn_out.transpose(0, 2, 1)], axis=0).reshape(4 * fan, wide),
+    )
+
+
+def gather_all(self_qkv, self_out, cross_q, cross_kv, cross_out, ffn_in, ffn_out, vectors):
+    fan, own = ffn_in.shape[1], vectors.shape[1]
+    shards = pack_weights(
+        self_qkv, self_out, cross_q, cross_kv, cross_out, ffn_in, ffn_out, vectors
+    )
+    count = lax.axis_size("dp")
+    if fan % 16 or count % 2:
+        wholes = [lax.all_gather(item, "dp", axis=0) for item in shards]
+    else:
+        wholes = gather_dp(shards, count)
+    vec_all, self_all, kv_all, cross_all, ffn_all = wholes
+    return (
+        vec_all[:, :10, :own].transpose(1, 0, 2).reshape(10, -1),
+        self_all.reshape(-1, self_all.shape[-1]),
+        kv_all.reshape(-1, kv_all.shape[-1]),
+        cross_all.reshape(-1, cross_all.shape[-1]),
+        ffn_all.reshape(count, 4, fan, -1).transpose(1, 0, 2, 3).reshape(4, count * fan, -1),
+    )
+
+
+def scatter_all(terms):
+    count = lax.axis_size("dp")
+    blocks = [item.astype(jnp.bfloat16).reshape(count, -1, item.shape[-1]) for item in terms]
+    if any(item.shape[1] % 16 for item in blocks) or count % 2:
+        return [lax.psum_scatter(item, "dp", scatter_dimension=0, tiled=True) for item in terms]
+    return scatter_dp(blocks, count)
 
 
 def layer_norm(values, gain_row, shift_row):
@@ -99,23 +379,15 @@
     return (round_low(grad_queries), round_low(grad_keys), round_low(grad_values))
 
 
-def heads_total(partial_terms):
-    return lax.psum(partial_terms, "mp")
-
-
-def inputs_total(partial_terms):
-    return lax.psum(partial_terms, "mp")
-
-
 def ffn_forward(normed_low, weight_up, bias_up, weight_down):
     up_value = matmul(normed_low, weight_up) + bias_up
     hidden = round_low(gelu_exact(up_value))
-    return (up_value, hidden, matmul(hidden, weight_down))
+    return (up_value, hidden, matmul_right(hidden, weight_down))
 
 
 def ffn_back(normed_low, up_value, hidden, weight_up, weight_down, grad_low):
-    grad_down = matmul_left(hidden, grad_low)
-    grad_hidden = matmul_right(grad_low, weight_down)
+    grad_down = matmul_left(grad_low, hidden)
+    grad_hidden = matmul(grad_low, weight_down)
     grad_up = round_low(jax.vjp(gelu_exact, up_value)[1](grad_hidden)[0])
     grad_in = matmul_left(normed_low, grad_up)
     return (grad_in, grad_down, column_sum(grad_up), matmul_right(grad_up, weight_up))
@@ -139,17 +411,15 @@
     ffn_bias,
     out_grad,
 ):
-    gathered = (
-        lax.all_gather(self_qkv, "dp", axis=1, tiled=True),
-        lax.all_gather(self_out, "dp", axis=1, tiled=True),
-        lax.all_gather(cross_q, "dp", axis=0, tiled=True),
-        lax.all_gather(cross_kv, "dp", axis=1, tiled=True),
-        lax.all_gather(cross_out, "dp", axis=1, tiled=True),
-        lax.all_gather(ffn_in, "dp", axis=1, tiled=True),
-        lax.all_gather(ffn_out, "dp", axis=2, tiled=True),
-        lax.all_gather(vectors, "dp", axis=1, tiled=True),
-    )
-    qkv_w, proj_w, cq_w, ckv_w, cproj_w, up_w, down_w, vector_low = gathered
+    vector_low, self_w, ckv_all, cross_w, ffn_w = gather_all(
+        self_qkv, self_out, cross_q, cross_kv, cross_out, ffn_in, ffn_out, vectors
+    )
+    local = self_qkv.shape[2]
+    qkv_w = [self_w[:, i * local : (i + 1) * local] for i in range(3)]
+    proj_w = self_w[:, 3 * local :]
+    cq_w, cproj_w = cross_w[:, :local], cross_w[:, local:]
+    ckv_w = [ckv_all[:, :local], ckv_all[:, local:]]
+    up_w, down_w = ffn_w[:2], ffn_w[2:]
     vecs = vector_low.astype(jnp.float32)
     bias_heads = head_bias.astype(jnp.float32)
     bias_hidden = ffn_bias.astype(jnp.float32)
@@ -158,7 +428,7 @@
     row_count = tokens // ROW_LEN
     query_count = SLOTS * QUERIES
     text_len = ROW_LEN - query_count
-    local_width = qkv_w.shape[2]
+    local_width = local
     local_heads = local_width // HEAD
     query_segment = jnp.arange(query_count, dtype=jnp.int32) // QUERIES
     segment = jnp.concatenate(
@@ -175,8 +445,8 @@
     self_value = round_low(matmul(normed_low, qkv_w[2]) + bias_heads[1]).reshape(heads_shape)
     self_mixed, self_total = attend(self_query, self_key, self_value, key_mask)
     self_mixed = self_mixed.reshape(tokens, local_width)
-    self_term = matmul(self_mixed, proj_w).reshape(row_count, ROW_LEN, model_width)
-    after_self = stream + heads_total(self_term.reshape(tokens, model_width)) + vecs[6]
+    self_term = matmul_right(self_mixed, proj_w).reshape(row_count, ROW_LEN, model_width)
+    after_self = stream + total_mp(self_term.reshape(tokens, model_width), 0) + vecs[6]
     self_rows = after_self.reshape(row_count, ROW_LEN, model_width)
     query_part = self_rows[:, :query_count].reshape(-1, model_width)
     cross_normed = round_low(layer_norm(query_part, vecs[2], vecs[3]))
@@ -205,8 +475,8 @@
     cross_values = cross_values.reshape(slot_count, KEYS, local_heads, HEAD)
     cross_mixed, cross_total = attend(cross_query, cross_keys, cross_values, None)
     cross_mixed = cross_mixed.reshape(-1, local_width)
-    cross_term = matmul(cross_mixed, cproj_w).reshape(row_count, query_count, model_width)
-    after_query = query_part + heads_total(cross_term.reshape(-1, model_width)) + vecs[7]
+    cross_term = matmul_right(cross_mixed, cproj_w).reshape(row_count, query_count, model_width)
+    after_query = query_part + total_mp(cross_term.reshape(-1, model_width), 1) + vecs[7]
     after_cross = jnp.concatenate(
         [after_query.reshape(row_count, query_count, model_width), self_rows[:, query_count:]],
         axis=1,
@@ -227,7 +497,7 @@
     )
     query_flag = jnp.arange(ROW_LEN) < query_count
     bias_rows = jnp.where(query_flag[:, None], vecs[8], vecs[9])
-    ffn_sum = heads_total(ffn_terms.reshape(tokens, model_width)).reshape(
+    ffn_sum = total_mp(ffn_terms.reshape(tokens, model_width), 0).reshape(
         row_count, ROW_LEN, model_width
     )
     after_ffn = after_cross + (ffn_sum + bias_rows).reshape(tokens, model_width)
@@ -240,18 +510,6 @@
         + [jnp.sum(token_weight)]
     )
     out_low = round_low(after_ffn)
-    regathered = (
-        lax.all_gather(self_qkv, "dp", axis=1, tiled=True),
-        lax.all_gather(self_out, "dp", axis=1, tiled=True),
-        lax.all_gather(cross_q, "dp", axis=0, tiled=True),
-        lax.all_gather(cross_kv, "dp", axis=1, tiled=True),
-        lax.all_gather(cross_out, "dp", axis=1, tiled=True),
-        lax.all_gather(ffn_in, "dp", axis=1, tiled=True),
-        lax.all_gather(ffn_out, "dp", axis=2, tiled=True),
-        lax.all_gather(vectors, "dp", axis=1, tiled=True),
-    )
-    qkv_w, proj_w, cq_w, ckv_w, cproj_w, up_w, down_w, vector_low = regathered
-    vecs = vector_low.astype(jnp.float32)
     grad_out = out_grad.astype(jnp.float32)
     grad_out_rows = grad_out.reshape(row_count, ROW_LEN, model_width)
     grad_low = round_low(grad_out_rows)
@@ -266,13 +524,13 @@
     normed_grad_q = normed_grad_query.reshape(row_count, query_count, model_width)
     normed_grad_t = normed_grad_text.reshape(row_count, text_len, model_width)
     normed_grad = jnp.concatenate([normed_grad_q, normed_grad_t], axis=1)
-    normed_grad = inputs_total(normed_grad.reshape(tokens, model_width))
+    normed_grad = total_mp(normed_grad.reshape(tokens, model_width), 0)
     cross_back, gain_three, shift_three = norm_back(after_cross, vecs[4], vecs[5], normed_grad)
     grad_cross = grad_out + cross_back
     grad_cross_rows = grad_cross.reshape(row_count, ROW_LEN, model_width)
     grad_branch_cross = round_low(grad_cross_rows[:, :query_count].reshape(-1, model_width))
-    grad_cproj = matmul_left(cross_mixed, grad_branch_cross)
-    grad_cross_mixed = round_low(matmul_right(grad_branch_cross, cproj_w)).reshape(
+    grad_cproj = matmul_left(grad_branch_cross, cross_mixed)
+    grad_cross_mixed = round_low(matmul(grad_branch_cross, cproj_w)).reshape(
         cross_query.shape
     )
     grad_cq_part, grad_ck_part, grad_cv_part = attend_back(
@@ -295,15 +553,16 @@
             preferred_element_type=jnp.float32,
         )
     )
-    grad_ckv = jnp.stack(
+    grad_ckv = jnp.concatenate(
         [
             jnp.einsum("nkf,nkc->fc", features, grad_ck_all, preferred_element_type=jnp.float32),
             jnp.einsum("nkf,nkc->fc", features, grad_cv_all, preferred_element_type=jnp.float32),
-        ]
+        ],
+        axis=1,
     )
     grad_cq = matmul_left(cross_normed, grad_cq_part)
     cross_grad_term = matmul_right(grad_cq_part, cq_w)
-    cross_normed_grad = inputs_total(cross_grad_term)
+    cross_normed_grad = total_mp(cross_grad_term, 1)
     query_back, gain_two, shift_two = norm_back(query_part, vecs[2], vecs[3], cross_normed_grad)
     grad_self = jnp.concatenate(
         [
@@ -314,27 +573,29 @@
         axis=1,
     ).reshape(tokens, model_width)
     grad_branch_self = round_low(grad_self)
-    grad_proj = matmul_left(self_mixed, grad_branch_self)
-    grad_self_mixed = round_low(matmul_right(grad_branch_self, proj_w)).reshape(heads_shape)
+    grad_proj = matmul_left(grad_branch_self, self_mixed)
+    grad_self_mixed = round_low(matmul(grad_branch_self, proj_w)).reshape(heads_shape)
     grad_sq, grad_sk, grad_sv = attend_back(
         self_query, self_key, self_value, key_mask, self_total, grad_self_mixed
     )
     grad_sq = grad_sq.reshape(tokens, local_width)
     grad_sk = grad_sk.reshape(tokens, local_width)
     grad_sv = grad_sv.reshape(tokens, local_width)
-    grad_qkv = jnp.stack(
+    grad_self_w = jnp.concatenate(
         [
             matmul_left(normed_low, grad_sq),
             matmul_left(normed_low, grad_sk),
             matmul_left(normed_low, grad_sv),
-        ]
+            grad_proj,
+        ],
+        axis=1,
     )
     self_grad_term = (
         matmul_right(grad_sq, qkv_w[0])
         + matmul_right(grad_sk, qkv_w[1])
         + matmul_right(grad_sv, qkv_w[2])
     )
-    normed_grad_self = inputs_total(self_grad_term)
+    normed_grad_self = total_mp(self_grad_term, 0)
     stream_back, gain_one, shift_one = norm_back(stream, vecs[0], vecs[1], normed_grad_self)
     stream_grad = grad_self + stream_back
     norm_rows = jnp.stack([gain_one, shift_one, gain_two, shift_two, gain_three, shift_three])
@@ -351,16 +612,25 @@
             ),
         ]
     )
-    grad_up = jnp.stack([in_query, in_text])
-    grad_down = jnp.stack([down_query, down_text])
+    owned_self, owned_ckv, owned_cross, own_in, own_in_text, own_out, own_out_text = scatter_all(
+        [
+            grad_self_w,
+            grad_ckv,
+            jnp.concatenate([grad_cq, grad_cproj], axis=1),
+            in_query,
+            in_text,
+            down_query,
+            down_text,
+        ]
+    )
     owned = (
-        lax.psum_scatter(grad_qkv, "dp", scatter_dimension=1, tiled=True),
-        lax.psum_scatter(grad_proj, "dp", scatter_dimension=1, tiled=True),
-        lax.psum_scatter(grad_cq, "dp", scatter_dimension=0, tiled=True),
-        lax.psum_scatter(grad_ckv, "dp", scatter_dimension=1, tiled=True),
-        lax.psum_scatter(grad_cproj, "dp", scatter_dimension=1, tiled=True),
-        lax.psum_scatter(grad_up, "dp", scatter_dimension=1, tiled=True),
-        lax.psum_scatter(grad_down, "dp", scatter_dimension=2, tiled=True),
+        jnp.stack([owned_self[:, i * local : (i + 1) * local] for i in range(3)]),
+        owned_self[:, 3 * local :].T,
+        owned_cross[:, :local],
+        jnp.stack([owned_ckv[:, :local], owned_ckv[:, local:]]),
+        owned_cross[:, local:].T,
+        jnp.stack([own_in, own_in_text]),
+        jnp.stack([own_out.T, own_out_text.T]),
         lax.psum_scatter(grad_vectors, "dp", scatter_dimension=1, tiled=True),
     )
     grad_heads = jnp.stack(

time: 1330 us -> 728 us (0.55)
  waiting for transfers between devices: 787 us -> 0.02 us
  Pallas kernels: 0 us -> 358 us
  blocking collectives: 196 us -> 36.2 us
  local copies, waits for them, and re-layouts: 135 us -> 118 us
    unnamed x20 -> x2, waiting for transfers between devices: 375 us -> 0.02 us
    pallas_call x0 -> x8, Pallas kernels: none -> 358 us  [the longest x6 148 us: total_mp(): pl.pallas_call(total_kernel, out_shape=jax.ShapeDtypeStruct((ranks, *bloc...]
    psum x5 -> x0, waiting for transfers between devices: 216 us -> none  [the longest x3 157 us: heads_total(): return lax.psum(partial_terms, 'mp')]
    all_gather x5 -> x0, blocking collectives: 161 us -> none  [the longest x1 33.9 us: body(): lax.all_gather(self_qkv, 'dp', axis=1, tiled=True)]
    reduce_scatter x2 -> x0, waiting for transfers between devices: 160 us -> none  [the longest x1 98.5 us: body(): lax.psum_scatter(grad_up, 'dp', scatter_dimension=1, tiled=True)]
    all_gather x3 -> x0, waiting for transfers between devices: 35.4 us -> none  [the longest x1 30.7 us: body(): lax.all_gather(ffn_in, 'dp', axis=1, tiled=True)]
    unnamed x275 -> x300, local copies, waits for them, and re-layouts: 59.9 us -> 27.2 us
    dot_general x0 -> x2, matrix products: none -> 18.4 us  [the longest x1 9.8 us: body(): jnp.einsum('nkf,fc->nkc', features, ckv_w[0], preferred_element_type=jnp....]
  transfers between devices with their start and end apart: 15 -> 1, of which waited for: 13 -> 0; matrix products, arithmetic and copies ran while one was open for 12% -> 14% of each run, Pallas kernels for 0% -> 14%
where the time goes in v1:
time: 728 us; the launch traced here: 716 us
  Pallas kernels  358 us (49%)
  matrix products  120 us (16%)
  local copies, waits for them, and re-layouts  118 us (16%)
  other arithmetic  67.9 us (9%)
  blocking collectives  36.2 us (5%)
  between operations  16.9 us (2%)
    pallas_call x6, Pallas kernels, total_mp(): pl.pallas_call(total_kernel, out_shape=jax.ShapeDtypeStruct((ranks, *bloc...  148 us
    pallas_call x1, Pallas kernels, gather_dp(): pl.pallas_call(functools.partial(gather_kernel, count, pieces), out_shape...  108 us
    pallas_call x1, Pallas kernels, scatter_dp(): pl.pallas_call(functools.partial(scatter_kernel, count, pieces), out_shap...  102 us
    psum x1, blocking collectives, body(): lax.psum((grad_heads, grad_hidden_bias, stream_stats), 'dp')  36.2 us
    dot_general x10, matrix products, matmul(): return jnp.dot(left_side, right_side, preferred_element_type=jnp.float32)  27.5 us
    unnamed x300, local copies, waits for them, and re-layouts  27.2 us
    dot_general x10, matrix products, matmul_left(): lax.dot_general(left_side, right_side, (((0,), (0,)), ((), ())), preferre...  15 us
  transfers between devices with their start and end apart: 1, of which 0 were waited for; matrix products, arithmetic and copies ran while one was open for 14% of the time, Pallas kernels for 14%

profile of v1, /device:TPU:0, one launch (start us, length us, event | category | flops | bytes accessed | tf_op | source)
XLA Modules:
  0.0 716.4 jit_solution(17547664733668873750)
XLA Ops:
  20.3 108.3 %shard_map.255 = (bf16[8,16,128]{2,1,0:T(8,128)(2,1)}, bf16[8,96,768]{2,1,0:T(8,128)(2,1)}, bf16[8,176,384]{2,1,0:T(8,128)(2,1)}, bf16[8,96,384]{2,1,0:T(8,128)(2,1)}, bf16[8,384,768]{2,1,0:T(8,128)(2,1)}) custom-call(bf16[16,128]{1,0:T(8,128)(2,1)} %pad.5.refs_0_, bf16[96,768]{1,0:T(8,128)(2,1)} %pad_maximum_fusion.12.refs_1_, ...), custom_call_target="tpu_custom_call" | custom-call | tf_op jit(solution)/shard_map/pallas_call | solution.py:91
  144.9 9.8 %convert_bitcast_fusion = bf16[16,257,192]{2,1,0:T(8,128)(2,1)} fusion(bf16[16,257,1408]{2,0,1:T(8,128)(2,1)} %param.17, bf16[1408,384]{1,0:T(8,128)(2,1)} %bitcast.459), kind=kOutput, calls=%fused_computation.71 | convolution fusion | flops 2224032768 | bytes 13879296 | tf_op jit(solution)/shard_map/nkf,fc->nkc/dot_general | solution.py:462
  154.7 8.6 %fusion.29 = bf16[16,257,192]{2,1,0:T(8,128)(2,1)S(1)} fusion(f32[192]{0:T(256)S(1)} %bitcast.456, bf16[16,257,1408]{2,0,1:T(8,128)(2,1)} %param.17, bf16[1408,384]{1,0:T(8,128)(2,1)S(1)} %bitcast.460), kind=kOutput, calls=%fused_computation.70 | convolution fusion | flops 2224822272 | bytes 13880320 | tf_op jit(solution)/shard_map/nkf,fc->nkc/dot_general | solution.py:465
  165.4 4.5 copy.123
  169.9 3.7 fusion.48
  173.6 4.5 copy.129
  185.6 27.6 %shard_map.256 = f32[4,256,768]{2,1,0:T(8,128)} custom-call(bf16[4,256,768]{2,1,0:T(8,128)(2,1)} %bitcast.380), custom_call_target="tpu_custom_call" | custom-call | tf_op jit(solution)/shard_map/pallas_call | solution.py:239
  216.7 4.7 multiply_reduce_fusion.2
  221.4 4.0 copy.118
  241.2 18.5 %shard_map.257 = f32[4,128,768]{2,1,0:T(8,128)} custom-call(bf16[4,128,768]{2,1,0:T(8,128)(2,1)} %bitcast.405), custom_call_target="tpu_custom_call" | custom-call | tf_op jit(solution)/shard_map/pallas_call | solution.py:239
  265.4 10.4 %multiply_convert_fusion.4 = (bf16[512,768]{1,0:T(8,128)(2,1)S(1)}, f32[512,768]{1,0:T(8,128)S(1)}, f32[512,768]{1,0:T(8,128)S(1)}) fusion(f32[768]{0:T(1024)S(1)} %copy-done.118, bf16[512,768]{1,0:T(8,128)(2,1)S(1)} %bitcast.436, bf16[768,768]{1,0:T(8,128)(2,1)S(1)} %bitcast.424), kind=kOutput, calls=%fused_computation.138 | convolution fusion | flops 629932032 | bytes 5901312 | tf_op jit(solution)/shard_map/dot_general | solution.py:318
  278.5 5.2 multiply_convert_fusion.3
  288.4 27.4 %shard_map.259 = f32[4,256,768]{2,1,0:T(8,128)} custom-call(bf16[4,256,768]{2,1,0:T(8,128)(2,1)} %pad_maximum_fusion.3.part_ref), custom_call_target="tpu_custom_call" | custom-call | tf_op jit(solution)/shard_map/pallas_call | solution.py:239
  321.7 28.3 %shard_map.258 = f32[4,256,768]{2,1,0:T(8,128)} custom-call(bf16[4,256,768]{2,1,0:T(8,128)(2,1)} %pad_maximum_fusion.2.part_ref), custom_call_target="tpu_custom_call" | custom-call | tf_op jit(solution)/shard_map/pallas_call | solution.py:239
  350.2 4.8 multiply_reduce_fusion
  374.9 17.5 %shard_map.260 = f32[4,128,768]{2,1,0:T(8,128)} custom-call(bf16[4,128,768]{2,1,0:T(8,128)(2,1)} %bitcast.404), custom_call_target="tpu_custom_call" | custom-call | tf_op jit(solution)/shard_map/pallas_call | solution.py:239
  423.8 28.3 %shard_map.261 = f32[4,256,768]{2,1,0:T(8,128)} custom-call(bf16[4,256,768]{2,1,0:T(8,128)(2,1)} %bitcast.381), custom_call_target="tpu_custom_call" | custom-call | tf_op jit(solution)/shard_map/pallas_call | solution.py:239
  498.4 4.7 copy.155
  503.1 9.1 %fusion.26 = bf16[1408,192]{0,1:T(8,128)(2,1)} fusion(bf16[16,257,1408]{2,0,1:T(8,128)(2,1)} %param.17, bf16[16,257,192]{2,0,1:T(8,128)(2,1)} %copy.155, s32[16]{0:T(128)S(1)} %bitcast.454), kind=kOutput, calls=%fused_computation.59 | convolution fusion | flops 2249567488 | bytes 13699136 | tf_op jit(solution)/shard_map/nkf,nkc->fc/dot_general | solution.py:559
  518.5 4.5 copy.150
  523.0 8.3 %fusion.27 = bf16[1408,192]{0,1:T(8,128)(2,1)S(1)} fusion(bf16[16,257,1408]{2,0,1:T(8,128)(2,1)} %param.17, bf16[16,257,192]{2,0,1:T(8,128)(2,1)} %copy.150, s32[16]{0:T(128)S(1)} %bitcast.455), kind=kOutput, calls=%fused_computation.60 | convolution fusion | flops 2249567488 | bytes 13699136 | tf_op jit(solution)/shard_map/nkf,nkc->fc/dot_general | solution.py:558
  546.6 102.1 %shard_map.262 = (f32[96,768]{1,0:T(8,128)}, f32[176,384]{1,0:T(8,128)}, f32[96,384]{1,0:T(8,128)}, f32[96,768]{1,0:T(8,128)}, f32[96,768]{1,0:T(8,128)}, /*index=5*/f32[96,768]{1,0:T(8,128)}, f32[96,768]{1,0:T(8,128)}) custom-call(bf16[8,96,768]{2,1,0:T(8,128)(2,1)} %pad_maximum_fusion.4.refs_0_, bf16[8,176,384]{2,1,0:T(8,128)(2,1)} %pad_maximum_fusion.5.refs_1_, ...), custom_call_target="tpu_custom_call" | custom-call | tf_op jit(solution)/shard_map/pallas_call | solution.py:168
  657.4 36.2 %all-reduce.2 = (f32[4,192]{1,0:T(4,128)}, f32[2,768]{1,0:T(2,128)}, f32[5]{0:T(128)S(1)}) all-reduce(f32[4,192]{1,0:T(4,128)S(1)} %pad_maximum_fusion.16, f32[2,768]{1,0:T(2,128)S(1)} %pad_maximum_fusion.15, f32[5]{0:T(128)S(1)} %stack.125), channel_id=1, replica_groups=mesh['dp'=8,'mp'=4] {'dp'}, use_global_device_ids=true, to_apply=%region_33.34 | all-reduce | flops 2309 | bytes 18472 | tf_op jit(solution)/shard_map/psum | solution.py:645
  695.3 5.5 add_add_fusion.3
  (483 shorter events, 213.1 us)
Async XLA Ops:
  7.2 700.5 %reduce-scatter.4.cloned.1.call-start = ((), (), s32[]{:S(2)}) async-start(), calls=%async_computation.1 | async-start | bytes 442368
  16.1 118.9 %copy-start.68 = (f32[1024]{0:T(1024)}, f32[1024]{0:T(1024)S(1)}, u32[]{:S(2)}) copy-start(f32[1024]{0:T(1024)S(1)} %broadcast_multiply_fusion.1) | copy-start | bytes 12292
  16.5 113.0 %copy-start.85 = (f32[1024]{0:T(1024)}, f32[1024]{0:T(1024)S(1)}, u32[]{:S(2)}) copy-start(f32[1024]{0:T(1024)S(1)} %fusion.16) | copy-start | bytes 12292
  16.6 118.4 %copy-start.76 = (f32[1024]{0:T(1024)}, f32[1024]{0:T(1024)S(1)}, u32[]{:S(2)}) copy-start(f32[1024]{0:T(1024)S(1)} %fusion.150) | copy-start | bytes 12292
  138.5 39.9 %copy-start.42 = (bf16[4,256,3,64]{1,0,3,2:T(4,128)(2,1)}, bf16[4,256,3,64]{1,0,3,2:T(4,128)(2,1)S(1)}, u32[]{:S(2)}) copy-start(bf16[4,256,3,64]{1,0,3,2:T(4,128)(2,1)S(1)} %reshape.617) | copy-start | bytes 1179652
  142.7 38.0 %copy-start.44 = (bf16[4,256,3,64]{1,0,3,2:T(4,128)(2,1)}, bf16[4,256,3,64]{1,0,3,2:T(4,128)(2,1)S(1)}, u32[]{:S(2)}) copy-start(bf16[4,256,3,64]{1,0,3,2:T(4,128)(2,1)S(1)} %reshape.616) | copy-start | bytes 1179652
  144.9 9.8 %copy-start.132 = (bf16[8,176,384]{2,1,0:T(8,128)(2,1)S(1)}, bf16[8,176,384]{2,1,0:T(8,128)(2,1)}, u32[]{:S(2)}) copy-start(bf16[8,176,384]{2,1,0:T(8,128)(2,1)} %get-tuple-element.27) | copy-start | bytes 3244036
  154.7 8.6 %copy-start.127 = (s32[1,16]{1,0:T(1,128)S(1)}, s32[1,16]{1,0:T(1,128)}, u32[]{:S(2)}) copy-start(s32[1,16]{1,0:T(1,128)} %param.18) | copy-start | bytes 196
  238.7 21.0 %copy-start.35 = (bf16[512,192]{1,0:T(8,128)(2,1)}, bf16[512,192]{1,0:T(8,128)(2,1)S(1)}, u32[]{:S(2)}) copy-start(bf16[512,192]{1,0:T(8,128)(2,1)S(1)} %reshape.629) | copy-start | bytes 589828
  238.7 21.0 %copy-start = (f32[1024,768]{1,0:T(8,128)S(1)}, f32[1024,768]{1,0:T(8,128)}, u32[]{:S(2)}) copy-start(f32[1024,768]{1,0:T(8,128)} %copy.118) | copy-start | bytes 9437188
  238.7 21.0 %copy-start.89 = (f32[768]{0:T(1024)S(1)}, f32[768]{0:T(1024)}, u32[]{:S(2)}) copy-start(f32[768]{0:T(1024)} %add.249) | copy-start | bytes 9220
  262.9 15.6 %copy-start.52 = (bf16[4,128,768]{2,1,0:T(8,128)(2,1)}, bf16[4,128,768]{2,1,0:T(8,128)(2,1)S(1)}, u32[]{:S(2)}) copy-start(bf16[4,128,768]{2,1,0:T(8,128)(2,1)S(1)} %get-tuple-element.140) | copy-start | bytes 2359300
  265.4 10.4 %copy-start.50 = (bf16[4,128,768]{2,1,0:T(8,128)(2,1)S(1)}, bf16[4,128,768]{2,1,0:T(8,128)(2,1)}, u32[]{:S(2)}) copy-start(bf16[4,128,768]{2,1,0:T(8,128)(2,1)} %get-tuple-element.137) | copy-start | bytes 2359300
  275.8 42.7 %copy-start.133 = (bf16[512,768]{1,0:T(8,128)(2,1)}, bf16[512,768]{1,0:T(8,128)(2,1)S(1)}, u32[]{:S(2)}) copy-start(bf16[512,768]{1,0:T(8,128)(2,1)S(1)} %get-tuple-element.117) | copy-start | bytes 2359300
  321.7 28.3 %copy-start.98 = (f32[768]{0:T(1024)S(1)}, f32[768]{0:T(1024)}, u32[]{:S(2)}) copy-start(f32[768]{0:T(1024)} %slice.227) | copy-start | bytes 9220
  321.7 28.4 %copy-start.99 = (f32[768]{0:T(1024)S(1)}, f32[768]{0:T(1024)}, u32[]{:S(2)}) copy-start(f32[768]{0:T(1024)} %slice.229) | copy-start | bytes 9220
  321.7 28.4 %copy-start.131 = (pred[256]{0:T(512)(128)(4,1)S(1)}, pred[256]{0:T(512)(128)(4,1)}, u32[]{:S(2)}) copy-start(pred[256]{0:T(512)(128)(4,1)} %iota_compare_fusion.1) | copy-start | bytes 772
  321.7 28.5 %copy-start.7 = (f32[4,256,768]{2,1,0:T(8,128)S(1)}, f32[4,256,768]{2,1,0:T(8,128)}, u32[]{:S(2)}) copy-start(f32[4,256,768]{2,1,0:T(8,128)} %shard_map.259) | copy-start | bytes 9437188
  372.3 20.1 %copy-start.1 = (f32[1024,768]{1,0:T(8,128)S(1)}, f32[1024,768]{1,0:T(8,128)}, u32[]{:S(2)}) copy-start(f32[1024,768]{1,0:T(8,128)} %copy.118) | copy-start | bytes 9437188
  372.3 20.1 %copy-start.72 = (f32[768]{0:T(1024)S(1)}, f32[768]{0:T(1024)}, u32[]{:S(2)}) copy-start(f32[768]{0:T(1024)} %mul.374) | copy-start | bytes 9220
  372.3 20.1 %copy-start.79 = (f32[4,128]{1,0:T(4,128)S(1)}, f32[4,128]{1,0:T(4,128)}, u32[]{:S(2)}) copy-start(f32[4,128]{1,0:T(4,128)} %copy-done.78) | copy-start | bytes 6148
  412.2 5.2 copy-start.105
  492.3 5.4 copy-start.112
  503.1 9.1 %copy-start.110 = (f32[3,64]{1,0:T(4,128)S(1)}, f32[3,64]{1,0:T(4,128)}, u32[]{:S(2)}) copy-start(f32[3,64]{1,0:T(4,128)} %get-tuple-element.180) | copy-start | bytes 2308
  (119 other events, 318.9 us)
Sparse Core Ops, SparseCore 0:
  468.6 66.8 reduce-scatter.3

commit v2 on v0

--- a/solution.py
+++ b/solution.py
@@ -1,6 +1,12 @@
+import functools
+import math
+import types
+
 import jax
 import jax.numpy as jnp
 from jax import lax
+from jax.experimental import pallas as pl
+from jax.experimental.pallas import tpu as pltpu
 from jax.sharding import PartitionSpec as P
 
 HEAD = 64
@@ -12,6 +18,1109 @@
 
 EPSILON = 1e-06
 MASKED = -1e30
+MESH = pl.DeviceIdType.MESH
+VMEM_LIMIT = 62 * 2**20
+BF16 = jnp.bfloat16
+F32 = jnp.float32
+PIECES = ("vec", "self", "kv", "cross", "in1", "out1", "in0", "out0")
+TERMS = ("in1", "out1", "in0", "out0", "cross", "kv", "self")
+SUMS = ("self", "cross", "gft", "gfq", "out", "gc", "ga")
+SHARES = ("c", "ft", "fq", "gca", "gsat", "gsaq", "out", "sg")
+WIDE = 256
+CHUNK = 256
+CHUNKS_HELD = 3
+PADDED_KEYS = 272
+
+
+def dot(left, right):
+    return jnp.dot(left, right, preferred_element_type=F32)
+
+
+def dot_rows(left, right):
+    return lax.dot_general(left, right, (((0,), (0,)), ((), ())), preferred_element_type=F32)
+
+
+def dot_columns(left, right):
+    return lax.dot_general(left, right, (((1,), (1,)), ((), ())), preferred_element_type=F32)
+
+
+def norm_parts(values):
+    centred = values - jnp.mean(values, axis=-1, keepdims=True)
+    scale = lax.rsqrt(jnp.mean(centred * centred, axis=-1, keepdims=True) + EPSILON)
+    return centred * scale, scale
+
+
+def norm_grad(normed, scale, gain, grad):
+    scaled = grad * gain
+    return scale * (
+        scaled
+        - jnp.mean(scaled, axis=-1, keepdims=True)
+        - normed * jnp.mean(scaled * normed, axis=-1, keepdims=True)
+    )
+
+
+def lanes(width):
+    return lax.broadcasted_iota(jnp.int32, (1, width), 1)
+
+
+def of_head(head):
+    lane = lanes(WIDE)
+    return (lane >= head * HEAD) & (lane < (head + 1) * HEAD)
+
+
+def spread(values, heads):
+    return jnp.concatenate(
+        [jnp.where(of_head(head), values, jnp.zeros_like(values)) for head in range(heads)], axis=0
+    )
+
+
+def fold(values, heads, tokens):
+    total = jnp.where(of_head(0), values[:tokens], 0.0)
+    for head in range(1, heads):
+        total = total + jnp.where(of_head(head), values[head * tokens : (head + 1) * tokens], 0.0)
+    return total
+
+
+def softmax(scores):
+    exponent = jnp.exp(scores - jnp.max(scores, axis=-1, keepdims=True))
+    return exponent * (1.0 / jnp.sum(exponent, axis=-1, keepdims=True))
+
+
+def pack_columns(items, axis):
+    cut = items[0].shape[axis] // 128 * 128
+    first = [lax.slice_in_dim(item, 0, cut, axis=axis) for item in items]
+    last = [lax.slice_in_dim(item, cut, item.shape[axis], axis=axis) for item in items]
+    return jnp.concatenate(first + last, axis=axis)
+
+
+def unpack_columns(packed, count, width):
+    cut = width // 128 * 128
+    rest = width - cut
+    return [
+        jnp.concatenate(
+            [
+                packed[:, i * cut : (i + 1) * cut],
+                packed[:, count * cut + i * rest : count * cut + (i + 1) * rest],
+            ],
+            axis=1,
+        )
+        for i in range(count)
+    ]
+
+
+def widen(packed, wide, count):
+    low = lanes(128) < HEAD
+    for i in range(count):
+        at = (count + i // 2) * 128
+        tail = packed[:, at : at + 128]
+        if i % 2:
+            tail = pltpu.roll(tail, HEAD, 1)
+        wide[:, i * WIDE : i * WIDE + 128] = packed[:, i * 128 : (i + 1) * 128]
+        wide[:, i * WIDE + 128 : (i + 1) * WIDE] = jnp.where(low, tail, jnp.zeros_like(tail))
+
+
+def layer_kernel(names, sizes, *refs):
+    s = types.SimpleNamespace(**dict(zip(names, refs)))
+    z = sizes
+    count, lines, rows, length, query, width, heads = (
+        z.count,
+        z.count // 2,
+        z.rows,
+        ROW_LEN,
+        SLOTS * QUERIES,
+        z.width,
+        z.heads,
+    )
+    text = length - query
+    place, rank = lax.axis_index("dp"), lax.axis_index("mp")
+    line, side = place // 2, lax.rem(place, 2)
+    chip, core = rank // 2, lax.rem(rank, 2)
+    beside = chip * 2 + 1 - core
+    far = (1 - chip) * 2 + core
+    diagonal = (1 - chip) * 2 + 1 - core
+
+    def remote(source, target, sems, index, device):
+        return pltpu.make_async_remote_copy(
+            src_ref=source,
+            dst_ref=target,
+            send_sem=sems[0].at[index],
+            recv_sem=sems[1].at[index],
+            device_id=device,
+            device_id_type=MESH,
+        )
+
+    def along(step):
+        return (lax.rem(line + step, lines) * 2 + side, rank)
+
+    across = (line * 2 + 1 - side, rank)
+
+    def block(ref, index, size):
+        return ref.at[pl.ds(pl.multiple_of(index * size, 16), size)]
+
+    fan, feat_fan = z.fan, z.feat_fan
+    shard = {
+        "vec": s.vec_h,
+        "self": s.self_h,
+        "kv": s.kv_h,
+        "cross": s.cross_h,
+        "in0": s.ffn_h.at[pl.ds(0, fan)],
+        "in1": s.ffn_h.at[pl.ds(fan, fan)],
+        "out0": s.ffn_h.at[pl.ds(2 * fan, fan)],
+        "out1": s.ffn_h.at[pl.ds(3 * fan, fan)],
+    }
+    whole = {
+        "vec": s.w_vec,
+        "self": s.m_self,
+        "kv": s.m_kv,
+        "cross": s.m_cross,
+        "in0": s.m_in0,
+        "in1": s.m_in1,
+        "out0": s.m_out0,
+        "out1": s.m_out1,
+    }
+    size = {name: fan for name in PIECES} | {"vec": 16, "kv": feat_fan}
+
+    def gather_own(name):
+        p = PIECES.index(name)
+        return pltpu.make_async_copy(
+            shard[name], block(whole[name], place, size[name]), s.own_sem.at[p]
+        )
+
+    def gather_line(name, step):
+        return remote(
+            shard[name],
+            block(whole[name], place, size[name]),
+            (s.gl_send, s.gl_recv),
+            (PIECES.index(name), step),
+            along(step),
+        )
+
+    def gather_side(name, step):
+        origin = lax.rem(line - step + lines, lines) * 2 + side
+        target = block(whole[name], origin, size[name])
+        return remote(
+            shard[name] if step == 0 else target,
+            target,
+            (s.gs_send, s.gs_recv),
+            (PIECES.index(name), step),
+            across,
+        )
+
+    def gather_start(name):
+        gather_own(name).start()
+        for step in range(1, lines):
+            gather_line(name, step).start()
+        gather_side(name, 0).start()
+
+    def gather_forward(name):
+        for step in range(1, lines):
+            gather_line(name, step).wait_recv()
+            gather_side(name, step).start()
+
+    def gather_finish(name):
+        gather_own(name).wait()
+        for step in range(lines):
+            gather_side(name, step).wait_recv()
+
+    def gather_sent(name):
+        for step in range(1, lines):
+            gather_line(name, step).wait_send()
+        for step in range(lines):
+            gather_side(name, step).wait_send()
+
+    side_in = {name: getattr(s, "y_" + name) for name in TERMS}
+    line_in = {name: getattr(s, "z_" + name) for name in TERMS}
+    owned = {
+        "self": s.own_self,
+        "kv": s.own_kv,
+        "cross": s.own_cross,
+        "in0": s.own_ffn.at[pl.ds(0, fan)],
+        "in1": s.own_ffn.at[pl.ds(fan, fan)],
+        "out0": s.own_ffn.at[pl.ds(2 * fan, fan)],
+        "out1": s.own_ffn.at[pl.ds(3 * fan, fan)],
+    }
+    order = [*range(1, lines), 0]
+
+    def scatter_side(name, step):
+        other = lax.rem(line + step, lines)
+        return remote(
+            block(whole[name], other * 2 + 1 - side, size[name]),
+            side_in[name].at[step],
+            (s.ss_send, s.ss_recv),
+            (TERMS.index(name), step),
+            across,
+        )
+
+    def scatter_line(name, step):
+        other = lax.rem(line + step, lines)
+        return remote(
+            block(whole[name], other * 2 + side, size[name]),
+            line_in[name].at[step - 1],
+            (s.sl_send, s.sl_recv),
+            (TERMS.index(name), step),
+            along(step),
+        )
+
+    def scatter_start(name):
+        for step in order:
+            scatter_side(name, step).start()
+
+    def scatter_forward(name):
+        for step in range(1, lines):
+            other = lax.rem(line + step, lines)
+            mine = block(whole[name], other * 2 + side, size[name])
+            scatter_side(name, step).wait_recv()
+            mine[...] = (mine[...].astype(F32) + side_in[name][step].astype(F32)).astype(BF16)
+            scatter_line(name, step).start()
+
+    def scatter_finish(name):
+        scatter_side(name, 0).wait_recv()
+        total = block(whole[name], place, size[name])[...].astype(F32)
+        total = total + side_in[name][0].astype(F32)
+        for step in range(1, lines):
+            scatter_line(name, step).wait_recv()
+            total = total + line_in[name][step - 1].astype(F32)
+        owned[name][...] = total
+        for step in range(1, lines):
+            scatter_line(name, step).wait_send()
+        for step in range(lines):
+            scatter_side(name, step).wait_send()
+
+    def sum_buffers(name):
+        landed = {"ga": "self", "gc": "cross"}.get(name, name)
+        half = {"gft": s.half_t, "self": s.half_row, "out": s.half_row, "ga": s.half_row}
+        return getattr(s, "pin_" + landed), half.get(name, s.half_q), getattr(s, "fin_" + landed)
+
+    def sum_copy(name, hop):
+        part = parts[name]
+        pair_in, half, far_in = sum_buffers(name)
+        source, target, device = (
+            (part.at[diagonal], pair_in.at[1], beside),
+            (part.at[beside], pair_in.at[0], beside),
+            (half, far_in, far),
+        )[hop]
+        return remote(
+            source, target, (s.sum_send, s.sum_recv), (SUMS.index(name), hop), (place, device)
+        )
+
+    parts = {
+        "self": s.part_row,
+        "cross": s.part_q,
+        "gft": s.part_t,
+        "gfq": s.part_q,
+        "out": s.part_row,
+        "gc": s.part_q,
+        "ga": s.part_row,
+    }
+
+    def sum_forward(name):
+        sum_copy(name, 0).wait_recv()
+        pair_in, half, _ = sum_buffers(name)
+        half[...] = (parts[name][far].astype(F32) + pair_in[1].astype(F32)).astype(BF16)
+        sum_copy(name, 2).start()
+
+    def sum_finish(name):
+        sum_copy(name, 1).wait_recv()
+        sum_copy(name, 2).wait_recv()
+        pair_in, _, far_in = sum_buffers(name)
+        total = parts[name][rank].astype(F32) + pair_in[0].astype(F32)
+        return total + far_in[...].astype(F32)
+
+    def sum_sent(name):
+        for hop in range(3):
+            sum_copy(name, hop).wait_send()
+
+    shared = {
+        "c": s.c,
+        "ft": s.f_t,
+        "fq": s.f_q,
+        "gca": s.f_t,
+        "gsat": s.gsa_t,
+        "gsaq": s.f_q,
+        "out": s.gy,
+        "sg": s.x,
+    }
+
+    def share_copy(name, hop):
+        ref = shared[name]
+        index, device = ((rank, far), (rank, beside), (far, beside))[hop]
+        return remote(
+            ref.at[index],
+            ref.at[index],
+            (s.share_send, s.share_recv),
+            (SHARES.index(name), hop),
+            (place, device),
+        )
+
+    def share_start(name):
+        share_copy(name, 0).start()
+        share_copy(name, 1).start()
+
+    def share_forward(name):
+        share_copy(name, 0).wait_recv()
+        share_copy(name, 2).start()
+
+    def share_finish(name):
+        share_copy(name, 1).wait_recv()
+        share_copy(name, 2).wait_recv()
+
+    def share_sent(name):
+        for hop in range(3):
+            share_copy(name, hop).wait_send()
+
+    def vec(index):
+        return s.vecs[index : index + 1, :]
+
+    def column_total(values):
+        return jnp.sum(values.astype(F32), axis=0, keepdims=True)
+
+    def row_at(row):
+        return pl.ds(pl.multiple_of(row * length, length), length)
+
+    def put_stat(index, values, weight):
+        total = jnp.sum(
+            jnp.sum(values * values, axis=1, keepdims=True) * weight, axis=0, keepdims=True
+        )
+        s.small[10:11, :] += jnp.where(lanes(z.model) == index, total, 0.0)
+
+    load_x = pltpu.make_async_copy(s.x_h, s.x, s.load_sem.at[0])
+    load_gy = pltpu.make_async_copy(s.gy_h, s.gy, s.load_sem.at[1])
+    load_x.start()
+    barrier = pltpu.get_barrier_semaphore()
+    partners = [along(step) for step in range(1, lines)] + [
+        across,
+        (place, beside),
+        (place, far),
+    ]
+    for partner in partners:
+        pl.semaphore_signal(barrier, inc=1, device_id=partner, device_id_type=MESH)
+    pl.semaphore_wait(barrier, len(partners))
+    gather_start("vec")
+    gather_start("self")
+    gather_start("kv")
+    load_gy.start()
+
+    chunk_count = z.features // CHUNK
+    tail = z.features - chunk_count * CHUNK
+
+    def load_chunk(index):
+        slot = lax.rem(index, CHUNKS_HELD)
+        return pltpu.make_async_copy(
+            s.feat_h.at[pl.ds(pl.multiple_of(index * CHUNK, CHUNK), CHUNK)],
+            s.chunk.at[slot],
+            s.chunk_sem.at[slot],
+        )
+
+    load_tail = pltpu.make_async_copy(
+        s.feat_h.at[pl.ds(chunk_count * CHUNK, tail)], s.tail, s.load_sem.at[2]
+    )
+    for index in range(CHUNKS_HELD):
+        load_chunk(index).start()
+    load_tail.start()
+
+    s.small[...] = jnp.zeros_like(s.small)
+    gather_forward("vec")
+    gather_finish("vec")
+    own = z.model // count
+    for index in range(count):
+        s.vecs[:, index * own : (index + 1) * own] = s.w_vec[
+            index * 16 : (index + 1) * 16, :own
+        ].astype(F32)
+    load_x.wait()
+
+    @pl.loop(0, rows)
+    def _(row):
+        normed, _ = norm_parts(s.x[row].astype(F32))
+        s.a[row_at(row), :] = (normed * vec(0) + vec(1)).astype(BF16)
+
+    s.x_own[...] = s.x[rank]
+    weight_own = s.weight[...]
+    weight_query, weight_text = weight_own[:query], weight_own[query:]
+    s.small[10:11, :] += jnp.where(
+        lanes(z.model) == 4, jnp.sum(weight_own, axis=0, keepdims=True), 0.0
+    )
+    put_stat(0, s.x_own[...].astype(F32), weight_own)
+
+    gather_forward("self")
+    gather_start("cross")
+    gather_finish("self")
+    widen(s.m_self, s.w_self, 4)
+
+    def self_mask(row):
+        return s.query_code[row_at(row), :] == s.key_code[pl.ds(row, 1), :]
+
+    def send_order(step):
+        chip_at = chip + (1 - 2 * chip) * (1 - step // 2)
+        core_at = core + (1 - 2 * core) * (1 - lax.rem(step, 2))
+        return chip_at * 2 + core_at
+
+    @pl.loop(0, rows)
+    def _(step):
+        row = send_order(step)
+        at = row_at(row)
+        qkv = dot(s.a[at, :], s.w_self[:, : 3 * WIDE]) + s.bias[0:1, :]
+        low = qkv.astype(BF16)
+        s.qkv[at, :] = low
+        queries = spread(low[:, :WIDE] * jnp.asarray(z.scale, BF16), heads)
+        scores = dot_columns(queries, low[:, WIDE : 2 * WIDE])
+        mask = self_mask(row)
+        scores = jnp.concatenate(
+            [
+                jnp.where(mask, scores[head * length : (head + 1) * length], MASKED)
+                for head in range(heads)
+            ],
+            axis=0,
+        )
+        probs = softmax(scores).astype(BF16)
+        s.p_self[row] = probs
+        mixed = fold(dot(probs, low[:, 2 * WIDE :]), heads, length).astype(BF16)
+        s.o[at, :] = mixed
+        s.part_row[row] = dot_columns(mixed, s.w_self[:, 3 * WIDE :]).astype(BF16)
+
+        @pl.when(step == 0)
+        def _():
+            sum_copy("self", 0).start()
+
+        @pl.when(step == 2)
+        def _():
+            sum_copy("self", 1).start()
+
+    sum_forward("self")
+    gather_forward("kv")
+    gather_start("in1")
+    gather_start("out1")
+    gather_finish("kv")
+    widen(s.m_kv, s.w_kv, 2)
+
+    def project(values):
+        return dot(values, s.w_kv[...]) + s.bias[2:3, : 2 * WIDE]
+
+    def project_chunk(index):
+        load_chunk(index).wait()
+        result = project(s.chunk[lax.rem(index, CHUNKS_HELD)])
+
+        @pl.when(index + CHUNKS_HELD < chunk_count)
+        def _():
+            load_chunk(index + CHUNKS_HELD).start()
+
+        for tile in range(2 * WIDE // 128):
+            s.stage[tile // 2, (tile % 2) * CHUNK : (tile % 2 + 1) * CHUNK, :] = result[
+                :, tile * 128 : (tile + 1) * 128
+            ]
+        keys = CHUNK // z.images
+        key_at = pl.ds(pl.multiple_of(index * keys, keys), keys)
+        for image in range(z.images):
+            for tile in range(2 * WIDE // 128):
+                s.kv[image, key_at, tile * 128 : (tile + 1) * 128] = s.stage.at[tile // 2][
+                    pl.ds((tile % 2) * CHUNK + image, keys, stride=z.images), :
+                ].astype(BF16)
+
+    split = chunk_count // 2
+
+    @pl.loop(0, split)
+    def _(index):
+        project_chunk(index)
+
+    after_self = s.x_own[...].astype(F32) + sum_finish("self") + vec(6)
+    s.after_self[...] = after_self
+    normed, _ = norm_parts(after_self[:query])
+    s.c[rank] = (normed * vec(2) + vec(3)).astype(BF16)
+    share_start("c")
+    normed, _ = norm_parts(after_self[query:])
+    s.f_t[rank] = (normed * vec(4) + vec(5)).astype(BF16)
+    share_start("ft")
+    put_stat(1, after_self, weight_own)
+    put_stat(2, after_self[query:], weight_text)
+    gather_forward("cross")
+    gather_start("in0")
+    gather_start("out0")
+    share_forward("c")
+
+    @pl.loop(split, chunk_count)
+    def _(index):
+        project_chunk(index)
+
+    load_tail.wait()
+    last = project(s.tail[...])
+    first_row = lax.broadcasted_iota(jnp.int32, (tail, 1), 0) == 0
+    for image in range(z.images):
+        s.kv[image, z.keys - 1 :, :] = jnp.where(
+            first_row, jnp.broadcast_to(last[image : image + 1, :], last.shape), 0.0
+        ).astype(BF16)
+    for index in range(CHUNKS_HELD):
+        load_chunk(index).start()
+    gather_finish("cross")
+    widen(s.m_cross, s.w_cross, 2)
+    share_forward("ft")
+    share_finish("c")
+    queries_total = rows * query
+    cross_query = dot(s.c[...].reshape(queries_total, z.model), s.w_cross[:, :WIDE])
+    s.qc[...] = (cross_query + s.bias[1:2, :WIDE]).astype(BF16).reshape(s.qc.shape)
+    is_key = lanes(PADDED_KEYS) < z.keys
+
+    def all_slots(ref):
+        return ref[...].reshape(queries_total, WIDE)
+
+    def cross_queries(image):
+        values = s.qc[s.slot_of[image]]
+        return spread(values * jnp.asarray(z.scale, BF16), heads)
+
+    unroll = 4
+
+    @pl.loop(0, z.images // unroll)
+    def _(group):
+        for inner in range(unroll):
+            image = group * unroll + inner
+            scores = dot_columns(cross_queries(image), s.kv[image, :, :WIDE])
+            probs = softmax(jnp.where(is_key, scores, MASKED)).astype(BF16)
+            s.p_cross[image] = probs
+            mixed = fold(dot(probs, s.kv[image, :, WIDE:]), heads, QUERIES)
+            s.oc_image[image] = mixed.astype(BF16)
+
+    @pl.loop(0, z.images)
+    def _(slot):
+        s.oc[slot] = s.oc_image[s.image_of[slot]]
+
+    s.part_q[...] = (
+        dot_columns(all_slots(s.oc), s.w_cross[:, WIDE:]).astype(BF16).reshape(s.part_q.shape)
+    )
+    sum_copy("cross", 0).start()
+    sum_copy("cross", 1).start()
+    sum_forward("cross")
+    share_finish("ft")
+
+    f_of = {0: s.f_q, 1: s.f_t}
+    w_in = {0: s.m_in0, 1: s.m_in1}
+    w_out = {0: s.m_out0, 1: s.m_out1}
+    load_gy.wait()
+
+    def grad_rows(kind, row):
+        return s.gy[row, kind * query : (kind + 1) * query, :]
+
+    def feed_forward(kind, part, send):
+        for pair in (1 - chip, chip):
+            values = f_of[kind][pl.ds(pair * 2, 2)].reshape(2 * query, z.model)
+            grads = jnp.concatenate(
+                [grad_rows(kind, pair * 2), grad_rows(kind, pair * 2 + 1)], axis=0
+            )
+            up = dot(values, w_in[kind][...]) + s.bias[3 + kind : 4 + kind, :]
+            share = 0.5 * (1.0 + lax.erf(up * (0.5**0.5)))
+            hidden = (up * share).astype(BF16)
+            slope = share + up * (jnp.exp(-0.5 * up * up) * ((0.5 / math.pi) ** 0.5))
+            grad_up = (dot(grads, w_out[kind][...]) * slope).astype(BF16)
+            at = pl.ds(pl.multiple_of(pair * 2 * query, 2 * query), 2 * query)
+            s.hid[at, :] = hidden
+            s.gu[at, :] = grad_up
+            s.small[20 + kind : 21 + kind, :] += column_total(grad_up)
+            back = dot_columns(grad_up, w_in[kind][...]).astype(BF16)
+            part[pl.ds(pair * 2, 2)] = back.reshape(2, query, z.model)
+            send(pair)
+            out = dot_columns(hidden, w_out[kind][...]).astype(BF16)
+            out = out.reshape(2, query, z.model)
+            s.part_row[pl.ds(pair * 2, 2), kind * query : (kind + 1) * query, :] = out
+
+    def weight_terms(kind):
+        values = f_of[kind][...].reshape(queries_total, z.model)
+        grads = jnp.concatenate([grad_rows(kind, row) for row in range(rows)], axis=0)
+        for name, left, right in (
+            ("in%d" % kind, values, s.gu[...]),
+            ("out%d" % kind, grads, s.hid[...]),
+        ):
+            gather_sent(name)
+            for at in range(0, z.model, WIDE):
+                whole[name][at : at + WIDE, :] = dot_rows(left[:, at : at + WIDE], right).astype(
+                    BF16
+                )
+
+    gather_forward("in1")
+    gather_forward("out1")
+    gather_finish("in1")
+    gather_finish("out1")
+    sum_sent("self")
+    hops = iter((0, 1))
+    feed_forward(1, s.part_t, lambda pair: sum_copy("gft", next(hops)).start())
+    after_query = s.after_self[:query, :] + sum_finish("cross") + vec(7)
+    s.after_query[...] = after_query
+    normed, _ = norm_parts(after_query)
+    s.f_q[rank] = (normed * vec(4) + vec(5)).astype(BF16)
+    share_start("fq")
+    sum_forward("gft")
+    put_stat(2, after_query, weight_query)
+    weight_terms(1)
+    share_sent("ft")
+    share_forward("fq")
+    gather_forward("in0")
+    gather_forward("out0")
+
+    def own_back(total, after, grads, slot):
+        normed, scale = norm_parts(after)
+        s.small[4:5, :] += column_total(total * normed)
+        s.small[5:6, :] += column_total(total)
+        s.small[slot : slot + 1, :] += column_total(grads)
+        return grads.astype(F32) + norm_grad(normed, scale, vec(4), total)
+
+    grad_text = own_back(
+        sum_finish("gft"), s.after_self[query:, :], grad_rows(1, rank), 9
+    )
+    s.g_own[query:, :] = grad_text
+    grad_text_low = grad_text.astype(BF16)
+    s.gsa_t[rank] = grad_text_low
+    s.small[6:7, :] += column_total(grad_text_low)
+    share_start("gsat")
+    gather_finish("in0")
+    gather_finish("out0")
+    scatter_start("in1")
+    scatter_start("out1")
+    sum_sent("cross")
+    share_finish("fq")
+    hops = iter((0, 1))
+    feed_forward(0, s.part_q, lambda pair: sum_copy("gfq", next(hops)).start())
+    sum_forward("gfq")
+    share_forward("gsat")
+    weight_terms(0)
+    share_sent("fq")
+    scatter_start("in0")
+    scatter_start("out0")
+    grad_query = own_back(sum_finish("gfq"), s.after_query[...], grad_rows(0, rank), 8)
+    s.g_own[:query, :] = grad_query
+    grad_query_low = grad_query.astype(BF16)
+    s.f_t[rank] = grad_query_low
+    s.small[7:8, :] += column_total(grad_query_low)
+    share_start("gca")
+    sum_copy("out", 0).start()
+    sum_copy("out", 1).start()
+    share_finish("gsat")
+    scatter_forward("in1")
+    share_forward("gca")
+    sum_forward("out")
+    share_finish("gca")
+
+    grad_mixed = dot(s.f_t[...].reshape(queries_total, z.model), s.w_cross[:, WIDE:])
+    s.goc[...] = grad_mixed.astype(BF16).reshape(s.goc.shape)
+
+    def stage_put(image, values):
+        for tile in range(WIDE // 128):
+            s.stage.at[tile][pl.ds(image, PADDED_KEYS, stride=z.images), :] = values[
+                :, tile * 128 : (tile + 1) * 128
+            ]
+
+    @pl.loop(0, z.images // unroll)
+    def _(group):
+        for inner in range(unroll):
+            image = group * unroll + inner
+            grads = spread(s.goc[s.slot_of[image]], heads)
+            probs = s.p_cross[image]
+            wide = probs.astype(F32)
+            grad_probs = dot_columns(grads, s.kv[image, :, WIDE:])
+            delta = jnp.sum(wide * grad_probs, axis=-1, keepdims=True)
+            grad_scores = (wide * (grad_probs - delta)).astype(BF16)
+            mixed = fold(dot(grad_scores, s.kv[image, :, :WIDE]), heads, QUERIES) * z.scale
+            s.kv[image, : heads * QUERIES, :PADDED_KEYS] = grad_scores
+            s.oc_image[image] = mixed.astype(BF16)
+
+    @pl.loop(0, z.images)
+    def _(slot):
+        s.gqc[slot] = s.oc_image[s.image_of[slot]]
+
+    sum_sent("gfq")
+    s.part_q[...] = (
+        dot_columns(all_slots(s.gqc), s.w_cross[:, :WIDE]).astype(BF16).reshape(s.part_q.shape)
+    )
+    sum_copy("gc", 0).start()
+    sum_copy("gc", 1).start()
+    s.small[18:19, :WIDE] += column_total(all_slots(s.gqc))
+    sum_forward("gc")
+    scatter_forward("out1")
+
+    after_ffn_sum = sum_finish("out")
+    after_query_out = s.after_query[...] + after_ffn_sum[:query] + vec(8)
+    after_text_out = s.after_self[query:, :] + after_ffn_sum[query:] + vec(9)
+    put_stat(3, after_query_out, weight_query)
+    put_stat(3, after_text_out, weight_text)
+    s.gy[rank, :query, :] = after_query_out.astype(BF16)
+    s.gy[rank, query:, :] = after_text_out.astype(BF16)
+
+    def key_grad(image):
+        grad_scores = s.kv[image, : heads * QUERIES, :PADDED_KEYS]
+        return dot_rows(grad_scores, cross_queries(image))
+
+    def value_grad(image):
+        grads = spread(s.goc[s.slot_of[image]], heads)
+        return dot_rows(s.p_cross[image], grads)
+
+    def features_pass(grad_of):
+        @pl.loop(0, z.images // unroll)
+        def _(group):
+            for inner in range(unroll):
+                image = group * unroll + inner
+                stage_put(image, grad_of(image))
+
+        def grads_at(at):
+            return jnp.concatenate(
+                [s.stage[tile, at, :].astype(BF16) for tile in range(WIDE // 128)], axis=1
+            )
+
+        s.turned[...] = dot_rows(grads_at(pl.ds(chunk_count * CHUNK, tail)), s.tail[...])
+        s.col_sum[...] = column_total(grads_at(pl.ds(chunk_count * CHUNK, tail)))
+
+        @pl.loop(0, chunk_count)
+        def _(index):
+            load_chunk(index).wait()
+            grads = grads_at(pl.ds(pl.multiple_of(index * CHUNK, CHUNK), CHUNK))
+            s.turned[...] += dot_rows(grads, s.chunk[lax.rem(index, CHUNKS_HELD)])
+            s.col_sum[...] += column_total(grads)
+
+            @pl.when(index + CHUNKS_HELD < chunk_count)
+            def _():
+                load_chunk(index + CHUNKS_HELD).start()
+
+    gather_sent("kv")
+    features_pass(key_grad)
+    for index in range(CHUNKS_HELD):
+        load_chunk(index).start()
+    turned = s.turned[...].T
+    s.m_kv[:, :128] = turned[:, :128].astype(BF16)
+    s.m_kv[:, 256:] = turned[:, 128:].astype(BF16)
+
+    cross_sum = sum_finish("gc")
+    normed, scale = norm_parts(s.after_self[:query, :])
+    s.small[2:3, :] += column_total(cross_sum * normed)
+    s.small[3:4, :] += column_total(cross_sum)
+    grad_query = s.g_own[:query, :] + norm_grad(normed, scale, vec(2), cross_sum)
+    s.g_own[:query, :] = grad_query
+    grad_query_low = grad_query.astype(BF16)
+    s.f_q[rank] = grad_query_low
+    s.small[6:7, :] += column_total(grad_query_low)
+    share_start("gsaq")
+    share_start("out")
+    low_half = lanes(128) < HEAD
+    gather_sent("cross")
+    grad_cq = dot_rows(s.c[...].reshape(queries_total, z.model), all_slots(s.gqc))
+    grad_co = dot_rows(s.f_t[...].reshape(queries_total, z.model), all_slots(s.oc))
+    s.m_cross[:, :128] = grad_cq[:, :128].astype(BF16)
+    s.m_cross[:, 128:256] = grad_co[:, :128].astype(BF16)
+    s.m_cross[:, 256:] = jnp.where(
+        low_half, grad_cq[:, 128:], pltpu.roll(grad_co[:, 128:], HEAD, 1)
+    ).astype(BF16)
+    scatter_start("cross")
+    share_forward("gsaq")
+    scatter_forward("in0")
+    share_finish("gsaq")
+    sum_sent("out")
+
+    @pl.loop(0, rows)
+    def _(step):
+        row = send_order(step)
+        at = row_at(row)
+        grads = jnp.concatenate([s.f_q[row], s.gsa_t[row]], axis=0)
+        low = s.qkv[at, :]
+        queries = spread(low[:, :WIDE] * jnp.asarray(z.scale, BF16), heads)
+        grad_mixed = dot(grads, s.w_self[:, 3 * WIDE :]).astype(BF16)
+        grad_mixed = spread(grad_mixed, heads)
+        probs = s.p_self[row]
+        wide = probs.astype(F32)
+        grad_probs = dot_columns(grad_mixed, low[:, 2 * WIDE :])
+        delta = jnp.sum(wide * grad_probs, axis=-1, keepdims=True)
+        grad_scores = (wide * (grad_probs - delta)).astype(BF16)
+        grad_q = fold(dot(grad_scores, low[:, WIDE : 2 * WIDE]), heads, length) * z.scale
+        grad_k = dot_rows(grad_scores, queries)
+        grad_v = dot_rows(probs, grad_mixed)
+        grad_low = jnp.concatenate([grad_q, grad_k, grad_v], axis=1).astype(BF16)
+        s.qkv[at, :] = grad_low
+        s.small[16:17, :WIDE] += column_total(grad_low[:, :WIDE])
+        s.small[17:18, :WIDE] += column_total(grad_low[:, 2 * WIDE :])
+        s.part_row[row] = dot_columns(grad_low, s.w_self[:, : 3 * WIDE]).astype(BF16)
+
+        @pl.when(step == 0)
+        def _():
+            sum_copy("ga", 0).start()
+
+        @pl.when(step == 2)
+        def _():
+            sum_copy("ga", 1).start()
+
+    sum_forward("ga")
+    share_forward("out")
+
+    gather_sent("self")
+    grads_all = [
+        dot_rows(s.a[...], s.qkv[:, i * WIDE : (i + 1) * WIDE]) for i in range(3)
+    ]
+    grad_stream = jnp.concatenate(
+        [ref[row] for row in range(rows) for ref in (s.f_q, s.gsa_t)], axis=0
+    )
+    grads_all.append(dot_rows(grad_stream, s.o[...]))
+    for i, value in enumerate(grads_all):
+        s.m_self[:, i * 128 : (i + 1) * 128] = value[:, :128].astype(BF16)
+    for i in range(2):
+        s.m_self[:, (4 + i) * 128 : (5 + i) * 128] = jnp.where(
+            low_half, grads_all[2 * i][:, 128:], pltpu.roll(grads_all[2 * i + 1][:, 128:], HEAD, 1)
+        ).astype(BF16)
+    scatter_start("self")
+    scatter_forward("out0")
+    scatter_forward("cross")
+
+    self_sum = sum_finish("ga")
+    normed, scale = norm_parts(s.x_own[...].astype(F32))
+    s.small[0:1, :] += column_total(self_sum * normed)
+    s.small[1:2, :] += column_total(self_sum)
+    s.x[rank] = (s.g_own[...] + norm_grad(normed, scale, vec(0), self_sum)).astype(BF16)
+    share_start("sg")
+
+    features_pass(value_grad)
+    s.small[19:20, :WIDE] += s.col_sum[...]
+    turned = s.turned[...].T
+    s.m_kv[:, 128:256] = turned[:, :128].astype(BF16)
+    s.m_kv[:, 256:] = jnp.where(
+        low_half, s.m_kv[:, 256:].astype(F32), pltpu.roll(turned[:, 128:], HEAD, 1)
+    ).astype(BF16)
+    scatter_start("kv")
+    share_forward("sg")
+
+    def small_copy(source, hop, device):
+        target = s.small_in.at[hop] if source is s.small else s.small_in.at[hop, pl.ds(0, 16)]
+        return remote(source, target, (s.small_send, s.small_recv), (hop,), device)
+
+    shared_rows = s.small.at[pl.ds(0, 16)]
+    for hop, device in enumerate(((place, beside), (place, far))):
+        item = small_copy(shared_rows, hop, device)
+        item.start()
+        item.wait()
+        s.small[:16, :] += s.small_in[hop, :16, :]
+    scatter_forward("self")
+    item = small_copy(s.small, 2, across)
+    item.start()
+    item.wait()
+    s.small[...] += s.small_in[2]
+    items = [small_copy(s.small, 2 + step, along(step)) for step in range(1, lines)]
+    for item in items:
+        item.start()
+    scatter_forward("kv")
+    share_finish("out")
+    store_out = pltpu.make_async_copy(s.gy, s.out_h, s.load_sem.at[3])
+    store_out.start()
+    share_finish("sg")
+    store_sg = pltpu.make_async_copy(s.x, s.sg_h, s.load_sem.at[4])
+    store_sg.start()
+    total = s.small[...]
+    for step in range(1, lines):
+        items[step - 1].wait_recv()
+        total = total + s.small_in[2 + step]
+    s.small_out[...] = total
+    for name in TERMS:
+        scatter_finish(name)
+    for item in items:
+        item.wait_send()
+    gather_sent("vec")
+    for name in ("gft", "gc", "ga"):
+        sum_sent(name)
+    for name in SHARES:
+        if name not in ("ft", "fq"):
+            share_sent(name)
+    store_out.wait()
+    store_sg.wait()
+
+
+def layer(
+    stream_in,
+    features,
+    image_index,
+    text_segment,
+    text_valid,
+    self_qkv,
+    self_out,
+    cross_q,
+    cross_kv,
+    cross_out,
+    ffn_in,
+    ffn_out,
+    vectors,
+    head_bias,
+    ffn_bias,
+    out_grad,
+):
+    count = lax.axis_size("dp")
+    tokens, model = stream_in.shape
+    width, hidden = self_qkv.shape[2], ffn_in.shape[2]
+    fan, feat_fan = ffn_in.shape[1], cross_kv.shape[1]
+    rows, text = text_segment.shape
+    images, keys, feat = features.shape
+    query = SLOTS * QUERIES
+    z = types.SimpleNamespace(
+        count=count,
+        rows=rows,
+        width=width,
+        heads=width // HEAD,
+        fan=fan,
+        feat_fan=feat_fan,
+        model=model,
+        features=images * keys,
+        images=images,
+        keys=keys,
+        scale=HEAD**-0.5,
+    )
+    lines = count // 2
+
+    def wide(row):
+        return jnp.pad(row.astype(F32), (0, WIDE - width))
+
+    none = jnp.zeros((WIDE,), F32)
+    bias = jnp.stack(
+        [
+            jnp.concatenate([wide(head_bias[0]), none, wide(head_bias[1])]),
+            jnp.concatenate([wide(head_bias[2]), none, none]),
+            jnp.concatenate([none, wide(head_bias[3]), none]),
+            ffn_bias[0].astype(F32),
+            ffn_bias[1].astype(F32),
+        ]
+    )
+    query_segment = jnp.arange(query, dtype=jnp.int32) // QUERIES
+    segment = jnp.concatenate(
+        [jnp.broadcast_to(query_segment, (rows, query)), text_segment], axis=1
+    )
+    valid = jnp.concatenate([jnp.ones((rows, query), jnp.int32), text_valid], axis=1)
+    key_code = jnp.where(valid == 1, segment, -1)
+    image_of = image_index.reshape(-1)
+    slot_of = jnp.argmax(image_of[None, :] == jnp.arange(images)[:, None], axis=1)
+    operands = {
+        "slot_of": slot_of.astype(jnp.int32),
+        "image_of": image_of,
+        "vec_h": jnp.pad(vectors, ((0, 6), (0, 128 - vectors.shape[1]))),
+        "self_h": pack_columns([self_qkv[0], self_qkv[1], self_qkv[2], self_out.T], 1),
+        "kv_h": pack_columns([cross_kv[0], cross_kv[1]], 1),
+        "cross_h": pack_columns([cross_q, cross_out.T], 1),
+        "ffn_h": jnp.concatenate([ffn_in, ffn_out.transpose(0, 2, 1)], axis=0).reshape(
+            4 * fan, hidden
+        ),
+        "x_h": stream_in.reshape(rows, ROW_LEN, model),
+        "gy_h": out_grad.reshape(rows, ROW_LEN, model),
+        "feat_h": features.transpose(1, 0, 2).reshape(keys * images, feat),
+        "bias": bias,
+        "query_code": segment.reshape(-1, 1),
+        "key_code": key_code,
+        "weight": lax.dynamic_index_in_dim(valid, lax.axis_index("mp"), 0, False)
+        .reshape(-1, 1)
+        .astype(F32),
+    }
+    spaces = {name: pltpu.SMEM for name in ("slot_of", "image_of")}
+    spaces |= {name: pltpu.VMEM for name in ("bias", "query_code", "key_code", "weight")}
+    results = {
+        "out_h": ((rows, ROW_LEN, model), BF16),
+        "sg_h": ((rows, ROW_LEN, model), BF16),
+        "own_self": ((fan, 4 * width), F32),
+        "own_kv": ((feat_fan, 2 * width), F32),
+        "own_cross": ((fan, 2 * width), F32),
+        "own_ffn": ((4 * fan, hidden), F32),
+        "small_out": ((24, model), F32),
+    }
+    chunk_rows = (keys + PADDED_KEYS - keys) * images
+    buffers = {
+        "w_vec": ((count * 16, 128), BF16),
+        "vecs": ((16, model), F32),
+        "m_self": ((model, 4 * width), BF16),
+        "m_kv": ((feat, 2 * width), BF16),
+        "m_cross": ((model, 2 * width), BF16),
+        "w_self": ((model, 4 * WIDE), BF16),
+        "w_kv": ((feat, 2 * WIDE), BF16),
+        "w_cross": ((model, 2 * WIDE), BF16),
+        "x": ((rows, ROW_LEN, model), BF16),
+        "x_own": ((ROW_LEN, model), BF16),
+        "gy": ((rows, ROW_LEN, model), BF16),
+        "a": ((tokens, model), BF16),
+        "qkv": ((tokens, 3 * WIDE), BF16),
+        "o": ((tokens, WIDE), BF16),
+        "p_self": ((rows, z.heads * ROW_LEN, ROW_LEN), BF16),
+        "c": ((rows, query, model), BF16),
+        "f_q": ((rows, query, model), BF16),
+        "f_t": ((rows, query, model), BF16),
+        "gsa_t": ((rows, query, model), BF16),
+        "qc": ((images, QUERIES, WIDE), BF16),
+        "gqc": ((images, QUERIES, WIDE), BF16),
+        "goc": ((images, QUERIES, WIDE), BF16),
+        "oc": ((images, QUERIES, WIDE), BF16),
+        "oc_image": ((images, QUERIES, WIDE), BF16),
+        "kv": ((images, PADDED_KEYS, 2 * WIDE), BF16),
+        "p_cross": ((images, z.heads * QUERIES, PADDED_KEYS), BF16),
+        "stage": ((WIDE // 128, PADDED_KEYS * images, 128), F32),
+        "turned": ((WIDE, feat), F32),
+        "col_sum": ((1, WIDE), F32),
+        "chunk": ((CHUNKS_HELD, CHUNK, feat), BF16),
+        "tail": ((images * keys % CHUNK, feat), BF16),
+        "hid": ((rows * query, hidden), BF16),
+        "gu": ((rows * query, hidden), BF16),
+        "part_row": ((rows, ROW_LEN, model), BF16),
+        "part_q": ((rows, query, model), BF16),
+        "part_t": ((rows, query, model), BF16),
+        "after_self": ((ROW_LEN, model), F32),
+        "after_query": ((query, model), F32),
+        "g_own": ((ROW_LEN, model), F32),
+        "small": ((24, model), F32),
+        "small_in": ((2 + lines, 24, model), F32),
+    }
+    for name in ("in0", "in1", "out0", "out1"):
+        buffers["m_" + name] = ((model, hidden), BF16)
+    for name in ("self", "out", "cross", "gft", "gfq"):
+        block = (ROW_LEN if name in ("self", "out") else query, model)
+        buffers["pin_" + name] = ((2, *block), BF16)
+        buffers["fin_" + name] = (block, BF16)
+    buffers["half_row"] = ((ROW_LEN, model), BF16)
+    buffers["half_q"] = ((query, model), BF16)
+    buffers["half_t"] = ((query, model), BF16)
+    for name in TERMS:
+        high = feat_fan if name == "kv" else fan
+        across = {"self": 4 * width, "kv": 2 * width, "cross": 2 * width}.get(name, hidden)
+        buffers["y_" + name] = ((lines, high, across), BF16)
+        buffers["z_" + name] = ((lines - 1, high, across), BF16)
+    semaphores = {
+        "own_sem": (len(PIECES),),
+        "load_sem": (5,),
+        "chunk_sem": (CHUNKS_HELD,),
+    }
+    for name in ("gl_send", "gl_recv", "gs_send", "gs_recv"):
+        semaphores[name] = (len(PIECES), lines)
+    for name in ("ss_send", "ss_recv", "sl_send", "sl_recv"):
+        semaphores[name] = (len(TERMS), lines)
+    for kind in ("send", "recv"):
+        semaphores["sum_" + kind] = (len(SUMS), 3)
+        semaphores["share_" + kind] = (len(SHARES), 3)
+        semaphores["small_" + kind] = (2 + lines,)
+    names = (*operands, *results, *buffers, *semaphores)
+    held = ("out_h", "sg_h")
+    done = pl.pallas_call(
+        functools.partial(layer_kernel, names, z),
+        out_shape=[jax.ShapeDtypeStruct(*item) for item in results.values()],
+        in_specs=[pl.BlockSpec(memory_space=spaces.get(name, pl.ANY)) for name in operands],
+        out_specs=[
+            pl.BlockSpec(memory_space=pl.ANY if name in held else pltpu.VMEM) for name in results
+        ],
+        scratch_shapes=[pltpu.VMEM(*item) for item in buffers.values()]
+        + [pltpu.SemaphoreType.DMA(item) for item in semaphores.values()],
+        compiler_params=pltpu.CompilerParams(
+            collective_id=0, has_side_effects=True, vmem_limit_bytes=VMEM_LIMIT
+        ),
+    )(*operands.values())
+    out_all, grad_all, own_self, own_kv, own_cross, own_ffn, small = done
+    grad_q, grad_k, grad_v, grad_out = unpack_columns(own_self, 4, width)
+    grad_cq, grad_co = unpack_columns(own_cross, 2, width)
+    own_ffn = own_ffn.reshape(4, fan, hidden)
+    stats = small[10, :5]
+    return (
+        out_all.reshape(tokens, model),
+        grad_all.reshape(tokens, model).astype(F32),
+        jnp.stack([grad_q, grad_k, grad_v]),
+        grad_out.T,
+        grad_cq,
+        jnp.stack(unpack_columns(own_kv, 2, width)),
+        grad_co.T,
+        own_ffn[:2],
+        own_ffn[2:].transpose(0, 2, 1),
+        lax.dynamic_slice_in_dim(
+            small[:10], lax.axis_index("dp") * vectors.shape[1], vectors.shape[1], axis=1
+        ),
+        small[16:20, :width],
+        small[20:22, :hidden],
+        jnp.sqrt(stats[:4] / (stats[4] * model)),
+    )
 
 
 def layer_norm(values, gain_row, shift_row):
@@ -427,4 +1536,13 @@
         P(None, "mp"),
         P(),
     )
-    return jax.shard_map(body, mesh=mesh, in_specs=in_specs, out_specs=out_specs, check_vma=False)
+
+    def apply(*args):
+        fan = args[5].shape[1] // mesh.shape["dp"]
+        whole_tiles = fan % 16 == 0 and fan <= 128 and mesh.shape["dp"] % 2 == 0
+        run = layer if whole_tiles and mesh.shape["mp"] == 4 else body
+        return jax.shard_map(
+            run, mesh=mesh, in_specs=in_specs, out_specs=out_specs, check_vma=False
+        )(*args)
+
+    return apply

time: 1330 us -> 264 us (0.20)
  the two profiles are of different devices: /device:TPU:0 before, /device:TPU:24 now
where the time goes in v2:
time: 264 us; the launch traced here: 263 us
  Pallas kernels  237 us (90%)
  local copies, waits for them, and re-layouts  13.9 us (5%)
  other arithmetic  10.4 us (4%)
    pallas_call x1, Pallas kernels, layer(): pl.pallas_call(functools.partial(layer_kernel, names, z), out_shape=[jax....  237 us

profile of v2, /device:TPU:24, one launch (start us, length us, event | category | flops | bytes accessed | tf_op | source)
XLA Modules:
  0.0 263.1 jit_solution(7306301275989431958)
XLA Ops:
  0.7 1.4 iota_reduce_fusion
  2.1 1.3 pad.30.refs_2_
  3.3 0.9 slice_bitcast_fusion.2
  4.2 0.9 copy.40
  5.2 0.8 concatenate.52.refs_3_
  6.0 0.9 slice_bitcast_fusion.1
  7.0 0.7 pad_maximum_fusion.3.refs_4_
  7.9 0.7 pad_maximum_fusion.5.refs_5_
  8.6 0.9 pad_maximum_fusion
  9.6 0.6 stack.42.refs_10_
  10.3 0.6 fusion
  10.9 1.0 copy.47
  11.9 0.8 copy.43.refs_13_
  12.7 237.0 %shard_map.255 = (bf16[4,256,768]{2,1,0:T(8,128)(2,1)}, bf16[4,256,768]{2,1,0:T(8,128)(2,1)}, f32[96,768]{1,0:T(8,128)}, f32[176,384]{1,0:T(8,128)}, f32[96,384]...) custom-call(s32[16]{0:T(128)} %get-tuple-element.21.refs_0_, s32[16]{0:T(128)} %bitcast.67, ...), custom_call_target="tpu_custom_call" | custom-call | tf_op jit(solution)/shard_map/pallas_call | solution.py:1089
  249.8 3.3 %bitcast_convert_fusion = f32[1024,768]{1,0:T(8,128)} fusion(bf16[4,256,768]{2,1,0:T(8,128)(2,1)} %get-tuple-element.23), kind=kLoop, calls=%fused_computation | loop fusion | flops 786432 | bytes 4718592 | tf_op jit(solution)/shard_map/convert_element_type | solution.py:1109
  253.3 0.7 pad_maximum_fusion.2
  254.1 0.7 copy.44
  254.9 0.6 pad_maximum_fusion.4
  255.7 0.8 pad_maximum_fusion.1
  256.5 0.7 copy.45
  257.2 1.1 fusion.4
  258.3 0.7 constant_dynamic-slice_fusion
  259.6 0.6 slice.210
  262.0 1.1 copy.49
  (76 shorter events, 2.4 us)
Async XLA Ops:
  0.6 7.1 %copy-start.7 = (bf16[192,96]{1,0:T(8,128)(2,1)S(1)}, bf16[192,96]{1,0:T(8,128)(2,1)}, u32[]{:S(2)}) copy-start(bf16[192,96]{1,0:T(8,128)(2,1)} %param.25) | copy-start | bytes 110596
  0.7 7.2 %slice-start = ((bf16[96,192]{1,0:T(8,128)(2,1)}), bf16[96,64]{1,0:T(8,128)(2,1)S(1)}, s32[]{:S(2)}) async-start(bf16[96,192]{1,0:T(8,128)(2,1)} %param.23), calls=%async_computation | async-start | bytes 49152 | tf_op jit(solution)/shard_map/slice | solution.py:92
  0.7 7.2 %slice-start.1 = ((bf16[96,192]{1,0:T(8,128)(2,1)}), bf16[96,128]{1,0:T(8,128)(2,1)S(1)}, s32[]{:S(2)}) async-start(bf16[96,192]{1,0:T(8,128)(2,1)} %param.23), calls=%async_computation.1 | async-start | bytes 49152 | tf_op jit(solution)/shard_map/slice | solution.py:91
  0.7 7.9 %copy-start.4 = (bf16[2,768,96]{1,2,0:T(8,128)(2,1)S(1)}, bf16[2,768,96]{1,2,0:T(8,128)(2,1)}, u32[]{:S(2)}) copy-start(bf16[2,768,96]{1,2,0:T(8,128)(2,1)} %param.27) | copy-start | bytes 884740
  0.7 7.9 %copy-start.5 = (bf16[2,96,768]{2,1,0:T(8,128)(2,1)S(1)}, bf16[2,96,768]{2,1,0:T(8,128)(2,1)}, u32[]{:S(2)}) copy-start(bf16[2,96,768]{2,1,0:T(8,128)(2,1)} %param.26) | copy-start | bytes 884740
  5.2 4.3 %copy-start.10 = (bf16[4,192]{1,0:T(4,128)(2,1)S(1)}, bf16[4,192]{1,0:T(4,128)(2,1)}, u32[]{:S(2)}) copy-start(bf16[4,192]{1,0:T(4,128)(2,1)} %param.29) | copy-start | bytes 4612
  5.2 4.4 %copy-start.9 = (bf16[2,768]{1,0:T(2,128)(2,1)S(1)}, bf16[2,768]{1,0:T(2,128)(2,1)}, u32[]{:S(2)}) copy-start(bf16[2,768]{1,0:T(2,128)(2,1)} %param.30) | copy-start | bytes 9220
  5.2 5.1 %copy-start.11 = (s32[4,128]{1,0:T(4,128)S(1)}, s32[4,128]{1,0:T(4,128)}, u32[]{:S(2)}) copy-start(s32[4,128]{1,0:T(4,128)} %param.20) | copy-start | bytes 6148
  5.2 5.1 %copy-start.12 = (s32[4,128]{1,0:T(4,128)S(1)}, s32[4,128]{1,0:T(4,128)}, u32[]{:S(2)}) copy-start(s32[4,128]{1,0:T(4,128)} %param.19) | copy-start | bytes 6148
  249.8 3.4 %copy-start.2 = (f32[96,768]{1,0:T(8,128)S(1)}, f32[96,768]{1,0:T(8,128)}, u32[]{:S(2)}) copy-start(f32[96,768]{1,0:T(8,128)} %get-tuple-element.24) | copy-start | bytes 884740
  253.1 1.7 copy-start.6
  253.1 2.4 copy-start.3
  254.8 2.4 copy-start.1
  255.7 2.6 copy-start.8
  256.5 5.5 %copy-start = (bf16[4,256,768]{2,1,0:T(8,128)(2,1)S(1)}, bf16[4,256,768]{2,1,0:T(8,128)(2,1)}, u32[]{:S(2)}) copy-start(bf16[4,256,768]{2,1,0:T(8,128)(2,1)} %get-tuple-element.22) | copy-start | bytes 4718596

commit v3 on v2

--- a/solution.py
+++ b/solution.py
@@ -22,10 +22,11 @@
 VMEM_LIMIT = 62 * 2**20
 BF16 = jnp.bfloat16
 F32 = jnp.float32
-PIECES = ("vec", "self", "kv", "cross", "in1", "out1", "in0", "out0")
-TERMS = ("in1", "out1", "in0", "out0", "cross", "kv", "self")
-SUMS = ("self", "cross", "gft", "gfq", "out", "gc", "ga")
-SHARES = ("c", "ft", "fq", "gca", "gsat", "gsaq", "out", "sg")
+PIECES = ("vec", "self", "kv", "cross")
+TERMS = ("cross", "kv", "self")
+SUMS = ("selfq", "selft", "cross", "gft", "gfq", "out", "gc", "gaq", "gat")
+SHARES = ("c", "ft", "fq", "gca", "gsat", "gsaq", "out", "sgq", "sgt")
+RINGED = ("in1", "out1", "in0", "out0")
 WIDE = 256
 CHUNK = 256
 CHUNKS_HELD = 3
@@ -84,28 +85,6 @@
 def softmax(scores):
     exponent = jnp.exp(scores - jnp.max(scores, axis=-1, keepdims=True))
     return exponent * (1.0 / jnp.sum(exponent, axis=-1, keepdims=True))
-
-
-def pack_columns(items, axis):
-    cut = items[0].shape[axis] // 128 * 128
-    first = [lax.slice_in_dim(item, 0, cut, axis=axis) for item in items]
-    last = [lax.slice_in_dim(item, cut, item.shape[axis], axis=axis) for item in items]
-    return jnp.concatenate(first + last, axis=axis)
-
-
-def unpack_columns(packed, count, width):
-    cut = width // 128 * 128
-    rest = width - cut
-    return [
-        jnp.concatenate(
-            [
-                packed[:, i * cut : (i + 1) * cut],
-                packed[:, count * cut + i * rest : count * cut + (i + 1) * rest],
-            ],
-            axis=1,
-        )
-        for i in range(count)
-    ]
 
 
 def widen(packed, wide, count):
@@ -149,8 +128,16 @@
             device_id_type=MESH,
         )
 
+    def other_line(step):
+        at, weight = 0, 1
+        while weight < lines:
+            bit = lax.rem(line // weight, 2)
+            at = at + weight * (1 - bit if step // weight % 2 else bit)
+            weight *= 2
+        return at
+
     def along(step):
-        return (lax.rem(line + step, lines) * 2 + side, rank)
+        return (other_line(step) * 2 + side, rank)
 
     across = (line * 2 + 1 - side, rank)
 
@@ -158,16 +145,6 @@
         return ref.at[pl.ds(pl.multiple_of(index * size, 16), size)]
 
     fan, feat_fan = z.fan, z.feat_fan
-    shard = {
-        "vec": s.vec_h,
-        "self": s.self_h,
-        "kv": s.kv_h,
-        "cross": s.cross_h,
-        "in0": s.ffn_h.at[pl.ds(0, fan)],
-        "in1": s.ffn_h.at[pl.ds(fan, fan)],
-        "out0": s.ffn_h.at[pl.ds(2 * fan, fan)],
-        "out1": s.ffn_h.at[pl.ds(3 * fan, fan)],
-    }
     whole = {
         "vec": s.w_vec,
         "self": s.m_self,
@@ -178,13 +155,24 @@
         "out0": s.m_out0,
         "out1": s.m_out1,
     }
-    size = {name: fan for name in PIECES} | {"vec": 16, "kv": feat_fan}
-
-    def gather_own(name):
-        p = PIECES.index(name)
-        return pltpu.make_async_copy(
-            shard[name], block(whole[name], place, size[name]), s.own_sem.at[p]
-        )
+    size = {name: fan for name in PIECES + RINGED} | {"vec": 16, "kv": feat_fan}
+    shard = {name: block(whole[name], place, size[name]) for name in PIECES + RINGED}
+    own_in = [
+        pltpu.make_async_copy(s.ffn_in.at[kind], shard["in%d" % kind], s.own_sem.at[kind])
+        for kind in range(2)
+    ]
+
+    def pack(name, items):
+        for i, item in enumerate(items):
+            shard[name][:, i * 128 : (i + 1) * 128] = item[:, :128]
+        for i in range(0, len(items), 2):
+            at = (len(items) + i // 2) * 128
+            shard[name][:, at : at + 128] = jnp.concatenate(
+                [items[i][:, 128:], items[i + 1][:, 128:]], axis=1
+            )
+
+    def turn(values):
+        return values.astype(F32).T.astype(BF16)
 
     def gather_line(name, step):
         return remote(
@@ -196,10 +184,10 @@
         )
 
     def gather_side(name, step):
-        origin = lax.rem(line - step + lines, lines) * 2 + side
+        origin = other_line(step) * 2 + side
         target = block(whole[name], origin, size[name])
         return remote(
-            shard[name] if step == 0 else target,
+            target,
             target,
             (s.gs_send, s.gs_recv),
             (PIECES.index(name), step),
@@ -207,7 +195,6 @@
         )
 
     def gather_start(name):
-        gather_own(name).start()
         for step in range(1, lines):
             gather_line(name, step).start()
         gather_side(name, 0).start()
@@ -218,7 +205,6 @@
             gather_side(name, step).start()
 
     def gather_finish(name):
-        gather_own(name).wait()
         for step in range(lines):
             gather_side(name, step).wait_recv()
 
@@ -227,6 +213,76 @@
             gather_line(name, step).wait_send()
         for step in range(lines):
             gather_side(name, step).wait_send()
+
+    spot = line + side * (count - 1 - 2 * line)
+
+    def ring_index(at):
+        at = lax.rem(at + 2 * count, count)
+        on = at // lines
+        return (at + on * (count - 1 - 2 * at)) * 2 + on
+
+    ring_to = ((ring_index(spot + 1), rank), (ring_index(spot - 1), rank))
+
+    def ring_part(name, way):
+        cut = -(-size[name] // 32) * 16
+        return (0, cut) if way == 0 else (cut, size[name] - cut)
+
+    def ring_block(name, at, way):
+        first, high = ring_part(name, way)
+        return whole[name].at[
+            pl.ds(pl.multiple_of(ring_index(at) * size[name] + first, 16), high)
+        ]
+
+    def ring_gather(name, way, hop):
+        target = ring_block(name, spot - hop if way == 0 else spot + hop, way)
+        index = (RINGED.index(name), way, hop)
+        return remote(target, target, (s.rg_send, s.rg_recv), index, ring_to[way])
+
+    def ring_pass(names, hop):
+        for name in names:
+            for way in range(2):
+                if hop > 0:
+                    ring_gather(name, way, hop - 1).wait_recv()
+                if hop < count - 1:
+                    ring_gather(name, way, hop).start()
+
+    first_pair, last_pair = RINGED[:2], RINGED[2:]
+
+    def ring_gather_sent(name):
+        for way in range(2):
+            for hop in range(count - 1):
+                ring_gather(name, way, hop).wait_send()
+
+    def ring_scatter(name, way, hop):
+        first, high = ring_part(name, way)
+        return remote(
+            ring_block(name, spot - 1 - hop if way == 0 else spot + 1 + hop, way),
+            getattr(s, "r_" + name).at[hop, pl.ds(first, high)],
+            (s.rs_send, s.rs_recv),
+            (RINGED.index(name), way, hop),
+            ring_to[way],
+        )
+
+    def scatter_pass(names, hop):
+        for name in names:
+            for way in range(2):
+                first, high = ring_part(name, way)
+                if hop > 0:
+                    ring_scatter(name, way, hop - 1).wait_recv()
+                    landed = getattr(s, "r_" + name)[hop - 1, first : first + high, :]
+                    mine = ring_block(name, spot - 1 - hop if way == 0 else spot + 1 + hop, way)
+                    total = mine[...].astype(F32) + landed.astype(F32)
+                    if hop < count - 1:
+                        mine[...] = total.astype(BF16)
+                    else:
+                        owned[name][first : first + high, :] = total
+                if hop < count - 1:
+                    ring_scatter(name, way, hop).start()
+
+    def ring_scatter_sent(name):
+        for way in range(2):
+            for hop in range(count - 1):
+                ring_scatter(name, way, hop).wait_send()
 
     side_in = {name: getattr(s, "y_" + name) for name in TERMS}
     line_in = {name: getattr(s, "z_" + name) for name in TERMS}
@@ -242,7 +298,7 @@
     order = [*range(1, lines), 0]
 
     def scatter_side(name, step):
-        other = lax.rem(line + step, lines)
+        other = other_line(step)
         return remote(
             block(whole[name], other * 2 + 1 - side, size[name]),
             side_in[name].at[step],
@@ -252,7 +308,7 @@
         )
 
     def scatter_line(name, step):
-        other = lax.rem(line + step, lines)
+        other = other_line(step)
         return remote(
             block(whole[name], other * 2 + side, size[name]),
             line_in[name].at[step - 1],
@@ -267,7 +323,7 @@
 
     def scatter_forward(name):
         for step in range(1, lines):
-            other = lax.rem(line + step, lines)
+            other = other_line(step)
             mine = block(whole[name], other * 2 + side, size[name])
             scatter_side(name, step).wait_recv()
             mine[...] = (mine[...].astype(F32) + side_in[name][step].astype(F32)).astype(BF16)
@@ -286,67 +342,69 @@
         for step in range(lines):
             scatter_side(name, step).wait_send()
 
+    halves = {"selfq": 0, "selft": 1, "cross": 0, "gft": 1, "gfq": 0, "gc": 1, "gaq": 0, "gat": 1}
+
     def sum_buffers(name):
-        landed = {"ga": "self", "gc": "cross"}.get(name, name)
-        half = {"gft": s.half_t, "self": s.half_row, "out": s.half_row, "ga": s.half_row}
-        return getattr(s, "pin_" + landed), half.get(name, s.half_q), getattr(s, "fin_" + landed)
+        landed = {"gaq": "selfq", "gat": "selft", "gc": "cross"}.get(name, name)
+        half = s.half_row if name == "out" else s.half.at[halves[name]]
+        return getattr(s, "pin_" + landed), half, getattr(s, "fin_" + landed)
+
+    def part(name, index):
+        if name in ("selfq", "gaq"):
+            return s.part_row.at[index, pl.ds(0, query)]
+        if name in ("selft", "gat"):
+            return s.part_row.at[index, pl.ds(query, text)]
+        return {"out": s.part_row, "gft": s.part_t}.get(name, s.part_q).at[index]
 
     def sum_copy(name, hop):
-        part = parts[name]
         pair_in, half, far_in = sum_buffers(name)
         source, target, device = (
-            (part.at[diagonal], pair_in.at[1], beside),
-            (part.at[beside], pair_in.at[0], beside),
+            (part(name, diagonal), pair_in.at[1], beside),
+            (part(name, beside), pair_in.at[0], beside),
             (half, far_in, far),
         )[hop]
-        return remote(
-            source, target, (s.sum_send, s.sum_recv), (SUMS.index(name), hop), (place, device)
-        )
-
-    parts = {
-        "self": s.part_row,
-        "cross": s.part_q,
-        "gft": s.part_t,
-        "gfq": s.part_q,
-        "out": s.part_row,
-        "gc": s.part_q,
-        "ga": s.part_row,
-    }
+        index = (SUMS.index(name), hop)
+        return remote(source, target, (s.sum_send, s.sum_recv), index, (place, device))
 
     def sum_forward(name):
         sum_copy(name, 0).wait_recv()
         pair_in, half, _ = sum_buffers(name)
-        half[...] = (parts[name][far].astype(F32) + pair_in[1].astype(F32)).astype(BF16)
+        half[...] = (part(name, far)[...].astype(F32) + pair_in[1].astype(F32)).astype(BF16)
         sum_copy(name, 2).start()
 
     def sum_finish(name):
         sum_copy(name, 1).wait_recv()
         sum_copy(name, 2).wait_recv()
         pair_in, _, far_in = sum_buffers(name)
-        total = parts[name][rank].astype(F32) + pair_in[0].astype(F32)
+        total = part(name, rank)[...].astype(F32) + pair_in[0].astype(F32)
         return total + far_in[...].astype(F32)
 
-    def sum_sent(name):
-        for hop in range(3):
+    def sum_sent(name, hops=(0, 1, 2)):
+        for hop in hops:
             sum_copy(name, hop).wait_send()
 
     shared = {
         "c": s.c,
         "ft": s.f_t,
         "fq": s.f_q,
-        "gca": s.f_t,
+        "gca": s.part_t,
         "gsat": s.gsa_t,
         "gsaq": s.f_q,
         "out": s.gy,
-        "sg": s.x,
     }
 
+    def shared_part(name, index):
+        if name == "sgq":
+            return s.x.at[index, pl.ds(0, query)]
+        if name == "sgt":
+            return s.x.at[index, pl.ds(query, text)]
+        return shared[name].at[index]
+
     def share_copy(name, hop):
-        ref = shared[name]
         index, device = ((rank, far), (rank, beside), (far, beside))[hop]
         return remote(
-            ref.at[index],
-            ref.at[index],
+            shared_part(name, index),
+            shared_part(name, index),
             (s.share_send, s.share_recv),
             (SHARES.index(name), hop),
             (place, device),
@@ -394,11 +452,22 @@
     ]
     for partner in partners:
         pl.semaphore_signal(barrier, inc=1, device_id=partner, device_id_type=MESH)
+    for item in own_in:
+        item.start()
+    own = z.model // count
+    shard["vec"][...] = jnp.zeros((16, 128), BF16)
+    shard["vec"][: s.vectors.shape[0], :own] = s.vectors[...]
+    pack("self", [s.self_qkv[0], s.self_qkv[1], s.self_qkv[2], turn(s.self_out[...])])
     pl.semaphore_wait(barrier, len(partners))
     gather_start("vec")
     gather_start("self")
+    pack("kv", [s.cross_kv[0], s.cross_kv[1]])
+    pack("cross", [s.cross_q[...], turn(s.cross_out[...])])
     gather_start("kv")
-    load_gy.start()
+    gather_start("cross")
+    for kind in range(2):
+        shard["out%d" % kind][...] = s.ffn_out[kind]
+        own_in[kind].wait()
 
     chunk_count = z.features // CHUNK
     tail = z.features - chunk_count * CHUNK
@@ -411,17 +480,37 @@
             s.chunk_sem.at[slot],
         )
 
+    def load_chunks():
+        for index in range(CHUNKS_HELD):
+            load_chunk(index).start()
+
     load_tail = pltpu.make_async_copy(
         s.feat_h.at[pl.ds(chunk_count * CHUNK, tail)], s.tail, s.load_sem.at[2]
     )
-    for index in range(CHUNKS_HELD):
-        load_chunk(index).start()
+    load_chunks()
     load_tail.start()
+    load_gy.start()
 
     s.small[...] = jnp.zeros_like(s.small)
+    s.bias[...] = jnp.zeros_like(s.bias)
+    for row, at, index in ((0, 0, 0), (0, 2, 1), (1, 0, 2), (2, 1, 3)):
+        s.bias[row : row + 1, at * WIDE : at * WIDE + width] = s.head_bias[
+            index : index + 1, :
+        ].astype(F32)
+    s.bias[3:5, : z.hidden] = s.ffn_bias[...].astype(F32)
+    slots = lanes(query).astype(F32) * (1.0 / QUERIES)
+    s.code[:, :query] = jnp.broadcast_to(jnp.floor(slots), (rows, query))
+    s.code[:, query:] = jnp.where(s.valid[...] == 1, s.segment[...], -1).astype(F32)
+    same = lax.broadcasted_iota(jnp.int32, (text, text), 0) == lanes(text)
+
+    def as_column(values):
+        return jnp.sum(jnp.where(same, values.astype(F32), 0.0), axis=1, keepdims=True)
+
+    for row in range(rows):
+        s.text_codes[row] = as_column(s.segment[row : row + 1, :])
+    s.weight[...] = as_column((s.valid[pl.ds(rank, 1), :] == 1).astype(jnp.int32))
     gather_forward("vec")
     gather_finish("vec")
-    own = z.model // count
     for index in range(count):
         s.vecs[:, index * own : (index + 1) * own] = s.w_vec[
             index * 16 : (index + 1) * 16, :own
@@ -434,31 +523,42 @@
         s.a[row_at(row), :] = (normed * vec(0) + vec(1)).astype(BF16)
 
     s.x_own[...] = s.x[rank]
-    weight_own = s.weight[...]
-    weight_query, weight_text = weight_own[:query], weight_own[query:]
+    weight_query, weight_text = jnp.ones((query, 1), F32), s.weight[...]
+    weight_own = jnp.concatenate([weight_query, weight_text], axis=0)
     s.small[10:11, :] += jnp.where(
         lanes(z.model) == 4, jnp.sum(weight_own, axis=0, keepdims=True), 0.0
     )
     put_stat(0, s.x_own[...].astype(F32), weight_own)
 
     gather_forward("self")
-    gather_start("cross")
     gather_finish("self")
     widen(s.m_self, s.w_self, 4)
 
     def self_mask(row):
-        return s.query_code[row_at(row), :] == s.key_code[pl.ds(row, 1), :]
+        at = lax.broadcasted_iota(jnp.int32, (query, 1), 0).astype(F32) * (1.0 / QUERIES)
+        codes = jnp.concatenate([jnp.floor(at), s.text_codes[row]], axis=0)
+        return codes == s.code[pl.ds(row, 1), :]
 
     def send_order(step):
         chip_at = chip + (1 - 2 * chip) * (1 - step // 2)
         core_at = core + (1 - 2 * core) * (1 - lax.rem(step, 2))
         return chip_at * 2 + core_at
 
-    @pl.loop(0, rows)
-    def _(step):
+    def send_pairs(step, names):
+        @pl.when(step == 0)
+        def _():
+            for name in names:
+                sum_copy(name, 0).start()
+
+        @pl.when(step == 2)
+        def _():
+            for name in names:
+                sum_copy(name, 1).start()
+
+    def self_row(step):
         row = send_order(step)
         at = row_at(row)
-        qkv = dot(s.a[at, :], s.w_self[:, : 3 * WIDE]) + s.bias[0:1, :]
+        qkv = dot(s.a[at, :], s.w_self[:, : 3 * WIDE]) + s.bias[0:1, : 3 * WIDE]
         low = qkv.astype(BF16)
         s.qkv[at, :] = low
         queries = spread(low[:, :WIDE] * jnp.asarray(z.scale, BF16), heads)
@@ -476,19 +576,18 @@
         mixed = fold(dot(probs, low[:, 2 * WIDE :]), heads, length).astype(BF16)
         s.o[at, :] = mixed
         s.part_row[row] = dot_columns(mixed, s.w_self[:, 3 * WIDE :]).astype(BF16)
-
-        @pl.when(step == 0)
-        def _():
-            sum_copy("self", 0).start()
-
-        @pl.when(step == 2)
-        def _():
-            sum_copy("self", 1).start()
-
-    sum_forward("self")
+        send_pairs(step, ("selfq", "selft"))
+
+    pl.loop(0, rows // 2)(self_row)
     gather_forward("kv")
-    gather_start("in1")
-    gather_start("out1")
+    ring_pass(first_pair, 0)
+    ring_pass(last_pair, 0)
+    pl.loop(rows // 2, rows)(self_row)
+    sum_forward("selfq")
+    sum_forward("selft")
+    ring_pass(first_pair, 1)
+    gather_forward("cross")
+    ring_pass(last_pair, 1)
     gather_finish("kv")
     widen(s.m_kv, s.w_kv, 2)
 
@@ -515,31 +614,26 @@
                     pl.ds((tile % 2) * CHUNK + image, keys, stride=z.images), :
                 ].astype(BF16)
 
-    split = chunk_count // 2
-
-    @pl.loop(0, split)
-    def _(index):
-        project_chunk(index)
-
-    after_self = s.x_own[...].astype(F32) + sum_finish("self") + vec(6)
-    s.after_self[...] = after_self
-    normed, _ = norm_parts(after_self[:query])
+    third = chunk_count // 3
+    pl.loop(0, third)(project_chunk)
+
+    after = s.x_own[:query, :].astype(F32) + sum_finish("selfq") + vec(6)
+    s.after_self[:query, :] = after
+    normed, _ = norm_parts(after)
     s.c[rank] = (normed * vec(2) + vec(3)).astype(BF16)
     share_start("c")
-    normed, _ = norm_parts(after_self[query:])
+    put_stat(1, after, weight_query)
+    after = s.x_own[query:, :].astype(F32) + sum_finish("selft") + vec(6)
+    s.after_self[query:, :] = after
+    normed, _ = norm_parts(after)
     s.f_t[rank] = (normed * vec(4) + vec(5)).astype(BF16)
     share_start("ft")
-    put_stat(1, after_self, weight_own)
-    put_stat(2, after_self[query:], weight_text)
-    gather_forward("cross")
-    gather_start("in0")
-    gather_start("out0")
-    share_forward("c")
-
-    @pl.loop(split, chunk_count)
-    def _(index):
-        project_chunk(index)
-
+    put_stat(1, after, weight_text)
+    put_stat(2, after, weight_text)
+    ring_pass(first_pair, 2)
+    pl.loop(third, 2 * third)(project_chunk)
+    ring_pass(last_pair, 2)
+    pl.loop(2 * third, chunk_count)(project_chunk)
     load_tail.wait()
     last = project(s.tail[...])
     first_row = lax.broadcasted_iota(jnp.int32, (tail, 1), 0) == 0
@@ -547,11 +641,11 @@
         s.kv[image, z.keys - 1 :, :] = jnp.where(
             first_row, jnp.broadcast_to(last[image : image + 1, :], last.shape), 0.0
         ).astype(BF16)
-    for index in range(CHUNKS_HELD):
-        load_chunk(index).start()
+    load_chunks()
+    share_forward("c")
+    ring_pass(first_pair, 3)
     gather_finish("cross")
     widen(s.m_cross, s.w_cross, 2)
-    share_forward("ft")
     share_finish("c")
     queries_total = rows * query
     cross_query = dot(s.c[...].reshape(queries_total, z.model), s.w_cross[:, :WIDE])
@@ -561,14 +655,20 @@
     def all_slots(ref):
         return ref[...].reshape(queries_total, WIDE)
 
+    def slot_of(image):
+        slot = jnp.int32(0)
+        for other in range(1, z.images):
+            slot = jnp.where(s.image_of[other] == image, other, slot)
+        return slot
+
     def cross_queries(image):
-        values = s.qc[s.slot_of[image]]
+        values = s.qc[slot_of(image)]
         return spread(values * jnp.asarray(z.scale, BF16), heads)
 
     unroll = 4
-
-    @pl.loop(0, z.images // unroll)
-    def _(group):
+    groups = z.images // unroll
+
+    def cross_group(group):
         for inner in range(unroll):
             image = group * unroll + inner
             scores = dot_columns(cross_queries(image), s.kv[image, :, :WIDE])
@@ -577,44 +677,74 @@
             mixed = fold(dot(probs, s.kv[image, :, WIDE:]), heads, QUERIES)
             s.oc_image[image] = mixed.astype(BF16)
 
+    pl.loop(0, groups // 2)(cross_group)
+    ring_pass(last_pair, 3)
+    pl.loop(groups // 2, groups)(cross_group)
+
     @pl.loop(0, z.images)
     def _(slot):
         s.oc[slot] = s.oc_image[s.image_of[slot]]
 
+    share_forward("ft")
+    ring_pass(first_pair, 4)
+    sum_sent("selfq")
+    sum_sent("selft")
     s.part_q[...] = (
         dot_columns(all_slots(s.oc), s.w_cross[:, WIDE:]).astype(BF16).reshape(s.part_q.shape)
     )
     sum_copy("cross", 0).start()
     sum_copy("cross", 1).start()
     sum_forward("cross")
+    ring_pass(last_pair, 4)
+    ring_pass(first_pair, 5)
+    ring_pass(last_pair, 5)
+    after_query = s.after_self[:query, :] + sum_finish("cross") + vec(7)
+    s.after_query[...] = after_query
+    normed, _ = norm_parts(after_query)
+    s.f_q[rank] = (normed * vec(4) + vec(5)).astype(BF16)
+    share_start("fq")
+    put_stat(2, after_query, weight_query)
+    ring_pass(first_pair, 6)
+    ring_pass(last_pair, 6)
+    ring_pass(first_pair, 7)
+    share_forward("fq")
     share_finish("ft")
+    load_gy.wait()
+    gather_sent("self")
+    gather_sent("kv")
 
     f_of = {0: s.f_q, 1: s.f_t}
     w_in = {0: s.m_in0, 1: s.m_in1}
     w_out = {0: s.m_out0, 1: s.m_out1}
-    load_gy.wait()
 
     def grad_rows(kind, row):
         return s.gy[row, kind * query : (kind + 1) * query, :]
 
-    def feed_forward(kind, part, send):
+    def feed_forward(kind, target, send):
         for pair in (1 - chip, chip):
             values = f_of[kind][pl.ds(pair * 2, 2)].reshape(2 * query, z.model)
             grads = jnp.concatenate(
                 [grad_rows(kind, pair * 2), grad_rows(kind, pair * 2 + 1)], axis=0
             )
-            up = dot(values, w_in[kind][...]) + s.bias[3 + kind : 4 + kind, :]
+            up = dot(values, w_in[kind][...]) + s.bias[3 + kind : 4 + kind, : z.hidden]
             share = 0.5 * (1.0 + lax.erf(up * (0.5**0.5)))
             hidden = (up * share).astype(BF16)
             slope = share + up * (jnp.exp(-0.5 * up * up) * ((0.5 / math.pi) ** 0.5))
             grad_up = (dot(grads, w_out[kind][...]) * slope).astype(BF16)
             at = pl.ds(pl.multiple_of(pair * 2 * query, 2 * query), 2 * query)
-            s.hid[at, :] = hidden
-            s.gu[at, :] = grad_up
+            if kind == 0:
+                s.hid[at, :] = hidden
+                s.gu[at, :] = grad_up
+            else:
+                s.m_self[at, :] = hidden
+                cut = s.m_kv.shape[1]
+                for first in range(0, z.hidden, cut):
+                    below = pl.ds(pl.multiple_of(first // cut * queries_total + at.start, 16), at.size)
+                    s.m_kv[below, :] = grad_up[:, first : first + cut]
+            back = dot_columns(grad_up, w_in[kind][...]).astype(BF16)
+            target[pl.ds(pair * 2, 2)] = back.reshape(2, query, z.model)
+            send(pair)
             s.small[20 + kind : 21 + kind, :] += column_total(grad_up)
-            back = dot_columns(grad_up, w_in[kind][...]).astype(BF16)
-            part[pl.ds(pair * 2, 2)] = back.reshape(2, query, z.model)
-            send(pair)
             out = dot_columns(hidden, w_out[kind][...]).astype(BF16)
             out = out.reshape(2, query, z.model)
             s.part_row[pl.ds(pair * 2, 2), kind * query : (kind + 1) * query, :] = out
@@ -622,35 +752,39 @@
     def weight_terms(kind):
         values = f_of[kind][...].reshape(queries_total, z.model)
         grads = jnp.concatenate([grad_rows(kind, row) for row in range(rows)], axis=0)
+        if kind == 0:
+            hidden, grad_up = s.hid[...], s.gu[...]
+        else:
+            hidden = s.m_self[:queries_total, :]
+            grad_up = jnp.concatenate(
+                [
+                    s.m_kv[at : at + queries_total, :]
+                    for at in range(0, z.hidden // s.m_kv.shape[1] * queries_total, queries_total)
+                ],
+                axis=1,
+            )
         for name, left, right in (
-            ("in%d" % kind, values, s.gu[...]),
-            ("out%d" % kind, grads, s.hid[...]),
+            ("in%d" % kind, values, grad_up),
+            ("out%d" % kind, grads, hidden),
         ):
-            gather_sent(name)
+            ring_gather_sent(name)
             for at in range(0, z.model, WIDE):
                 whole[name][at : at + WIDE, :] = dot_rows(left[:, at : at + WIDE], right).astype(
                     BF16
                 )
 
-    gather_forward("in1")
-    gather_forward("out1")
-    gather_finish("in1")
-    gather_finish("out1")
-    sum_sent("self")
     hops = iter((0, 1))
     feed_forward(1, s.part_t, lambda pair: sum_copy("gft", next(hops)).start())
-    after_query = s.after_self[:query, :] + sum_finish("cross") + vec(7)
-    s.after_query[...] = after_query
-    normed, _ = norm_parts(after_query)
-    s.f_q[rank] = (normed * vec(4) + vec(5)).astype(BF16)
-    share_start("fq")
+    ring_pass(last_pair, 7)
+    sum_sent("cross")
+    share_finish("fq")
     sum_forward("gft")
-    put_stat(2, after_query, weight_query)
+    sum_sent("gft", (0, 1))
+    hops = iter((0, 1))
+    feed_forward(0, s.part_q, lambda pair: sum_copy("gfq", next(hops)).start())
+    sum_forward("gfq")
     weight_terms(1)
-    share_sent("ft")
-    share_forward("fq")
-    gather_forward("in0")
-    gather_forward("out0")
+    scatter_pass(first_pair, 0)
 
     def own_back(total, after, grads, slot):
         normed, scale = norm_parts(after)
@@ -659,43 +793,35 @@
         s.small[slot : slot + 1, :] += column_total(grads)
         return grads.astype(F32) + norm_grad(normed, scale, vec(4), total)
 
-    grad_text = own_back(
-        sum_finish("gft"), s.after_self[query:, :], grad_rows(1, rank), 9
-    )
+    grad_text = own_back(sum_finish("gft"), s.after_self[query:, :], grad_rows(1, rank), 9)
     s.g_own[query:, :] = grad_text
     grad_text_low = grad_text.astype(BF16)
     s.gsa_t[rank] = grad_text_low
     s.small[6:7, :] += column_total(grad_text_low)
     share_start("gsat")
-    gather_finish("in0")
-    gather_finish("out0")
-    scatter_start("in1")
-    scatter_start("out1")
-    sum_sent("cross")
-    share_finish("fq")
-    hops = iter((0, 1))
-    feed_forward(0, s.part_q, lambda pair: sum_copy("gfq", next(hops)).start())
-    sum_forward("gfq")
-    share_forward("gsat")
     weight_terms(0)
     share_sent("fq")
-    scatter_start("in0")
-    scatter_start("out0")
     grad_query = own_back(sum_finish("gfq"), s.after_query[...], grad_rows(0, rank), 8)
     s.g_own[:query, :] = grad_query
     grad_query_low = grad_query.astype(BF16)
-    s.f_t[rank] = grad_query_low
+    s.part_t[rank] = grad_query_low
     s.small[7:8, :] += column_total(grad_query_low)
     share_start("gca")
+    scatter_pass(("in1",), 1)
+    scatter_pass(last_pair, 0)
+    scatter_pass(("out1",), 1)
     sum_copy("out", 0).start()
     sum_copy("out", 1).start()
+    share_forward("gsat")
+    sum_forward("out")
+    scatter_pass(("in1",), 2)
+    scatter_pass(("in0",), 1)
+    share_forward("gca")
+    scatter_pass(("out0",), 1)
     share_finish("gsat")
-    scatter_forward("in1")
-    share_forward("gca")
-    sum_forward("out")
     share_finish("gca")
 
-    grad_mixed = dot(s.f_t[...].reshape(queries_total, z.model), s.w_cross[:, WIDE:])
+    grad_mixed = dot(s.part_t[...].reshape(queries_total, z.model), s.w_cross[:, WIDE:])
     s.goc[...] = grad_mixed.astype(BF16).reshape(s.goc.shape)
 
     def stage_put(image, values):
@@ -704,11 +830,10 @@
                 :, tile * 128 : (tile + 1) * 128
             ]
 
-    @pl.loop(0, z.images // unroll)
-    def _(group):
+    def cross_back(group):
         for inner in range(unroll):
             image = group * unroll + inner
-            grads = spread(s.goc[s.slot_of[image]], heads)
+            grads = spread(s.goc[slot_of(image)], heads)
             probs = s.p_cross[image]
             wide = probs.astype(F32)
             grad_probs = dot_columns(grads, s.kv[image, :, WIDE:])
@@ -718,19 +843,34 @@
             s.kv[image, : heads * QUERIES, :PADDED_KEYS] = grad_scores
             s.oc_image[image] = mixed.astype(BF16)
 
+    pl.loop(0, groups)(cross_back)
+
     @pl.loop(0, z.images)
     def _(slot):
         s.gqc[slot] = s.oc_image[s.image_of[slot]]
 
     sum_sent("gfq")
+    sum_sent("gft", (2,))
     s.part_q[...] = (
         dot_columns(all_slots(s.gqc), s.w_cross[:, :WIDE]).astype(BF16).reshape(s.part_q.shape)
     )
     sum_copy("gc", 0).start()
     sum_copy("gc", 1).start()
+    scatter_pass(("out1",), 2)
+    scatter_pass(("in1",), 3)
+    scatter_pass(last_pair, 2)
     s.small[18:19, :WIDE] += column_total(all_slots(s.gqc))
+    low_half = lanes(128) < HEAD
+    gather_sent("cross")
+    grad_cq = dot_rows(s.c[...].reshape(queries_total, z.model), all_slots(s.gqc))
+    grad_co = dot_rows(s.part_t[...].reshape(queries_total, z.model), all_slots(s.oc))
+    s.m_cross[:, :128] = grad_cq[:, :128].astype(BF16)
+    s.m_cross[:, 128:256] = grad_co[:, :128].astype(BF16)
+    s.m_cross[:, 256:] = jnp.where(
+        low_half, grad_cq[:, 128:], pltpu.roll(grad_co[:, 128:], HEAD, 1)
+    ).astype(BF16)
     sum_forward("gc")
-    scatter_forward("out1")
+    scatter_start("cross")
 
     after_ffn_sum = sum_finish("out")
     after_query_out = s.after_query[...] + after_ffn_sum[:query] + vec(8)
@@ -739,45 +879,47 @@
     put_stat(3, after_text_out, weight_text)
     s.gy[rank, :query, :] = after_query_out.astype(BF16)
     s.gy[rank, query:, :] = after_text_out.astype(BF16)
+    share_start("out")
 
     def key_grad(image):
         grad_scores = s.kv[image, : heads * QUERIES, :PADDED_KEYS]
         return dot_rows(grad_scores, cross_queries(image))
 
     def value_grad(image):
-        grads = spread(s.goc[s.slot_of[image]], heads)
-        return dot_rows(s.p_cross[image], grads)
-
-    def features_pass(grad_of):
-        @pl.loop(0, z.images // unroll)
+        return dot_rows(s.p_cross[image], spread(s.goc[slot_of(image)], heads))
+
+    def grads_at(at):
+        return jnp.concatenate(
+            [s.stage[tile, at, :].astype(BF16) for tile in range(WIDE // 128)], axis=1
+        )
+
+    def features_start(grad_of):
+        @pl.loop(0, groups)
         def _(group):
             for inner in range(unroll):
                 image = group * unroll + inner
                 stage_put(image, grad_of(image))
 
-        def grads_at(at):
-            return jnp.concatenate(
-                [s.stage[tile, at, :].astype(BF16) for tile in range(WIDE // 128)], axis=1
-            )
-
-        s.turned[...] = dot_rows(grads_at(pl.ds(chunk_count * CHUNK, tail)), s.tail[...])
-        s.col_sum[...] = column_total(grads_at(pl.ds(chunk_count * CHUNK, tail)))
-
-        @pl.loop(0, chunk_count)
-        def _(index):
-            load_chunk(index).wait()
-            grads = grads_at(pl.ds(pl.multiple_of(index * CHUNK, CHUNK), CHUNK))
-            s.turned[...] += dot_rows(grads, s.chunk[lax.rem(index, CHUNKS_HELD)])
-            s.col_sum[...] += column_total(grads)
-
-            @pl.when(index + CHUNKS_HELD < chunk_count)
-            def _():
-                load_chunk(index + CHUNKS_HELD).start()
-
-    gather_sent("kv")
-    features_pass(key_grad)
-    for index in range(CHUNKS_HELD):
-        load_chunk(index).start()
+        grads = grads_at(pl.ds(chunk_count * CHUNK, tail))
+        s.turned[...] = dot_rows(grads, s.tail[...])
+        s.col_sum[...] = column_total(grads)
+
+    def features_chunk(index):
+        load_chunk(index).wait()
+        grads = grads_at(pl.ds(pl.multiple_of(index * CHUNK, CHUNK), CHUNK))
+        s.turned[...] += dot_rows(grads, s.chunk[lax.rem(index, CHUNKS_HELD)])
+        s.col_sum[...] += column_total(grads)
+
+        @pl.when(index + CHUNKS_HELD < chunk_count)
+        def _():
+            load_chunk(index + CHUNKS_HELD).start()
+
+    features_start(key_grad)
+    scatter_pass(("out1",), 3)
+    scatter_pass(("in1",), 4)
+    scatter_pass(("in0",), 3)
+    pl.loop(0, chunk_count)(features_chunk)
+    load_chunks()
     turned = s.turned[...].T
     s.m_kv[:, :128] = turned[:, :128].astype(BF16)
     s.m_kv[:, 256:] = turned[:, 128:].astype(BF16)
@@ -792,24 +934,25 @@
     s.f_q[rank] = grad_query_low
     s.small[6:7, :] += column_total(grad_query_low)
     share_start("gsaq")
-    share_start("out")
-    low_half = lanes(128) < HEAD
-    gather_sent("cross")
-    grad_cq = dot_rows(s.c[...].reshape(queries_total, z.model), all_slots(s.gqc))
-    grad_co = dot_rows(s.f_t[...].reshape(queries_total, z.model), all_slots(s.oc))
-    s.m_cross[:, :128] = grad_cq[:, :128].astype(BF16)
-    s.m_cross[:, 128:256] = grad_co[:, :128].astype(BF16)
-    s.m_cross[:, 256:] = jnp.where(
-        low_half, grad_cq[:, 128:], pltpu.roll(grad_co[:, 128:], HEAD, 1)
+    scatter_pass(("out0",), 3)
+    scatter_forward("cross")
+    features_start(value_grad)
+    scatter_pass(("out1",), 4)
+    scatter_pass(("in1",), 5)
+    pl.loop(0, chunk_count)(features_chunk)
+    s.small[19:20, :WIDE] += s.col_sum[...]
+    turned = s.turned[...].T
+    s.m_kv[:, 128:256] = turned[:, :128].astype(BF16)
+    s.m_kv[:, 256:] = jnp.where(
+        low_half, s.m_kv[:, 256:].astype(F32), pltpu.roll(turned[:, 128:], HEAD, 1)
     ).astype(BF16)
-    scatter_start("cross")
     share_forward("gsaq")
-    scatter_forward("in0")
+    scatter_pass(last_pair, 4)
+    scatter_start("kv")
+    share_forward("out")
     share_finish("gsaq")
-    sum_sent("out")
-
-    @pl.loop(0, rows)
-    def _(step):
+
+    def self_back(step):
         row = send_order(step)
         at = row_at(row)
         grads = jnp.concatenate([s.f_q[row], s.gsa_t[row]], axis=0)
@@ -830,22 +973,19 @@
         s.small[16:17, :WIDE] += column_total(grad_low[:, :WIDE])
         s.small[17:18, :WIDE] += column_total(grad_low[:, 2 * WIDE :])
         s.part_row[row] = dot_columns(grad_low, s.w_self[:, : 3 * WIDE]).astype(BF16)
-
-        @pl.when(step == 0)
-        def _():
-            sum_copy("ga", 0).start()
-
-        @pl.when(step == 2)
-        def _():
-            sum_copy("ga", 1).start()
-
-    sum_forward("ga")
-    share_forward("out")
-
-    gather_sent("self")
-    grads_all = [
-        dot_rows(s.a[...], s.qkv[:, i * WIDE : (i + 1) * WIDE]) for i in range(3)
-    ]
+        send_pairs(step, ("gaq", "gat"))
+
+    scatter_pass(("out1",), 5)
+    sum_sent("out")
+    sum_sent("gc")
+    pl.loop(0, rows // 2)(self_back)
+    scatter_pass(("in1",), 6)
+    scatter_pass(last_pair, 5)
+    pl.loop(rows // 2, rows)(self_back)
+    sum_forward("gaq")
+    sum_forward("gat")
+
+    grads_all = [dot_rows(s.a[...], s.qkv[:, i * WIDE : (i + 1) * WIDE]) for i in range(3)]
     grad_stream = jnp.concatenate(
         [ref[row] for row in range(rows) for ref in (s.f_q, s.gsa_t)], axis=0
     )
@@ -857,25 +997,25 @@
             low_half, grads_all[2 * i][:, 128:], pltpu.roll(grads_all[2 * i + 1][:, 128:], HEAD, 1)
         ).astype(BF16)
     scatter_start("self")
-    scatter_forward("out0")
-    scatter_forward("cross")
-
-    self_sum = sum_finish("ga")
-    normed, scale = norm_parts(s.x_own[...].astype(F32))
-    s.small[0:1, :] += column_total(self_sum * normed)
-    s.small[1:2, :] += column_total(self_sum)
-    s.x[rank] = (s.g_own[...] + norm_grad(normed, scale, vec(0), self_sum)).astype(BF16)
-    share_start("sg")
-
-    features_pass(value_grad)
-    s.small[19:20, :WIDE] += s.col_sum[...]
-    turned = s.turned[...].T
-    s.m_kv[:, 128:256] = turned[:, :128].astype(BF16)
-    s.m_kv[:, 256:] = jnp.where(
-        low_half, s.m_kv[:, 256:].astype(F32), pltpu.roll(turned[:, 128:], HEAD, 1)
-    ).astype(BF16)
-    scatter_start("kv")
-    share_forward("sg")
+    scatter_pass(("out1",), 6)
+    scatter_forward("kv")
+    scatter_pass(("in1",), 7)
+    scatter_pass(last_pair, 6)
+
+    def stream_back(name, at):
+        total = sum_finish(name)
+        normed, scale = norm_parts(s.x_own[at, :].astype(F32))
+        s.small[0:1, :] += column_total(total * normed)
+        s.small[1:2, :] += column_total(total)
+        grad = s.g_own[at, :] + norm_grad(normed, scale, vec(0), total)
+        s.x[rank, at, :] = grad.astype(BF16)
+
+    stream_back("gaq", pl.ds(0, query))
+    share_start("sgq")
+    stream_back("gat", pl.ds(query, text))
+    share_start("sgt")
+    scatter_forward("self")
+    scatter_pass(("out1",), 7)
 
     def small_copy(source, hop, device):
         target = s.small_in.at[hop] if source is s.small else s.small_in.at[hop, pl.ds(0, 16)]
@@ -887,19 +1027,20 @@
         item.start()
         item.wait()
         s.small[:16, :] += s.small_in[hop, :16, :]
-    scatter_forward("self")
     item = small_copy(s.small, 2, across)
     item.start()
+    share_forward("sgq")
+    share_forward("sgt")
     item.wait()
     s.small[...] += s.small_in[2]
     items = [small_copy(s.small, 2 + step, along(step)) for step in range(1, lines)]
     for item in items:
         item.start()
-    scatter_forward("kv")
     share_finish("out")
     store_out = pltpu.make_async_copy(s.gy, s.out_h, s.load_sem.at[3])
     store_out.start()
-    share_finish("sg")
+    share_finish("sgq")
+    share_finish("sgt")
     store_sg = pltpu.make_async_copy(s.x, s.sg_h, s.load_sem.at[4])
     store_sg.start()
     total = s.small[...]
@@ -907,18 +1048,81 @@
         items[step - 1].wait_recv()
         total = total + s.small_in[2 + step]
     s.small_out[...] = total
+    scatter_pass(last_pair, 7)
     for name in TERMS:
         scatter_finish(name)
+    for name in RINGED:
+        ring_scatter_sent(name)
     for item in items:
         item.wait_send()
     gather_sent("vec")
-    for name in ("gft", "gc", "ga"):
+    for name in ("gaq", "gat"):
         sum_sent(name)
     for name in SHARES:
-        if name not in ("ft", "fq"):
+        if name != "fq":
             share_sent(name)
     store_out.wait()
     store_sg.wait()
+
+
+def finish_kernel(
+    out_in,
+    grad_in,
+    own_self,
+    own_kv,
+    own_cross,
+    own_ffn,
+    small,
+    out_stream,
+    stream_grad,
+    grad_qkv,
+    grad_out,
+    grad_cq,
+    grad_ckv,
+    grad_co,
+    grad_in_w,
+    grad_out_w,
+    grad_vectors,
+    grad_heads,
+    grad_hidden,
+    rms,
+):
+    out_stream[...] = out_in[...]
+    stream_grad[...] = grad_in[...].astype(F32)
+
+    def piece(packed, count, index):
+        at = (count + index // 2) * 128 + index % 2 * HEAD
+        return packed[:, index * 128 : (index + 1) * 128], packed[:, at : at + HEAD]
+
+    def put(ref, pieces):
+        ref[:, :128] = pieces[0]
+        ref[:, 128:] = pieces[1]
+
+    def put_turned(ref, pieces):
+        ref[:128, :] = pieces[0].T
+        ref[128:, :] = pieces[1].T
+
+    for index in range(3):
+        put(grad_qkv.at[index], piece(own_self, 4, index))
+    put_turned(grad_out, piece(own_self, 4, 3))
+    put(grad_cq, piece(own_cross, 2, 0))
+    put_turned(grad_co, piece(own_cross, 2, 1))
+    for index in range(2):
+        put(grad_ckv.at[index], piece(own_kv, 2, index))
+        fan = grad_in_w.shape[1]
+        grad_in_w[index] = own_ffn[index * fan : (index + 1) * fan, :]
+        grad_out_w[index] = own_ffn[(2 + index) * fan : (3 + index) * fan, :]
+    place, own = lax.axis_index("dp"), grad_vectors.shape[1]
+    total = jnp.zeros(grad_vectors.shape, F32)
+    for index in range(small.shape[1] // own):
+        mine = small[: total.shape[0], index * own : (index + 1) * own]
+        total = total + jnp.where(place == index, mine, 0.0)
+    grad_vectors[...] = total
+    grad_heads[...] = small[16:20, : grad_heads.shape[1]]
+    grad_hidden[...] = small[20:22, : grad_hidden.shape[1]]
+    stats = small[10:11, :128]
+    valid = jnp.sum(jnp.where(lanes(128) == 4, stats, 0.0), axis=1, keepdims=True)
+    rms[...] = jnp.sqrt(stats / (valid * small.shape[1]))[:, :4]
 
 
 def layer(
@@ -954,6 +1158,7 @@
         fan=fan,
         feat_fan=feat_fan,
         model=model,
+        hidden=hidden,
         features=images * keys,
         images=images,
         keys=keys,
@@ -961,49 +1166,26 @@
     )
     lines = count // 2
 
-    def wide(row):
-        return jnp.pad(row.astype(F32), (0, WIDE - width))
-
-    none = jnp.zeros((WIDE,), F32)
-    bias = jnp.stack(
-        [
-            jnp.concatenate([wide(head_bias[0]), none, wide(head_bias[1])]),
-            jnp.concatenate([wide(head_bias[2]), none, none]),
-            jnp.concatenate([none, wide(head_bias[3]), none]),
-            ffn_bias[0].astype(F32),
-            ffn_bias[1].astype(F32),
-        ]
-    )
-    query_segment = jnp.arange(query, dtype=jnp.int32) // QUERIES
-    segment = jnp.concatenate(
-        [jnp.broadcast_to(query_segment, (rows, query)), text_segment], axis=1
-    )
-    valid = jnp.concatenate([jnp.ones((rows, query), jnp.int32), text_valid], axis=1)
-    key_code = jnp.where(valid == 1, segment, -1)
-    image_of = image_index.reshape(-1)
-    slot_of = jnp.argmax(image_of[None, :] == jnp.arange(images)[:, None], axis=1)
     operands = {
-        "slot_of": slot_of.astype(jnp.int32),
-        "image_of": image_of,
-        "vec_h": jnp.pad(vectors, ((0, 6), (0, 128 - vectors.shape[1]))),
-        "self_h": pack_columns([self_qkv[0], self_qkv[1], self_qkv[2], self_out.T], 1),
-        "kv_h": pack_columns([cross_kv[0], cross_kv[1]], 1),
-        "cross_h": pack_columns([cross_q, cross_out.T], 1),
-        "ffn_h": jnp.concatenate([ffn_in, ffn_out.transpose(0, 2, 1)], axis=0).reshape(
-            4 * fan, hidden
-        ),
+        "image_of": image_index.reshape(-1),
+        "vectors": vectors,
+        "self_qkv": self_qkv,
+        "self_out": self_out,
+        "cross_q": cross_q,
+        "cross_kv": cross_kv,
+        "cross_out": cross_out,
+        "ffn_out": ffn_out.transpose(0, 2, 1),
+        "head_bias": head_bias,
+        "ffn_bias": ffn_bias,
+        "segment": text_segment,
+        "valid": text_valid,
+        "ffn_in": ffn_in,
         "x_h": stream_in.reshape(rows, ROW_LEN, model),
         "gy_h": out_grad.reshape(rows, ROW_LEN, model),
         "feat_h": features.transpose(1, 0, 2).reshape(keys * images, feat),
-        "bias": bias,
-        "query_code": segment.reshape(-1, 1),
-        "key_code": key_code,
-        "weight": lax.dynamic_index_in_dim(valid, lax.axis_index("mp"), 0, False)
-        .reshape(-1, 1)
-        .astype(F32),
     }
-    spaces = {name: pltpu.SMEM for name in ("slot_of", "image_of")}
-    spaces |= {name: pltpu.VMEM for name in ("bias", "query_code", "key_code", "weight")}
+    spaces = dict.fromkeys(operands, pltpu.VMEM) | {"image_of": pltpu.SMEM}
+    spaces |= dict.fromkeys(("ffn_in", "x_h", "gy_h", "feat_h"), pl.ANY)
     results = {
         "out_h": ((rows, ROW_LEN, model), BF16),
         "sg_h": ((rows, ROW_LEN, model), BF16),
@@ -1017,6 +1199,10 @@
     buffers = {
         "w_vec": ((count * 16, 128), BF16),
         "vecs": ((16, model), F32),
+        "bias": ((8, max(3 * WIDE, hidden)), F32),
+        "code": ((rows, ROW_LEN), F32),
+        "text_codes": ((rows, text, 1), F32),
+        "weight": ((text, 1), F32),
         "m_self": ((model, 4 * width), BF16),
         "m_kv": ((feat, 2 * width), BF16),
         "m_cross": ((model, 2 * width), BF16),
@@ -1059,20 +1245,20 @@
     }
     for name in ("in0", "in1", "out0", "out1"):
         buffers["m_" + name] = ((model, hidden), BF16)
-    for name in ("self", "out", "cross", "gft", "gfq"):
-        block = (ROW_LEN if name in ("self", "out") else query, model)
+        buffers["r_" + name] = ((count - 1, fan, hidden), BF16)
+    for name in ("selfq", "selft", "out", "cross", "gft", "gfq"):
+        block = (ROW_LEN if name == "out" else query, model)
         buffers["pin_" + name] = ((2, *block), BF16)
         buffers["fin_" + name] = (block, BF16)
     buffers["half_row"] = ((ROW_LEN, model), BF16)
-    buffers["half_q"] = ((query, model), BF16)
-    buffers["half_t"] = ((query, model), BF16)
+    buffers["half"] = ((2, query, model), BF16)
     for name in TERMS:
         high = feat_fan if name == "kv" else fan
-        across = {"self": 4 * width, "kv": 2 * width, "cross": 2 * width}.get(name, hidden)
+        across = (4 if name == "self" else 2) * width
         buffers["y_" + name] = ((lines, high, across), BF16)
         buffers["z_" + name] = ((lines - 1, high, across), BF16)
     semaphores = {
-        "own_sem": (len(PIECES),),
+        "own_sem": (2,),
         "load_sem": (5,),
         "chunk_sem": (CHUNKS_HELD,),
     }
@@ -1081,6 +1267,8 @@
     for name in ("ss_send", "ss_recv", "sl_send", "sl_recv"):
         semaphores[name] = (len(TERMS), lines)
     for kind in ("send", "recv"):
+        semaphores["rg_" + kind] = (len(RINGED), 2, count - 1)
+        semaphores["rs_" + kind] = (len(RINGED), 2, count - 1)
         semaphores["sum_" + kind] = (len(SUMS), 3)
         semaphores["share_" + kind] = (len(SHARES), 3)
         semaphores["small_" + kind] = (2 + lines,)
@@ -1089,7 +1277,7 @@
     done = pl.pallas_call(
         functools.partial(layer_kernel, names, z),
         out_shape=[jax.ShapeDtypeStruct(*item) for item in results.values()],
-        in_specs=[pl.BlockSpec(memory_space=spaces.get(name, pl.ANY)) for name in operands],
+        in_specs=[pl.BlockSpec(memory_space=spaces[name]) for name in operands],
         out_specs=[
             pl.BlockSpec(memory_space=pl.ANY if name in held else pltpu.VMEM) for name in results
         ],
@@ -1099,27 +1287,38 @@
             collective_id=0, has_side_effects=True, vmem_limit_bytes=VMEM_LIMIT
         ),
     )(*operands.values())
-    out_all, grad_all, own_self, own_kv, own_cross, own_ffn, small = done
-    grad_q, grad_k, grad_v, grad_out = unpack_columns(own_self, 4, width)
-    grad_cq, grad_co = unpack_columns(own_cross, 2, width)
-    own_ffn = own_ffn.reshape(4, fan, hidden)
-    stats = small[10, :5]
+    local = [
+        ((rows, ROW_LEN, model), BF16),
+        ((rows, ROW_LEN, model), F32),
+        (self_qkv.shape, F32),
+        (self_out.shape, F32),
+        (cross_q.shape, F32),
+        (cross_kv.shape, F32),
+        (cross_out.shape, F32),
+        (ffn_in.shape, F32),
+        (ffn_in.shape, F32),
+        (vectors.shape, F32),
+        (head_bias.shape, F32),
+        (ffn_bias.shape, F32),
+        ((1, 4), F32),
+    ]
+    inside = pl.BlockSpec(memory_space=pltpu.VMEM)
+    out_all, grad_all, *others, grad_down, grad_vectors, grad_heads, grad_hidden, rms = pl.pallas_call(
+        finish_kernel,
+        out_shape=[jax.ShapeDtypeStruct(*item) for item in local],
+        in_specs=[inside] * len(done),
+        out_specs=[inside] * len(local),
+        compiler_params=pltpu.CompilerParams(vmem_limit_bytes=VMEM_LIMIT),
+    )(*done)
     return (
         out_all.reshape(tokens, model),
-        grad_all.reshape(tokens, model).astype(F32),
-        jnp.stack([grad_q, grad_k, grad_v]),
-        grad_out.T,
-        grad_cq,
-        jnp.stack(unpack_columns(own_kv, 2, width)),
-        grad_co.T,
-        own_ffn[:2],
-        own_ffn[2:].transpose(0, 2, 1),
-        lax.dynamic_slice_in_dim(
-            small[:10], lax.axis_index("dp") * vectors.shape[1], vectors.shape[1], axis=1
-        ),
-        small[16:20, :width],
-        small[20:22, :hidden],
-        jnp.sqrt(stats[:4] / (stats[4] * model)),
+        grad_all.reshape(tokens, model),
+        *others,
+        grad_down.transpose(0, 2, 1),
+        grad_vectors,
+        grad_heads,
+        grad_hidden,
+        rms.reshape(4),
     )
 
 

time: 264 us -> 211 us (0.80)
  the two profiles are of different devices: /device:TPU:24 before, /device:TPU:0 now
where the time goes in v3:
time: 211 us
  Pallas kernels  210 us (100%)
    pallas_call x1, Pallas kernels, layer(): pl.pallas_call(functools.partial(layer_kernel, names, z), out_shape=[jax....  204 us
    pallas_call x1, Pallas kernels, layer(): pl.pallas_call(finish_kernel, out_shape=[jax.ShapeDtypeStruct(*item) for...  5.7 us

profile of v3, /device:TPU:0, one launch (start us, length us, event | category | flops | bytes accessed | tf_op | source)
XLA Modules:
  0.0 210.7 jit_solution(3898100573841239528)
XLA Ops:
  0.7 204.3 %shard_map.255 = (bf16[4,256,768]{2,1,0:T(8,128)(2,1)}, bf16[4,256,768]{2,1,0:T(8,128)(2,1)}, f32[96,768]{1,0:T(8,128)}, f32[176,384]{1,0:T(8,128)}, f32[96,384]...) custom-call(s32[16]{0:T(128)} %bitcast.15, bf16[10,96]{1,0:T(8,128)(2,1)} %refs_1_.1, bf16[3,96,192]{2,1,0:T(8,128)(2,1)} %refs_2_.1, ...), custom_call_target="tpu_custom_call" | custom-call | tf_op jit(solution)/shard_map/pallas_call | solution.py:1277
  204.9 5.7 %shard_map.256 = (bf16[4,256,768]{2,1,0:T(8,128)(2,1)}, f32[4,256,768]{2,1,0:T(8,128)}, f32[3,96,192]{2,1,0:T(8,128)}, f32[192,96]{1,0:T(8,128)}, f32[96,192]{1,...) custom-call(bf16[4,256,768]{2,1,0:T(8,128)(2,1)} %get-tuple-element., ...), custom_call_target="tpu_custom_call" | custom-call | tf_op jit(solution)/shard_map/pallas_call | solution.py:1306

commit v4 on v3

--- a/solution.py
+++ b/solution.py
@@ -19,17 +19,17 @@
 EPSILON = 1e-06
 MASKED = -1e30
 MESH = pl.DeviceIdType.MESH
-VMEM_LIMIT = 62 * 2**20
+VMEM_LIMIT = 63 * 2**20
 BF16 = jnp.bfloat16
 F32 = jnp.float32
 PIECES = ("vec", "self", "kv", "cross")
 TERMS = ("cross", "kv", "self")
 SUMS = ("selfq", "selft", "cross", "gft", "gfq", "out", "gc", "gaq", "gat")
 SHARES = ("c", "ft", "fq", "gca", "gsat", "gsaq", "out", "sgq", "sgt")
-RINGED = ("in1", "out1", "in0", "out0")
+RINGED = ("in0", "out0", "in1", "out1")
 WIDE = 256
 CHUNK = 256
-CHUNKS_HELD = 3
+CHUNKS_HELD = 4
 PADDED_KEYS = 272
 
 
@@ -246,7 +246,15 @@
                 if hop < count - 1:
                     ring_gather(name, way, hop).start()
 
-    first_pair, last_pair = RINGED[:2], RINGED[2:]
+    query_pair, text_pair = RINGED[:2], RINGED[2:]
+
+    def ring_passes(*steps):
+        for *names, hop in steps:
+            ring_pass(names, hop)
+
+    def scatter_passes(*steps):
+        for *names, hop in steps:
+            scatter_pass(names, hop)
 
     def ring_gather_sent(name):
         for way in range(2):
@@ -271,10 +279,10 @@
                     ring_scatter(name, way, hop - 1).wait_recv()
                     landed = getattr(s, "r_" + name)[hop - 1, first : first + high, :]
                     mine = ring_block(name, spot - 1 - hop if way == 0 else spot + 1 + hop, way)
-                    total = mine[...].astype(F32) + landed.astype(F32)
                     if hop < count - 1:
-                        mine[...] = total.astype(BF16)
+                        mine[...] = mine[...] + landed
                     else:
+                        total = mine[...].astype(F32) + landed.astype(F32)
                         owned[name][first : first + high, :] = total
                 if hop < count - 1:
                     ring_scatter(name, way, hop).start()
@@ -326,7 +334,7 @@
             other = other_line(step)
             mine = block(whole[name], other * 2 + side, size[name])
             scatter_side(name, step).wait_recv()
-            mine[...] = (mine[...].astype(F32) + side_in[name][step].astype(F32)).astype(BF16)
+            mine[...] = mine[...] + side_in[name][step]
             scatter_line(name, step).start()
 
     def scatter_finish(name):
@@ -369,7 +377,7 @@
     def sum_forward(name):
         sum_copy(name, 0).wait_recv()
         pair_in, half, _ = sum_buffers(name)
-        half[...] = (part(name, far)[...].astype(F32) + pair_in[1].astype(F32)).astype(BF16)
+        half[...] = part(name, far)[...] + pair_in[1]
         sum_copy(name, 2).start()
 
     def sum_finish(name):
@@ -387,14 +395,13 @@
         "c": s.c,
         "ft": s.f_t,
         "fq": s.f_q,
-        "gca": s.part_t,
         "gsat": s.gsa_t,
         "gsaq": s.f_q,
         "out": s.gy,
     }
 
     def shared_part(name, index):
-        if name == "sgq":
+        if name in ("gca", "sgq"):
             return s.x.at[index, pl.ds(0, query)]
         if name == "sgt":
             return s.x.at[index, pl.ds(query, text)]
@@ -522,6 +529,7 @@
         normed, _ = norm_parts(s.x[row].astype(F32))
         s.a[row_at(row), :] = (normed * vec(0) + vec(1)).astype(BF16)
 
+    ring_pass(query_pair, 0)
     s.x_own[...] = s.x[rank]
     weight_query, weight_text = jnp.ones((query, 1), F32), s.weight[...]
     weight_own = jnp.concatenate([weight_query, weight_text], axis=0)
@@ -579,22 +587,19 @@
         send_pairs(step, ("selfq", "selft"))
 
     pl.loop(0, rows // 2)(self_row)
-    gather_forward("kv")
-    ring_pass(first_pair, 0)
-    ring_pass(last_pair, 0)
-    pl.loop(rows // 2, rows)(self_row)
     sum_forward("selfq")
     sum_forward("selft")
-    ring_pass(first_pair, 1)
+    ring_pass(text_pair, 0)
+    gather_forward("kv")
+    pl.loop(rows // 2, rows)(self_row)
     gather_forward("cross")
-    ring_pass(last_pair, 1)
     gather_finish("kv")
     widen(s.m_kv, s.w_kv, 2)
 
     def project(values):
         return dot(values, s.w_kv[...]) + s.bias[2:3, : 2 * WIDE]
 
-    def project_chunk(index):
+    def project_chunk(index, first):
         load_chunk(index).wait()
         result = project(s.chunk[lax.rem(index, CHUNKS_HELD)])
 
@@ -603,7 +608,8 @@
             load_chunk(index + CHUNKS_HELD).start()
 
         for tile in range(2 * WIDE // 128):
-            s.stage[tile // 2, (tile % 2) * CHUNK : (tile % 2 + 1) * CHUNK, :] = result[
+            at = first + tile % 2 * CHUNK
+            s.stage[tile // 2, at : at + CHUNK, :] = result[
                 :, tile * 128 : (tile + 1) * 128
             ]
         keys = CHUNK // z.images
@@ -611,11 +617,15 @@
         for image in range(z.images):
             for tile in range(2 * WIDE // 128):
                 s.kv[image, key_at, tile * 128 : (tile + 1) * 128] = s.stage.at[tile // 2][
-                    pl.ds((tile % 2) * CHUNK + image, keys, stride=z.images), :
+                    pl.ds(first + tile % 2 * CHUNK + image, keys, stride=z.images), :
                 ].astype(BF16)
 
-    third = chunk_count // 3
-    pl.loop(0, third)(project_chunk)
+    def project_pair(pair):
+        for inner in range(2):
+            project_chunk(pair * 2 + inner, inner * 2 * CHUNK)
+
+    quarter = chunk_count // 8
+    pl.loop(0, quarter)(project_pair)
 
     after = s.x_own[:query, :].astype(F32) + sum_finish("selfq") + vec(6)
     s.after_self[:query, :] = after
@@ -623,6 +633,9 @@
     s.c[rank] = (normed * vec(2) + vec(3)).astype(BF16)
     share_start("c")
     put_stat(1, after, weight_query)
+    ring_pass(query_pair, 1)
+    pl.loop(quarter, 2 * quarter)(project_pair)
+    ring_pass(text_pair, 1)
     after = s.x_own[query:, :].astype(F32) + sum_finish("selft") + vec(6)
     s.after_self[query:, :] = after
     normed, _ = norm_parts(after)
@@ -630,10 +643,11 @@
     share_start("ft")
     put_stat(1, after, weight_text)
     put_stat(2, after, weight_text)
-    ring_pass(first_pair, 2)
-    pl.loop(third, 2 * third)(project_chunk)
-    ring_pass(last_pair, 2)
-    pl.loop(2 * third, chunk_count)(project_chunk)
+    ring_passes(("in0", 2))
+    pl.loop(2 * quarter, 3 * quarter)(project_pair)
+    share_forward("c")
+    ring_passes(("out0", 2), ("in1", 2))
+    pl.loop(3 * quarter, chunk_count // 2)(project_pair)
     load_tail.wait()
     last = project(s.tail[...])
     first_row = lax.broadcasted_iota(jnp.int32, (tail, 1), 0) == 0
@@ -642,8 +656,7 @@
             first_row, jnp.broadcast_to(last[image : image + 1, :], last.shape), 0.0
         ).astype(BF16)
     load_chunks()
-    share_forward("c")
-    ring_pass(first_pair, 3)
+    ring_passes(("out1", 2), ("in0", 3))
     gather_finish("cross")
     widen(s.m_cross, s.w_cross, 2)
     share_finish("c")
@@ -661,57 +674,48 @@
             slot = jnp.where(s.image_of[other] == image, other, slot)
         return slot
 
-    def cross_queries(image):
-        values = s.qc[slot_of(image)]
-        return spread(values * jnp.asarray(z.scale, BF16), heads)
-
     unroll = 4
     groups = z.images // unroll
 
-    def cross_group(group):
-        for inner in range(unroll):
-            image = group * unroll + inner
-            scores = dot_columns(cross_queries(image), s.kv[image, :, :WIDE])
+    def cross_row(step):
+        row = send_order(step)
+        for inner in range(SLOTS):
+            slot = row * SLOTS + inner
+            image = s.image_of[slot]
+            queries = spread(s.qc[slot] * jnp.asarray(z.scale, BF16), heads)
+            scores = dot_columns(queries, s.kv[image, :, :WIDE])
             probs = softmax(jnp.where(is_key, scores, MASKED)).astype(BF16)
-            s.p_cross[image] = probs
+            s.p_cross[slot] = probs
             mixed = fold(dot(probs, s.kv[image, :, WIDE:]), heads, QUERIES)
-            s.oc_image[image] = mixed.astype(BF16)
-
-    pl.loop(0, groups // 2)(cross_group)
-    ring_pass(last_pair, 3)
-    pl.loop(groups // 2, groups)(cross_group)
-
-    @pl.loop(0, z.images)
-    def _(slot):
-        s.oc[slot] = s.oc_image[s.image_of[slot]]
-
-    share_forward("ft")
-    ring_pass(first_pair, 4)
+            s.oc[slot] = mixed.astype(BF16)
+        mixed = s.oc[pl.ds(row * SLOTS, SLOTS)].reshape(query, WIDE)
+        s.part_q[row] = dot_columns(mixed, s.w_cross[:, WIDE:]).astype(BF16)
+        send_pairs(step, ("cross",))
+
+    pl.loop(0, rows // 2)(cross_row)
+    ring_passes(("out0", 3), ("in1", 3))
     sum_sent("selfq")
     sum_sent("selft")
-    s.part_q[...] = (
-        dot_columns(all_slots(s.oc), s.w_cross[:, WIDE:]).astype(BF16).reshape(s.part_q.shape)
-    )
-    sum_copy("cross", 0).start()
-    sum_copy("cross", 1).start()
     sum_forward("cross")
-    ring_pass(last_pair, 4)
-    ring_pass(first_pair, 5)
-    ring_pass(last_pair, 5)
+    share_forward("ft")
+    ring_passes(("out1", 3))
+    pl.loop(rows // 2, rows)(cross_row)
+    ring_passes(("in0", "out0", 4), ("in1", 4))
+    ring_passes(("out1", 4), ("in0", "out0", 5), ("in1", "out1", 5))
     after_query = s.after_self[:query, :] + sum_finish("cross") + vec(7)
     s.after_query[...] = after_query
     normed, _ = norm_parts(after_query)
     s.f_q[rank] = (normed * vec(4) + vec(5)).astype(BF16)
     share_start("fq")
     put_stat(2, after_query, weight_query)
-    ring_pass(first_pair, 6)
-    ring_pass(last_pair, 6)
-    ring_pass(first_pair, 7)
+    ring_passes(("in0", "out0", 6), ("in1", "out1", 6), ("in0", 7))
     share_forward("fq")
-    share_finish("ft")
+    ring_passes(("out0", 7))
     load_gy.wait()
     gather_sent("self")
     gather_sent("kv")
+    sum_sent("cross")
+    share_finish("fq")
 
     f_of = {0: s.f_q, 1: s.f_t}
     w_in = {0: s.m_in0, 1: s.m_in1}
@@ -733,8 +737,9 @@
             grad_up = (dot(grads, w_out[kind][...]) * slope).astype(BF16)
             at = pl.ds(pl.multiple_of(pair * 2 * query, 2 * query), 2 * query)
             if kind == 0:
-                s.hid[at, :] = hidden
-                s.gu[at, :] = grad_up
+                slots = pl.ds(pair * 2 * SLOTS, 2 * SLOTS)
+                s.hid[slots] = hidden.reshape(2 * SLOTS, QUERIES, z.hidden)
+                s.gu[slots] = grad_up.reshape(2 * SLOTS, QUERIES, z.hidden)
             else:
                 s.m_self[at, :] = hidden
                 cut = s.m_kv.shape[1]
@@ -744,6 +749,8 @@
             back = dot_columns(grad_up, w_in[kind][...]).astype(BF16)
             target[pl.ds(pair * 2, 2)] = back.reshape(2, query, z.model)
             send(pair)
+            if kind == 0 and pair is not chip:
+                sum_forward("gfq")
             s.small[20 + kind : 21 + kind, :] += column_total(grad_up)
             out = dot_columns(hidden, w_out[kind][...]).astype(BF16)
             out = out.reshape(2, query, z.model)
@@ -753,7 +760,9 @@
         values = f_of[kind][...].reshape(queries_total, z.model)
         grads = jnp.concatenate([grad_rows(kind, row) for row in range(rows)], axis=0)
         if kind == 0:
-            hidden, grad_up = s.hid[...], s.gu[...]
+            hidden, grad_up = (
+                ref[...].reshape(queries_total, z.hidden) for ref in (s.hid, s.gu)
+            )
         else:
             hidden = s.m_self[:queries_total, :]
             grad_up = jnp.concatenate(
@@ -774,17 +783,20 @@
                 )
 
     hops = iter((0, 1))
+    feed_forward(0, s.part_q, lambda pair: sum_copy("gfq", next(hops)).start())
+    ring_pass(text_pair, 7)
+    share_finish("ft")
+    hops = iter((0, 1))
     feed_forward(1, s.part_t, lambda pair: sum_copy("gft", next(hops)).start())
-    ring_pass(last_pair, 7)
-    sum_sent("cross")
-    share_finish("fq")
+    weight_terms(0)
+    share_sent("fq")
     sum_forward("gft")
-    sum_sent("gft", (0, 1))
-    hops = iter((0, 1))
-    feed_forward(0, s.part_q, lambda pair: sum_copy("gfq", next(hops)).start())
-    sum_forward("gfq")
+    scatter_pass(query_pair, 0)
     weight_terms(1)
-    scatter_pass(first_pair, 0)
+    scatter_pass(text_pair, 0)
+    sum_copy("out", 0).start()
+    sum_copy("out", 1).start()
+    scatter_passes(("in0", 1))
 
     def own_back(total, after, grads, slot):
         normed, scale = norm_parts(after)
@@ -793,35 +805,26 @@
         s.small[slot : slot + 1, :] += column_total(grads)
         return grads.astype(F32) + norm_grad(normed, scale, vec(4), total)
 
+    grad_query = own_back(sum_finish("gfq"), s.after_query[...], grad_rows(0, rank), 8)
+    s.g_own[:query, :] = grad_query
+    grad_query_low = grad_query.astype(BF16)
+    s.x[rank, :query, :] = grad_query_low
+    s.small[7:8, :] += column_total(grad_query_low)
+    share_start("gca")
+    sum_forward("out")
+    scatter_passes(("out0", 1), ("in1", "out1", 1))
     grad_text = own_back(sum_finish("gft"), s.after_self[query:, :], grad_rows(1, rank), 9)
     s.g_own[query:, :] = grad_text
     grad_text_low = grad_text.astype(BF16)
     s.gsa_t[rank] = grad_text_low
     s.small[6:7, :] += column_total(grad_text_low)
     share_start("gsat")
-    weight_terms(0)
-    share_sent("fq")
-    grad_query = own_back(sum_finish("gfq"), s.after_query[...], grad_rows(0, rank), 8)
-    s.g_own[:query, :] = grad_query
-    grad_query_low = grad_query.astype(BF16)
-    s.part_t[rank] = grad_query_low
-    s.small[7:8, :] += column_total(grad_query_low)
-    share_start("gca")
-    scatter_pass(("in1",), 1)
-    scatter_pass(last_pair, 0)
-    scatter_pass(("out1",), 1)
-    sum_copy("out", 0).start()
-    sum_copy("out", 1).start()
-    share_forward("gsat")
-    sum_forward("out")
-    scatter_pass(("in1",), 2)
-    scatter_pass(("in0",), 1)
+    scatter_passes(("in0", "out0", 2))
     share_forward("gca")
-    scatter_pass(("out0",), 1)
-    share_finish("gsat")
+    scatter_passes(("in1", 2))
     share_finish("gca")
 
-    grad_mixed = dot(s.part_t[...].reshape(queries_total, z.model), s.w_cross[:, WIDE:])
+    grad_mixed = dot(s.x[:, :query, :].reshape(queries_total, z.model), s.w_cross[:, WIDE:])
     s.goc[...] = grad_mixed.astype(BF16).reshape(s.goc.shape)
 
     def stage_put(image, values):
@@ -830,46 +833,45 @@
                 :, tile * 128 : (tile + 1) * 128
             ]
 
-    def cross_back(group):
-        for inner in range(unroll):
-            image = group * unroll + inner
-            grads = spread(s.goc[slot_of(image)], heads)
-            probs = s.p_cross[image]
-            wide = probs.astype(F32)
+    score_places = [(s.hid, 0), (s.hid, z.hidden // 2), (s.gu, 0), (s.gu, z.hidden // 2)][:heads]
+
+    def cross_back(step):
+        row = send_order(step)
+        for inner in range(SLOTS):
+            slot = row * SLOTS + inner
+            image = s.image_of[slot]
+            grads = spread(s.goc[slot], heads)
+            wide = s.p_cross[slot].astype(F32)
             grad_probs = dot_columns(grads, s.kv[image, :, WIDE:])
             delta = jnp.sum(wide * grad_probs, axis=-1, keepdims=True)
             grad_scores = (wide * (grad_probs - delta)).astype(BF16)
+            for head, (ref, at) in enumerate(score_places):
+                ref[slot, :, at : at + PADDED_KEYS] = grad_scores[
+                    head * QUERIES : (head + 1) * QUERIES, :
+                ]
             mixed = fold(dot(grad_scores, s.kv[image, :, :WIDE]), heads, QUERIES) * z.scale
-            s.kv[image, : heads * QUERIES, :PADDED_KEYS] = grad_scores
-            s.oc_image[image] = mixed.astype(BF16)
-
-    pl.loop(0, groups)(cross_back)
-
-    @pl.loop(0, z.images)
-    def _(slot):
-        s.gqc[slot] = s.oc_image[s.image_of[slot]]
+            s.gqc[slot] = mixed.astype(BF16)
+        mixed = s.gqc[pl.ds(row * SLOTS, SLOTS)].reshape(query, WIDE)
+        s.part_q[row] = dot_columns(mixed, s.w_cross[:, :WIDE]).astype(BF16)
+        send_pairs(step, ("gc",))
 
     sum_sent("gfq")
-    sum_sent("gft", (2,))
-    s.part_q[...] = (
-        dot_columns(all_slots(s.gqc), s.w_cross[:, :WIDE]).astype(BF16).reshape(s.part_q.shape)
-    )
-    sum_copy("gc", 0).start()
-    sum_copy("gc", 1).start()
-    scatter_pass(("out1",), 2)
-    scatter_pass(("in1",), 3)
-    scatter_pass(last_pair, 2)
+    pl.loop(0, rows // 2)(cross_back)
+    sum_sent("gft")
+    sum_forward("gc")
+    scatter_passes(("out1", 2), ("in0", 3))
+    pl.loop(rows // 2, rows)(cross_back)
+    scatter_passes(("out0", 3), ("in1", "out1", 3))
     s.small[18:19, :WIDE] += column_total(all_slots(s.gqc))
     low_half = lanes(128) < HEAD
     gather_sent("cross")
     grad_cq = dot_rows(s.c[...].reshape(queries_total, z.model), all_slots(s.gqc))
-    grad_co = dot_rows(s.part_t[...].reshape(queries_total, z.model), all_slots(s.oc))
+    grad_co = dot_rows(s.x[:, :query, :].reshape(queries_total, z.model), all_slots(s.oc))
     s.m_cross[:, :128] = grad_cq[:, :128].astype(BF16)
     s.m_cross[:, 128:256] = grad_co[:, :128].astype(BF16)
     s.m_cross[:, 256:] = jnp.where(
         low_half, grad_cq[:, 128:], pltpu.roll(grad_co[:, 128:], HEAD, 1)
     ).astype(BF16)
-    sum_forward("gc")
     scatter_start("cross")
 
     after_ffn_sum = sum_finish("out")
@@ -882,11 +884,16 @@
     share_start("out")
 
     def key_grad(image):
-        grad_scores = s.kv[image, : heads * QUERIES, :PADDED_KEYS]
-        return dot_rows(grad_scores, cross_queries(image))
+        slot = slot_of(image)
+        queries = spread(s.qc[slot] * jnp.asarray(z.scale, BF16), heads)
+        grad_scores = jnp.concatenate(
+            [ref[slot, :, at : at + PADDED_KEYS] for ref, at in score_places], axis=0
+        )
+        return dot_rows(grad_scores, queries)
 
     def value_grad(image):
-        return dot_rows(s.p_cross[image], spread(s.goc[slot_of(image)], heads))
+        slot = slot_of(image)
+        return dot_rows(s.p_cross[slot], spread(s.goc[slot], heads))
 
     def grads_at(at):
         return jnp.concatenate(
@@ -904,26 +911,35 @@
         s.turned[...] = dot_rows(grads, s.tail[...])
         s.col_sum[...] = column_total(grads)
 
-    def features_chunk(index):
-        load_chunk(index).wait()
-        grads = grads_at(pl.ds(pl.multiple_of(index * CHUNK, CHUNK), CHUNK))
-        s.turned[...] += dot_rows(grads, s.chunk[lax.rem(index, CHUNKS_HELD)])
-        s.col_sum[...] += column_total(grads)
-
-        @pl.when(index + CHUNKS_HELD < chunk_count)
+    def features_pair(pair):
+        total, sums = s.turned[...], s.col_sum[...]
+        for inner in range(2):
+            index = pair * 2 + inner
+            load_chunk(index).wait()
+            grads = grads_at(pl.ds(pl.multiple_of(index * CHUNK, CHUNK), CHUNK))
+            total = total + dot_rows(grads, s.chunk[lax.rem(index, CHUNKS_HELD)])
+            sums = sums + column_total(grads)
+        s.turned[...] = total
+        s.col_sum[...] = sums
+
+        @pl.when(pair * 2 + CHUNKS_HELD < chunk_count)
         def _():
-            load_chunk(index + CHUNKS_HELD).start()
-
+            for inner in range(2):
+                load_chunk(pair * 2 + inner + CHUNKS_HELD).start()
+
+    scatter_passes(("in0", 4))
     features_start(key_grad)
-    scatter_pass(("out1",), 3)
-    scatter_pass(("in1",), 4)
-    scatter_pass(("in0",), 3)
-    pl.loop(0, chunk_count)(features_chunk)
+    share_forward("gsat")
+    scatter_passes(("out0", 4), ("in1", "out1", 4))
+    pl.loop(0, chunk_count // 2)(features_pair)
     load_chunks()
     turned = s.turned[...].T
     s.m_kv[:, :128] = turned[:, :128].astype(BF16)
     s.m_kv[:, 256:] = turned[:, 128:].astype(BF16)
 
+    scatter_passes(("in0", 5))
+    scatter_forward("cross")
+    features_start(value_grad)
     cross_sum = sum_finish("gc")
     normed, scale = norm_parts(s.after_self[:query, :])
     s.small[2:3, :] += column_total(cross_sum * normed)
@@ -934,22 +950,22 @@
     s.f_q[rank] = grad_query_low
     s.small[6:7, :] += column_total(grad_query_low)
     share_start("gsaq")
-    scatter_pass(("out0",), 3)
-    scatter_forward("cross")
-    features_start(value_grad)
-    scatter_pass(("out1",), 4)
-    scatter_pass(("in1",), 5)
-    pl.loop(0, chunk_count)(features_chunk)
+    scatter_passes(("out0", "in1", "out1", 5))
+    share_forward("out")
+    scatter_passes(("in0", 6))
+    pl.loop(0, chunk_count // 2)(features_pair)
     s.small[19:20, :WIDE] += s.col_sum[...]
     turned = s.turned[...].T
     s.m_kv[:, 128:256] = turned[:, :128].astype(BF16)
     s.m_kv[:, 256:] = jnp.where(
         low_half, s.m_kv[:, 256:].astype(F32), pltpu.roll(turned[:, 128:], HEAD, 1)
     ).astype(BF16)
+    scatter_passes(("out0", 6))
+    scatter_start("kv")
+    scatter_passes(("in1", 6))
     share_forward("gsaq")
-    scatter_pass(last_pair, 4)
-    scatter_start("kv")
-    share_forward("out")
+    scatter_passes(("out1", 6))
+    share_finish("gsat")
     share_finish("gsaq")
 
     def self_back(step):
@@ -975,15 +991,14 @@
         s.part_row[row] = dot_columns(grad_low, s.w_self[:, : 3 * WIDE]).astype(BF16)
         send_pairs(step, ("gaq", "gat"))
 
-    scatter_pass(("out1",), 5)
     sum_sent("out")
     sum_sent("gc")
+    share_sent("gca")
     pl.loop(0, rows // 2)(self_back)
-    scatter_pass(("in1",), 6)
-    scatter_pass(last_pair, 5)
-    pl.loop(rows // 2, rows)(self_back)
     sum_forward("gaq")
     sum_forward("gat")
+    scatter_passes(("in0", "out0", 7))
+    pl.loop(rows // 2, rows)(self_back)
 
     grads_all = [dot_rows(s.a[...], s.qkv[:, i * WIDE : (i + 1) * WIDE]) for i in range(3)]
     grad_stream = jnp.concatenate(
@@ -997,10 +1012,9 @@
             low_half, grads_all[2 * i][:, 128:], pltpu.roll(grads_all[2 * i + 1][:, 128:], HEAD, 1)
         ).astype(BF16)
     scatter_start("self")
-    scatter_pass(("out1",), 6)
+    scatter_passes(("in1", 7))
     scatter_forward("kv")
-    scatter_pass(("in1",), 7)
-    scatter_pass(last_pair, 6)
+    scatter_passes(("out1", 7))
 
     def stream_back(name, at):
         total = sum_finish(name)
@@ -1015,7 +1029,6 @@
     stream_back("gat", pl.ds(query, text))
     share_start("sgt")
     scatter_forward("self")
-    scatter_pass(("out1",), 7)
 
     def small_copy(source, hop, device):
         target = s.small_in.at[hop] if source is s.small else s.small_in.at[hop, pl.ds(0, 16)]
@@ -1048,7 +1061,6 @@
         items[step - 1].wait_recv()
         total = total + s.small_in[2 + step]
     s.small_out[...] = total
-    scatter_pass(last_pair, 7)
     for name in TERMS:
         scatter_finish(name)
     for name in RINGED:
@@ -1059,7 +1071,7 @@
     for name in ("gaq", "gat"):
         sum_sent(name)
     for name in SHARES:
-        if name != "fq":
+        if name not in ("fq", "gca"):
             share_sent(name)
     store_out.wait()
     store_sg.wait()
@@ -1224,7 +1236,6 @@
         "gqc": ((images, QUERIES, WIDE), BF16),
         "goc": ((images, QUERIES, WIDE), BF16),
         "oc": ((images, QUERIES, WIDE), BF16),
-        "oc_image": ((images, QUERIES, WIDE), BF16),
         "kv": ((images, PADDED_KEYS, 2 * WIDE), BF16),
         "p_cross": ((images, z.heads * QUERIES, PADDED_KEYS), BF16),
         "stage": ((WIDE // 128, PADDED_KEYS * images, 128), F32),
@@ -1232,8 +1243,8 @@
         "col_sum": ((1, WIDE), F32),
         "chunk": ((CHUNKS_HELD, CHUNK, feat), BF16),
         "tail": ((images * keys % CHUNK, feat), BF16),
-        "hid": ((rows * query, hidden), BF16),
-        "gu": ((rows * query, hidden), BF16),
+        "hid": ((images, QUERIES, hidden), BF16),
+        "gu": ((images, QUERIES, hidden), BF16),
         "part_row": ((rows, ROW_LEN, model), BF16),
         "part_q": ((rows, query, model), BF16),
         "part_t": ((rows, query, model), BF16),

time: 211 us -> 205 us (0.972)
  Pallas kernels: 210 us -> 203 us
    pallas_call x1, Pallas kernels: 204 us -> 198 us  [layer(): pl.pallas_call(functools.partial(layer_kernel, names, z), out_shape=[jax....]
where the time goes in v4:
time: 205 us; the launch traced here: 204 us
  Pallas kernels  203 us (99%)
    pallas_call x1, Pallas kernels, layer(): pl.pallas_call(functools.partial(layer_kernel, names, z), out_shape=[jax....  198 us
    pallas_call x1, Pallas kernels, layer(): pl.pallas_call(finish_kernel, out_shape=[jax.ShapeDtypeStruct(*item) for...  5.7 us

profile of v4, /device:TPU:0, one launch (start us, length us, event | category | flops | bytes accessed | tf_op | source)
XLA Modules:
  0.0 204.2 jit_solution(2955684064155526768)
XLA Ops:
  0.7 197.7 %shard_map.255 = (bf16[4,256,768]{2,1,0:T(8,128)(2,1)}, bf16[4,256,768]{2,1,0:T(8,128)(2,1)}, f32[96,768]{1,0:T(8,128)}, f32[176,384]{1,0:T(8,128)}, f32[96,384]...) custom-call(s32[16]{0:T(128)} %bitcast.15, bf16[10,96]{1,0:T(8,128)(2,1)} %refs_1_.1, bf16[3,96,192]{2,1,0:T(8,128)(2,1)} %refs_2_.1, ...), custom_call_target="tpu_custom_call" | custom-call | tf_op jit(solution)/shard_map/pallas_call | solution.py:1288
  198.4 5.7 %shard_map.256 = (bf16[4,256,768]{2,1,0:T(8,128)(2,1)}, f32[4,256,768]{2,1,0:T(8,128)}, f32[3,96,192]{2,1,0:T(8,128)}, f32[192,96]{1,0:T(8,128)}, f32[96,192]{1,...) custom-call(bf16[4,256,768]{2,1,0:T(8,128)(2,1)} %get-tuple-element., ...), custom_call_target="tpu_custom_call" | custom-call | tf_op jit(solution)/shard_map/pallas_call | solution.py:1317

commit v5 on v4

--- a/solution.py
+++ b/solution.py
@@ -16,17 +16,48 @@
 ROW_LEN = 256
 
 
+N_C = "c"
+N_CROSS = "cross"
+N_DP = "dp"
+N_FIN = "fin_"
+N_FQ = "fq"
+N_FT = "ft"
+N_GAQ = "gaq"
+N_GAT = "gat"
+N_GC = "gc"
+N_GCA = "gca"
+N_GFQ = "gfq"
+N_GFT = "gft"
+N_GSAQ = "gsaq"
+N_GSAT = "gsat"
+N_IN0 = "in0"
+N_IN1 = "in1"
+N_KV = "kv"
+N_MP = "mp"
+N_OUT = "out"
+N_OUT0 = "out0"
+N_OUT1 = "out1"
+N_PIN = "pin_"
+N_R = "r_"
+N_SELF = "self"
+N_SELFQ = "selfq"
+N_SELFT = "selft"
+N_SGQ = "sgq"
+N_SGT = "sgt"
+N_VEC = "vec"
+N_Y = "y_"
+N_Z = "z_"
 EPSILON = 1e-06
 MASKED = -1e30
 MESH = pl.DeviceIdType.MESH
 VMEM_LIMIT = 63 * 2**20
 BF16 = jnp.bfloat16
 F32 = jnp.float32
-PIECES = ("vec", "self", "kv", "cross")
-TERMS = ("cross", "kv", "self")
-SUMS = ("selfq", "selft", "cross", "gft", "gfq", "out", "gc", "gaq", "gat")
-SHARES = ("c", "ft", "fq", "gca", "gsat", "gsaq", "out", "sgq", "sgt")
-RINGED = ("in0", "out0", "in1", "out1")
+PIECES = (N_VEC, N_SELF, N_KV, N_CROSS)
+TERMS = (N_CROSS, N_KV, N_SELF)
+SUMS = (N_SELFQ, N_SELFT, N_CROSS, N_GFT, N_GFQ, N_OUT, N_GC, N_GAQ, N_GAT)
+SHARES = (N_C, N_FT, N_FQ, N_GCA, N_GSAT, N_GSAQ, N_OUT, N_SGQ, N_SGT)
+RINGED = (N_IN0, N_OUT0, N_IN1, N_OUT1)
 WIDE = 256
 CHUNK = 256
 CHUNKS_HELD = 4
@@ -111,7 +142,7 @@
         z.heads,
     )
     text = length - query
-    place, rank = lax.axis_index("dp"), lax.axis_index("mp")
+    place, rank = lax.axis_index(N_DP), lax.axis_index(N_MP)
     line, side = place // 2, lax.rem(place, 2)
     chip, core = rank // 2, lax.rem(rank, 2)
     beside = chip * 2 + 1 - core
@@ -145,17 +176,17 @@
         return ref.at[pl.ds(pl.multiple_of(index * size, 16), size)]
 
     fan, feat_fan = z.fan, z.feat_fan
-    whole = {
-        "vec": s.w_vec,
-        "self": s.m_self,
-        "kv": s.m_kv,
-        "cross": s.m_cross,
-        "in0": s.m_in0,
-        "in1": s.m_in1,
-        "out0": s.m_out0,
-        "out1": s.m_out1,
-    }
-    size = {name: fan for name in PIECES + RINGED} | {"vec": 16, "kv": feat_fan}
+    whole = dict(
+        vec=s.w_vec,
+        self=s.m_self,
+        kv=s.m_kv,
+        cross=s.m_cross,
+        in0=s.m_in0,
+        in1=s.m_in1,
+        out0=s.m_out0,
+        out1=s.m_out1,
+    )
+    size = {name: fan for name in PIECES + RINGED} | {N_VEC: 16, N_KV: feat_fan}
     shard = {name: block(whole[name], place, size[name]) for name in PIECES + RINGED}
     own_in = [
         pltpu.make_async_copy(s.ffn_in.at[kind], shard["in%d" % kind], s.own_sem.at[kind])
@@ -265,7 +296,7 @@
         first, high = ring_part(name, way)
         return remote(
             ring_block(name, spot - 1 - hop if way == 0 else spot + 1 + hop, way),
-            getattr(s, "r_" + name).at[hop, pl.ds(first, high)],
+            getattr(s, N_R + name).at[hop, pl.ds(first, high)],
             (s.rs_send, s.rs_recv),
             (RINGED.index(name), way, hop),
             ring_to[way],
@@ -277,7 +308,7 @@
                 first, high = ring_part(name, way)
                 if hop > 0:
                     ring_scatter(name, way, hop - 1).wait_recv()
-                    landed = getattr(s, "r_" + name)[hop - 1, first : first + high, :]
+                    landed = getattr(s, N_R + name)[hop - 1, first : first + high, :]
                     mine = ring_block(name, spot - 1 - hop if way == 0 else spot + 1 + hop, way)
                     if hop < count - 1:
                         mine[...] = mine[...] + landed
@@ -292,17 +323,17 @@
             for hop in range(count - 1):
                 ring_scatter(name, way, hop).wait_send()
 
-    side_in = {name: getattr(s, "y_" + name) for name in TERMS}
-    line_in = {name: getattr(s, "z_" + name) for name in TERMS}
-    owned = {
-        "self": s.own_self,
-        "kv": s.own_kv,
-        "cross": s.own_cross,
-        "in0": s.own_ffn.at[pl.ds(0, fan)],
-        "in1": s.own_ffn.at[pl.ds(fan, fan)],
-        "out0": s.own_ffn.at[pl.ds(2 * fan, fan)],
-        "out1": s.own_ffn.at[pl.ds(3 * fan, fan)],
-    }
+    side_in = {name: getattr(s, N_Y + name) for name in TERMS}
+    line_in = {name: getattr(s, N_Z + name) for name in TERMS}
+    owned = dict(
+        self=s.own_self,
+        kv=s.own_kv,
+        cross=s.own_cross,
+        in0=s.own_ffn.at[pl.ds(0, fan)],
+        in1=s.own_ffn.at[pl.ds(fan, fan)],
+        out0=s.own_ffn.at[pl.ds(2 * fan, fan)],
+        out1=s.own_ffn.at[pl.ds(3 * fan, fan)],
+    )
     order = [*range(1, lines), 0]
 
     def scatter_side(name, step):
@@ -350,19 +381,19 @@
         for step in range(lines):
             scatter_side(name, step).wait_send()
 
-    halves = {"selfq": 0, "selft": 1, "cross": 0, "gft": 1, "gfq": 0, "gc": 1, "gaq": 0, "gat": 1}
+    halves = {N_SELFQ: 0, N_SELFT: 1, N_CROSS: 0, N_GFT: 1, N_GFQ: 0, N_GC: 1, N_GAQ: 0, N_GAT: 1}
 
     def sum_buffers(name):
-        landed = {"gaq": "selfq", "gat": "selft", "gc": "cross"}.get(name, name)
-        half = s.half_row if name == "out" else s.half.at[halves[name]]
-        return getattr(s, "pin_" + landed), half, getattr(s, "fin_" + landed)
+        landed = {N_GAQ: N_SELFQ, N_GAT: N_SELFT, N_GC: N_CROSS}.get(name, name)
+        half = s.half_row if name == N_OUT else s.half.at[halves[name]]
+        return getattr(s, N_PIN + landed), half, getattr(s, N_FIN + landed)
 
     def part(name, index):
-        if name in ("selfq", "gaq"):
+        if name in (N_SELFQ, N_GAQ):
             return s.part_row.at[index, pl.ds(0, query)]
-        if name in ("selft", "gat"):
+        if name in (N_SELFT, N_GAT):
             return s.part_row.at[index, pl.ds(query, text)]
-        return {"out": s.part_row, "gft": s.part_t}.get(name, s.part_q).at[index]
+        return {N_OUT: s.part_row, N_GFT: s.part_t}.get(name, s.part_q).at[index]
 
     def sum_copy(name, hop):
         pair_in, half, far_in = sum_buffers(name)
@@ -391,19 +422,19 @@
         for hop in hops:
             sum_copy(name, hop).wait_send()
 
-    shared = {
-        "c": s.c,
-        "ft": s.f_t,
-        "fq": s.f_q,
-        "gsat": s.gsa_t,
-        "gsaq": s.f_q,
-        "out": s.gy,
-    }
+    shared = dict(
+        c=s.c,
+        ft=s.f_t,
+        fq=s.f_q,
+        gsat=s.gsa_t,
+        gsaq=s.f_q,
+        out=s.gy,
+    )
 
     def shared_part(name, index):
-        if name in ("gca", "sgq"):
+        if name in (N_GCA, N_SGQ):
             return s.x.at[index, pl.ds(0, query)]
-        if name == "sgt":
+        if name == N_SGT:
             return s.x.at[index, pl.ds(query, text)]
         return shared[name].at[index]
 
@@ -462,16 +493,16 @@
     for item in own_in:
         item.start()
     own = z.model // count
-    shard["vec"][...] = jnp.zeros((16, 128), BF16)
-    shard["vec"][: s.vectors.shape[0], :own] = s.vectors[...]
-    pack("self", [s.self_qkv[0], s.self_qkv[1], s.self_qkv[2], turn(s.self_out[...])])
+    shard[N_VEC][...] = jnp.zeros((16, 128), BF16)
+    shard[N_VEC][: s.vectors.shape[0], :own] = s.vectors[...]
+    pack(N_SELF, [s.self_qkv[0], s.self_qkv[1], s.self_qkv[2], turn(s.self_out[...])])
     pl.semaphore_wait(barrier, len(partners))
-    gather_start("vec")
-    gather_start("self")
-    pack("kv", [s.cross_kv[0], s.cross_kv[1]])
-    pack("cross", [s.cross_q[...], turn(s.cross_out[...])])
-    gather_start("kv")
-    gather_start("cross")
+    gather_start(N_VEC)
+    gather_start(N_SELF)
+    pack(N_KV, [s.cross_kv[0], s.cross_kv[1]])
+    pack(N_CROSS, [s.cross_q[...], turn(s.cross_out[...])])
+    gather_start(N_KV)
+    gather_start(N_CROSS)
     for kind in range(2):
         shard["out%d" % kind][...] = s.ffn_out[kind]
         own_in[kind].wait()
@@ -516,8 +547,8 @@
     for row in range(rows):
         s.text_codes[row] = as_column(s.segment[row : row + 1, :])
     s.weight[...] = as_column((s.valid[pl.ds(rank, 1), :] == 1).astype(jnp.int32))
-    gather_forward("vec")
-    gather_finish("vec")
+    gather_forward(N_VEC)
+    gather_finish(N_VEC)
     for index in range(count):
         s.vecs[:, index * own : (index + 1) * own] = s.w_vec[
             index * 16 : (index + 1) * 16, :own
@@ -538,8 +569,8 @@
     )
     put_stat(0, s.x_own[...].astype(F32), weight_own)
 
-    gather_forward("self")
-    gather_finish("self")
+    gather_forward(N_SELF)
+    gather_finish(N_SELF)
     widen(s.m_self, s.w_self, 4)
 
     def self_mask(row):
@@ -584,16 +615,16 @@
         mixed = fold(dot(probs, low[:, 2 * WIDE :]), heads, length).astype(BF16)
         s.o[at, :] = mixed
         s.part_row[row] = dot_columns(mixed, s.w_self[:, 3 * WIDE :]).astype(BF16)
-        send_pairs(step, ("selfq", "selft"))
+        send_pairs(step, (N_SELFQ, N_SELFT))
 
     pl.loop(0, rows // 2)(self_row)
-    sum_forward("selfq")
-    sum_forward("selft")
+    sum_forward(N_SELFQ)
+    sum_forward(N_SELFT)
     ring_pass(text_pair, 0)
-    gather_forward("kv")
+    gather_forward(N_KV)
     pl.loop(rows // 2, rows)(self_row)
-    gather_forward("cross")
-    gather_finish("kv")
+    gather_forward(N_CROSS)
+    gather_finish(N_KV)
     widen(s.m_kv, s.w_kv, 2)
 
     def project(values):
@@ -627,26 +658,26 @@
     quarter = chunk_count // 8
     pl.loop(0, quarter)(project_pair)
 
-    after = s.x_own[:query, :].astype(F32) + sum_finish("selfq") + vec(6)
+    after = s.x_own[:query, :].astype(F32) + sum_finish(N_SELFQ) + vec(6)
     s.after_self[:query, :] = after
     normed, _ = norm_parts(after)
     s.c[rank] = (normed * vec(2) + vec(3)).astype(BF16)
-    share_start("c")
+    share_start(N_C)
     put_stat(1, after, weight_query)
     ring_pass(query_pair, 1)
     pl.loop(quarter, 2 * quarter)(project_pair)
     ring_pass(text_pair, 1)
-    after = s.x_own[query:, :].astype(F32) + sum_finish("selft") + vec(6)
+    after = s.x_own[query:, :].astype(F32) + sum_finish(N_SELFT) + vec(6)
     s.after_self[query:, :] = after
     normed, _ = norm_parts(after)
     s.f_t[rank] = (normed * vec(4) + vec(5)).astype(BF16)
-    share_start("ft")
+    share_start(N_FT)
     put_stat(1, after, weight_text)
     put_stat(2, after, weight_text)
-    ring_passes(("in0", 2))
+    ring_passes((N_IN0, 2))
     pl.loop(2 * quarter, 3 * quarter)(project_pair)
-    share_forward("c")
-    ring_passes(("out0", 2), ("in1", 2))
+    share_forward(N_C)
+    ring_passes((N_OUT0, 2), (N_IN1, 2))
     pl.loop(3 * quarter, chunk_count // 2)(project_pair)
     load_tail.wait()
     last = project(s.tail[...])
@@ -656,10 +687,10 @@
             first_row, jnp.broadcast_to(last[image : image + 1, :], last.shape), 0.0
         ).astype(BF16)
     load_chunks()
-    ring_passes(("out1", 2), ("in0", 3))
-    gather_finish("cross")
+    ring_passes((N_OUT1, 2), (N_IN0, 3))
+    gather_finish(N_CROSS)
     widen(s.m_cross, s.w_cross, 2)
-    share_finish("c")
+    share_finish(N_C)
     queries_total = rows * query
     cross_query = dot(s.c[...].reshape(queries_total, z.model), s.w_cross[:, :WIDE])
     s.qc[...] = (cross_query + s.bias[1:2, :WIDE]).astype(BF16).reshape(s.qc.shape)
@@ -690,32 +721,32 @@
             s.oc[slot] = mixed.astype(BF16)
         mixed = s.oc[pl.ds(row * SLOTS, SLOTS)].reshape(query, WIDE)
         s.part_q[row] = dot_columns(mixed, s.w_cross[:, WIDE:]).astype(BF16)
-        send_pairs(step, ("cross",))
+        send_pairs(step, (N_CROSS,))
 
     pl.loop(0, rows // 2)(cross_row)
-    ring_passes(("out0", 3), ("in1", 3))
-    sum_sent("selfq")
-    sum_sent("selft")
-    sum_forward("cross")
-    share_forward("ft")
-    ring_passes(("out1", 3))
+    ring_passes((N_OUT0, 3), (N_IN1, 3))
+    sum_sent(N_SELFQ)
+    sum_sent(N_SELFT)
+    sum_forward(N_CROSS)
+    share_forward(N_FT)
+    ring_passes((N_OUT1, 3))
     pl.loop(rows // 2, rows)(cross_row)
-    ring_passes(("in0", "out0", 4), ("in1", 4))
-    ring_passes(("out1", 4), ("in0", "out0", 5), ("in1", "out1", 5))
-    after_query = s.after_self[:query, :] + sum_finish("cross") + vec(7)
+    ring_passes((N_IN0, N_OUT0, 4), (N_IN1, 4))
+    ring_passes((N_OUT1, 4), (N_IN0, N_OUT0, 5), (N_IN1, N_OUT1, 5))
+    after_query = s.after_self[:query, :] + sum_finish(N_CROSS) + vec(7)
     s.after_query[...] = after_query
     normed, _ = norm_parts(after_query)
     s.f_q[rank] = (normed * vec(4) + vec(5)).astype(BF16)
-    share_start("fq")
+    share_start(N_FQ)
     put_stat(2, after_query, weight_query)
-    ring_passes(("in0", "out0", 6), ("in1", "out1", 6), ("in0", 7))
-    share_forward("fq")
-    ring_passes(("out0", 7))
+    ring_passes((N_IN0, N_OUT0, 6), (N_IN1, N_OUT1, 6), (N_IN0, 7))
+    share_forward(N_FQ)
+    ring_passes((N_OUT0, 7))
     load_gy.wait()
-    gather_sent("self")
-    gather_sent("kv")
-    sum_sent("cross")
-    share_finish("fq")
+    gather_sent(N_SELF)
+    gather_sent(N_KV)
+    sum_sent(N_CROSS)
+    share_finish(N_FQ)
 
     f_of = {0: s.f_q, 1: s.f_t}
     w_in = {0: s.m_in0, 1: s.m_in1}
@@ -750,7 +781,7 @@
             target[pl.ds(pair * 2, 2)] = back.reshape(2, query, z.model)
             send(pair)
             if kind == 0 and pair is not chip:
-                sum_forward("gfq")
+                sum_forward(N_GFQ)
             s.small[20 + kind : 21 + kind, :] += column_total(grad_up)
             out = dot_columns(hidden, w_out[kind][...]).astype(BF16)
             out = out.reshape(2, query, z.model)
@@ -783,20 +814,20 @@
                 )
 
     hops = iter((0, 1))
-    feed_forward(0, s.part_q, lambda pair: sum_copy("gfq", next(hops)).start())
+    feed_forward(0, s.part_q, lambda pair: sum_copy(N_GFQ, next(hops)).start())
     ring_pass(text_pair, 7)
-    share_finish("ft")
+    share_finish(N_FT)
     hops = iter((0, 1))
-    feed_forward(1, s.part_t, lambda pair: sum_copy("gft", next(hops)).start())
+    feed_forward(1, s.part_t, lambda pair: sum_copy(N_GFT, next(hops)).start())
     weight_terms(0)
-    share_sent("fq")
-    sum_forward("gft")
+    share_sent(N_FQ)
+    sum_forward(N_GFT)
     scatter_pass(query_pair, 0)
     weight_terms(1)
     scatter_pass(text_pair, 0)
-    sum_copy("out", 0).start()
-    sum_copy("out", 1).start()
-    scatter_passes(("in0", 1))
+    sum_copy(N_OUT, 0).start()
+    sum_copy(N_OUT, 1).start()
+    scatter_passes((N_IN0, 1))
 
     def own_back(total, after, grads, slot):
         normed, scale = norm_parts(after)
@@ -805,24 +836,24 @@
         s.small[slot : slot + 1, :] += column_total(grads)
         return grads.astype(F32) + norm_grad(normed, scale, vec(4), total)
 
-    grad_query = own_back(sum_finish("gfq"), s.after_query[...], grad_rows(0, rank), 8)
+    grad_query = own_back(sum_finish(N_GFQ), s.after_query[...], grad_rows(0, rank), 8)
     s.g_own[:query, :] = grad_query
     grad_query_low = grad_query.astype(BF16)
     s.x[rank, :query, :] = grad_query_low
     s.small[7:8, :] += column_total(grad_query_low)
-    share_start("gca")
-    sum_forward("out")
-    scatter_passes(("out0", 1), ("in1", "out1", 1))
-    grad_text = own_back(sum_finish("gft"), s.after_self[query:, :], grad_rows(1, rank), 9)
+    share_start(N_GCA)
+    sum_forward(N_OUT)
+    scatter_passes((N_OUT0, 1), (N_IN1, N_OUT1, 1))
+    grad_text = own_back(sum_finish(N_GFT), s.after_self[query:, :], grad_rows(1, rank), 9)
     s.g_own[query:, :] = grad_text
     grad_text_low = grad_text.astype(BF16)
     s.gsa_t[rank] = grad_text_low
     s.small[6:7, :] += column_total(grad_text_low)
-    share_start("gsat")
-    scatter_passes(("in0", "out0", 2))
-    share_forward("gca")
-    scatter_passes(("in1", 2))
-    share_finish("gca")
+    share_start(N_GSAT)
+    scatter_passes((N_IN0, N_OUT0, 2))
+    share_forward(N_GCA)
+    scatter_passes((N_IN1, 2))
+    share_finish(N_GCA)
 
     grad_mixed = dot(s.x[:, :query, :].reshape(queries_total, z.model), s.w_cross[:, WIDE:])
     s.goc[...] = grad_mixed.astype(BF16).reshape(s.goc.shape)
@@ -853,18 +884,18 @@
             s.gqc[slot] = mixed.astype(BF16)
         mixed = s.gqc[pl.ds(row * SLOTS, SLOTS)].reshape(query, WIDE)
         s.part_q[row] = dot_columns(mixed, s.w_cross[:, :WIDE]).astype(BF16)
-        send_pairs(step, ("gc",))
-
-    sum_sent("gfq")
+        send_pairs(step, (N_GC,))
+
+    sum_sent(N_GFQ)
     pl.loop(0, rows // 2)(cross_back)
-    sum_sent("gft")
-    sum_forward("gc")
-    scatter_passes(("out1", 2), ("in0", 3))
+    sum_sent(N_GFT)
+    sum_forward(N_GC)
+    scatter_passes((N_OUT1, 2), (N_IN0, 3))
     pl.loop(rows // 2, rows)(cross_back)
-    scatter_passes(("out0", 3), ("in1", "out1", 3))
+    scatter_passes((N_OUT0, 3), (N_IN1, N_OUT1, 3))
     s.small[18:19, :WIDE] += column_total(all_slots(s.gqc))
     low_half = lanes(128) < HEAD
-    gather_sent("cross")
+    gather_sent(N_CROSS)
     grad_cq = dot_rows(s.c[...].reshape(queries_total, z.model), all_slots(s.gqc))
     grad_co = dot_rows(s.x[:, :query, :].reshape(queries_total, z.model), all_slots(s.oc))
     s.m_cross[:, :128] = grad_cq[:, :128].astype(BF16)
@@ -872,16 +903,16 @@
     s.m_cross[:, 256:] = jnp.where(
         low_half, grad_cq[:, 128:], pltpu.roll(grad_co[:, 128:], HEAD, 1)
     ).astype(BF16)
-    scatter_start("cross")
-
-    after_ffn_sum = sum_finish("out")
+    scatter_start(N_CROSS)
+
+    after_ffn_sum = sum_finish(N_OUT)
     after_query_out = s.after_query[...] + after_ffn_sum[:query] + vec(8)
     after_text_out = s.after_self[query:, :] + after_ffn_sum[query:] + vec(9)
     put_stat(3, after_query_out, weight_query)
     put_stat(3, after_text_out, weight_text)
     s.gy[rank, :query, :] = after_query_out.astype(BF16)
     s.gy[rank, query:, :] = after_text_out.astype(BF16)
-    share_start("out")
+    share_start(N_OUT)
 
     def key_grad(image):
         slot = slot_of(image)
@@ -927,20 +958,20 @@
             for inner in range(2):
                 load_chunk(pair * 2 + inner + CHUNKS_HELD).start()
 
-    scatter_passes(("in0", 4))
+    scatter_passes((N_IN0, 4))
     features_start(key_grad)
-    share_forward("gsat")
-    scatter_passes(("out0", 4), ("in1", "out1", 4))
+    share_forward(N_GSAT)
+    scatter_passes((N_OUT0, 4), (N_IN1, N_OUT1, 4))
     pl.loop(0, chunk_count // 2)(features_pair)
     load_chunks()
     turned = s.turned[...].T
     s.m_kv[:, :128] = turned[:, :128].astype(BF16)
     s.m_kv[:, 256:] = turned[:, 128:].astype(BF16)
 
-    scatter_passes(("in0", 5))
-    scatter_forward("cross")
+    scatter_passes((N_IN0, 5))
+    scatter_forward(N_CROSS)
     features_start(value_grad)
-    cross_sum = sum_finish("gc")
+    cross_sum = sum_finish(N_GC)
     normed, scale = norm_parts(s.after_self[:query, :])
     s.small[2:3, :] += column_total(cross_sum * normed)
     s.small[3:4, :] += column_total(cross_sum)
@@ -949,10 +980,10 @@
     grad_query_low = grad_query.astype(BF16)
     s.f_q[rank] = grad_query_low
     s.small[6:7, :] += column_total(grad_query_low)
-    share_start("gsaq")
-    scatter_passes(("out0", "in1", "out1", 5))
-    share_forward("out")
-    scatter_passes(("in0", 6))
+    share_start(N_GSAQ)
+    scatter_passes((N_OUT0, N_IN1, N_OUT1, 5))
+    share_forward(N_OUT)
+    scatter_passes((N_IN0, 6))
     pl.loop(0, chunk_count // 2)(features_pair)
     s.small[19:20, :WIDE] += s.col_sum[...]
     turned = s.turned[...].T
@@ -960,13 +991,13 @@
     s.m_kv[:, 256:] = jnp.where(
         low_half, s.m_kv[:, 256:].astype(F32), pltpu.roll(turned[:, 128:], HEAD, 1)
     ).astype(BF16)
-    scatter_passes(("out0", 6))
-    scatter_start("kv")
-    scatter_passes(("in1", 6))
-    share_forward("gsaq")
-    scatter_passes(("out1", 6))
-    share_finish("gsat")
-    share_finish("gsaq")
+    scatter_passes((N_OUT0, 6))
+    scatter_start(N_KV)
+    scatter_passes((N_IN1, 6))
+    share_forward(N_GSAQ)
+    scatter_passes((N_OUT1, 6))
+    share_finish(N_GSAT)
+    share_finish(N_GSAQ)
 
     def self_back(step):
         row = send_order(step)
@@ -989,15 +1020,15 @@
         s.small[16:17, :WIDE] += column_total(grad_low[:, :WIDE])
         s.small[17:18, :WIDE] += column_total(grad_low[:, 2 * WIDE :])
         s.part_row[row] = dot_columns(grad_low, s.w_self[:, : 3 * WIDE]).astype(BF16)
-        send_pairs(step, ("gaq", "gat"))
-
-    sum_sent("out")
-    sum_sent("gc")
-    share_sent("gca")
+        send_pairs(step, (N_GAQ, N_GAT))
+
+    sum_sent(N_OUT)
+    sum_sent(N_GC)
+    share_sent(N_GCA)
     pl.loop(0, rows // 2)(self_back)
-    sum_forward("gaq")
-    sum_forward("gat")
-    scatter_passes(("in0", "out0", 7))
+    sum_forward(N_GAQ)
+    sum_forward(N_GAT)
+    scatter_passes((N_IN0, N_OUT0, 7))
     pl.loop(rows // 2, rows)(self_back)
 
     grads_all = [dot_rows(s.a[...], s.qkv[:, i * WIDE : (i + 1) * WIDE]) for i in range(3)]
@@ -1011,10 +1042,10 @@
         s.m_self[:, (4 + i) * 128 : (5 + i) * 128] = jnp.where(
             low_half, grads_all[2 * i][:, 128:], pltpu.roll(grads_all[2 * i + 1][:, 128:], HEAD, 1)
         ).astype(BF16)
-    scatter_start("self")
-    scatter_passes(("in1", 7))
-    scatter_forward("kv")
-    scatter_passes(("out1", 7))
+    scatter_start(N_SELF)
+    scatter_passes((N_IN1, 7))
+    scatter_forward(N_KV)
+    scatter_passes((N_OUT1, 7))
 
     def stream_back(name, at):
         total = sum_finish(name)
@@ -1024,11 +1055,11 @@
         grad = s.g_own[at, :] + norm_grad(normed, scale, vec(0), total)
         s.x[rank, at, :] = grad.astype(BF16)
 
-    stream_back("gaq", pl.ds(0, query))
-    share_start("sgq")
-    stream_back("gat", pl.ds(query, text))
-    share_start("sgt")
-    scatter_forward("self")
+    stream_back(N_GAQ, pl.ds(0, query))
+    share_start(N_SGQ)
+    stream_back(N_GAT, pl.ds(query, text))
+    share_start(N_SGT)
+    scatter_forward(N_SELF)
 
     def small_copy(source, hop, device):
         target = s.small_in.at[hop] if source is s.small else s.small_in.at[hop, pl.ds(0, 16)]
@@ -1042,18 +1073,18 @@
         s.small[:16, :] += s.small_in[hop, :16, :]
     item = small_copy(s.small, 2, across)
     item.start()
-    share_forward("sgq")
-    share_forward("sgt")
+    share_forward(N_SGQ)
+    share_forward(N_SGT)
     item.wait()
     s.small[...] += s.small_in[2]
     items = [small_copy(s.small, 2 + step, along(step)) for step in range(1, lines)]
     for item in items:
         item.start()
-    share_finish("out")
+    share_finish(N_OUT)
     store_out = pltpu.make_async_copy(s.gy, s.out_h, s.load_sem.at[3])
     store_out.start()
-    share_finish("sgq")
-    share_finish("sgt")
+    share_finish(N_SGQ)
+    share_finish(N_SGT)
     store_sg = pltpu.make_async_copy(s.x, s.sg_h, s.load_sem.at[4])
     store_sg.start()
     total = s.small[...]
@@ -1067,11 +1098,11 @@
         ring_scatter_sent(name)
     for item in items:
         item.wait_send()
-    gather_sent("vec")
-    for name in ("gaq", "gat"):
+    gather_sent(N_VEC)
+    for name in (N_GAQ, N_GAT):
         sum_sent(name)
     for name in SHARES:
-        if name not in ("fq", "gca"):
+        if name not in (N_FQ, N_GCA):
             share_sent(name)
     store_out.wait()
     store_sg.wait()
@@ -1124,7 +1155,7 @@
         fan = grad_in_w.shape[1]
         grad_in_w[index] = own_ffn[index * fan : (index + 1) * fan, :]
         grad_out_w[index] = own_ffn[(2 + index) * fan : (3 + index) * fan, :]
-    place, own = lax.axis_index("dp"), grad_vectors.shape[1]
+    place, own = lax.axis_index(N_DP), grad_vectors.shape[1]
     total = jnp.zeros(grad_vectors.shape, F32)
     for index in range(small.shape[1] // own):
         mine = small[: total.shape[0], index * own : (index + 1) * own]
@@ -1155,7 +1186,7 @@
     ffn_bias,
     out_grad,
 ):
-    count = lax.axis_size("dp")
+    count = lax.axis_size(N_DP)
     tokens, model = stream_in.shape
     width, hidden = self_qkv.shape[2], ffn_in.shape[2]
     fan, feat_fan = ffn_in.shape[1], cross_kv.shape[1]
@@ -1178,101 +1209,101 @@
     )
     lines = count // 2
 
-    operands = {
-        "image_of": image_index.reshape(-1),
-        "vectors": vectors,
-        "self_qkv": self_qkv,
-        "self_out": self_out,
-        "cross_q": cross_q,
-        "cross_kv": cross_kv,
-        "cross_out": cross_out,
-        "ffn_out": ffn_out.transpose(0, 2, 1),
-        "head_bias": head_bias,
-        "ffn_bias": ffn_bias,
-        "segment": text_segment,
-        "valid": text_valid,
-        "ffn_in": ffn_in,
-        "x_h": stream_in.reshape(rows, ROW_LEN, model),
-        "gy_h": out_grad.reshape(rows, ROW_LEN, model),
-        "feat_h": features.transpose(1, 0, 2).reshape(keys * images, feat),
-    }
+    operands = dict(
+        image_of=image_index.reshape(-1),
+        vectors=vectors,
+        self_qkv=self_qkv,
+        self_out=self_out,
+        cross_q=cross_q,
+        cross_kv=cross_kv,
+        cross_out=cross_out,
+        ffn_out=ffn_out.transpose(0, 2, 1),
+        head_bias=head_bias,
+        ffn_bias=ffn_bias,
+        segment=text_segment,
+        valid=text_valid,
+        ffn_in=ffn_in,
+        x_h=stream_in.reshape(rows, ROW_LEN, model),
+        gy_h=out_grad.reshape(rows, ROW_LEN, model),
+        feat_h=features.transpose(1, 0, 2).reshape(keys * images, feat),
+    )
     spaces = dict.fromkeys(operands, pltpu.VMEM) | {"image_of": pltpu.SMEM}
     spaces |= dict.fromkeys(("ffn_in", "x_h", "gy_h", "feat_h"), pl.ANY)
-    results = {
-        "out_h": ((rows, ROW_LEN, model), BF16),
-        "sg_h": ((rows, ROW_LEN, model), BF16),
-        "own_self": ((fan, 4 * width), F32),
-        "own_kv": ((feat_fan, 2 * width), F32),
-        "own_cross": ((fan, 2 * width), F32),
-        "own_ffn": ((4 * fan, hidden), F32),
-        "small_out": ((24, model), F32),
-    }
+    results = dict(
+        out_h=((rows, ROW_LEN, model), BF16),
+        sg_h=((rows, ROW_LEN, model), BF16),
+        own_self=((fan, 4 * width), F32),
+        own_kv=((feat_fan, 2 * width), F32),
+        own_cross=((fan, 2 * width), F32),
+        own_ffn=((4 * fan, hidden), F32),
+        small_out=((24, model), F32),
+    )
     chunk_rows = (keys + PADDED_KEYS - keys) * images
-    buffers = {
-        "w_vec": ((count * 16, 128), BF16),
-        "vecs": ((16, model), F32),
-        "bias": ((8, max(3 * WIDE, hidden)), F32),
-        "code": ((rows, ROW_LEN), F32),
-        "text_codes": ((rows, text, 1), F32),
-        "weight": ((text, 1), F32),
-        "m_self": ((model, 4 * width), BF16),
-        "m_kv": ((feat, 2 * width), BF16),
-        "m_cross": ((model, 2 * width), BF16),
-        "w_self": ((model, 4 * WIDE), BF16),
-        "w_kv": ((feat, 2 * WIDE), BF16),
-        "w_cross": ((model, 2 * WIDE), BF16),
-        "x": ((rows, ROW_LEN, model), BF16),
-        "x_own": ((ROW_LEN, model), BF16),
-        "gy": ((rows, ROW_LEN, model), BF16),
-        "a": ((tokens, model), BF16),
-        "qkv": ((tokens, 3 * WIDE), BF16),
-        "o": ((tokens, WIDE), BF16),
-        "p_self": ((rows, z.heads * ROW_LEN, ROW_LEN), BF16),
-        "c": ((rows, query, model), BF16),
-        "f_q": ((rows, query, model), BF16),
-        "f_t": ((rows, query, model), BF16),
-        "gsa_t": ((rows, query, model), BF16),
-        "qc": ((images, QUERIES, WIDE), BF16),
-        "gqc": ((images, QUERIES, WIDE), BF16),
-        "goc": ((images, QUERIES, WIDE), BF16),
-        "oc": ((images, QUERIES, WIDE), BF16),
-        "kv": ((images, PADDED_KEYS, 2 * WIDE), BF16),
-        "p_cross": ((images, z.heads * QUERIES, PADDED_KEYS), BF16),
-        "stage": ((WIDE // 128, PADDED_KEYS * images, 128), F32),
-        "turned": ((WIDE, feat), F32),
-        "col_sum": ((1, WIDE), F32),
-        "chunk": ((CHUNKS_HELD, CHUNK, feat), BF16),
-        "tail": ((images * keys % CHUNK, feat), BF16),
-        "hid": ((images, QUERIES, hidden), BF16),
-        "gu": ((images, QUERIES, hidden), BF16),
-        "part_row": ((rows, ROW_LEN, model), BF16),
-        "part_q": ((rows, query, model), BF16),
-        "part_t": ((rows, query, model), BF16),
-        "after_self": ((ROW_LEN, model), F32),
-        "after_query": ((query, model), F32),
-        "g_own": ((ROW_LEN, model), F32),
-        "small": ((24, model), F32),
-        "small_in": ((2 + lines, 24, model), F32),
-    }
-    for name in ("in0", "in1", "out0", "out1"):
+    buffers = dict(
+        w_vec=((count * 16, 128), BF16),
+        vecs=((16, model), F32),
+        bias=((8, max(3 * WIDE, hidden)), F32),
+        code=((rows, ROW_LEN), F32),
+        text_codes=((rows, text, 1), F32),
+        weight=((text, 1), F32),
+        m_self=((model, 4 * width), BF16),
+        m_kv=((feat, 2 * width), BF16),
+        m_cross=((model, 2 * width), BF16),
+        w_self=((model, 4 * WIDE), BF16),
+        w_kv=((feat, 2 * WIDE), BF16),
+        w_cross=((model, 2 * WIDE), BF16),
+        x=((rows, ROW_LEN, model), BF16),
+        x_own=((ROW_LEN, model), BF16),
+        gy=((rows, ROW_LEN, model), BF16),
+        a=((tokens, model), BF16),
+        qkv=((tokens, 3 * WIDE), BF16),
+        o=((tokens, WIDE), BF16),
+        p_self=((rows, z.heads * ROW_LEN, ROW_LEN), BF16),
+        c=((rows, query, model), BF16),
+        f_q=((rows, query, model), BF16),
+        f_t=((rows, query, model), BF16),
+        gsa_t=((rows, query, model), BF16),
+        qc=((images, QUERIES, WIDE), BF16),
+        gqc=((images, QUERIES, WIDE), BF16),
+        goc=((images, QUERIES, WIDE), BF16),
+        oc=((images, QUERIES, WIDE), BF16),
+        kv=((images, PADDED_KEYS, 2 * WIDE), BF16),
+        p_cross=((images, z.heads * QUERIES, PADDED_KEYS), BF16),
+        stage=((WIDE // 128, PADDED_KEYS * images, 128), F32),
+        turned=((WIDE, feat), F32),
+        col_sum=((1, WIDE), F32),
+        chunk=((CHUNKS_HELD, CHUNK, feat), BF16),
+        tail=((images * keys % CHUNK, feat), BF16),
+        hid=((images, QUERIES, hidden), BF16),
+        gu=((images, QUERIES, hidden), BF16),
+        part_row=((rows, ROW_LEN, model), BF16),
+        part_q=((rows, query, model), BF16),
+        part_t=((rows, query, model), BF16),
+        after_self=((ROW_LEN, model), F32),
+        after_query=((query, model), F32),
+        g_own=((ROW_LEN, model), F32),
+        small=((24, model), F32),
+        small_in=((2 + lines, 24, model), F32),
+    )
+    for name in (N_IN0, N_IN1, N_OUT0, N_OUT1):
         buffers["m_" + name] = ((model, hidden), BF16)
-        buffers["r_" + name] = ((count - 1, fan, hidden), BF16)
-    for name in ("selfq", "selft", "out", "cross", "gft", "gfq"):
-        block = (ROW_LEN if name == "out" else query, model)
-        buffers["pin_" + name] = ((2, *block), BF16)
-        buffers["fin_" + name] = (block, BF16)
+        buffers[N_R + name] = ((count - 1, fan, hidden), BF16)
+    for name in (N_SELFQ, N_SELFT, N_OUT, N_CROSS, N_GFT, N_GFQ):
+        block = (ROW_LEN if name == N_OUT else query, model)
+        buffers[N_PIN + name] = ((2, *block), BF16)
+        buffers[N_FIN + name] = (block, BF16)
     buffers["half_row"] = ((ROW_LEN, model), BF16)
     buffers["half"] = ((2, query, model), BF16)
     for name in TERMS:
-        high = feat_fan if name == "kv" else fan
-        across = (4 if name == "self" else 2) * width
-        buffers["y_" + name] = ((lines, high, across), BF16)
-        buffers["z_" + name] = ((lines - 1, high, across), BF16)
-    semaphores = {
-        "own_sem": (2,),
-        "load_sem": (5,),
-        "chunk_sem": (CHUNKS_HELD,),
-    }
+        high = feat_fan if name == N_KV else fan
+        across = (4 if name == N_SELF else 2) * width
+        buffers[N_Y + name] = ((lines, high, across), BF16)
+        buffers[N_Z + name] = ((lines - 1, high, across), BF16)
+    semaphores = dict(
+        own_sem=(2,),
+        load_sem=(5,),
+        chunk_sem=(CHUNKS_HELD,),
+    )
     for name in ("gl_send", "gl_recv", "gs_send", "gs_recv"):
         semaphores[name] = (len(PIECES), lines)
     for name in ("ss_send", "ss_recv", "sl_send", "sl_recv"):
@@ -1419,11 +1450,11 @@
 
 
 def heads_total(partial_terms):
-    return lax.psum(partial_terms, "mp")
+    return lax.psum(partial_terms, N_MP)
 
 
 def inputs_total(partial_terms):
-    return lax.psum(partial_terms, "mp")
+    return lax.psum(partial_terms, N_MP)
 
 
 def ffn_forward(normed_low, weight_up, bias_up, weight_down):
@@ -1459,14 +1490,14 @@
     out_grad,
 ):
     gathered = (
-        lax.all_gather(self_qkv, "dp", axis=1, tiled=True),
-        lax.all_gather(self_out, "dp", axis=1, tiled=True),
-        lax.all_gather(cross_q, "dp", axis=0, tiled=True),
-        lax.all_gather(cross_kv, "dp", axis=1, tiled=True),
-        lax.all_gather(cross_out, "dp", axis=1, tiled=True),
-        lax.all_gather(ffn_in, "dp", axis=1, tiled=True),
-        lax.all_gather(ffn_out, "dp", axis=2, tiled=True),
-        lax.all_gather(vectors, "dp", axis=1, tiled=True),
+        lax.all_gather(self_qkv, N_DP, axis=1, tiled=True),
+        lax.all_gather(self_out, N_DP, axis=1, tiled=True),
+        lax.all_gather(cross_q, N_DP, axis=0, tiled=True),
+        lax.all_gather(cross_kv, N_DP, axis=1, tiled=True),
+        lax.all_gather(cross_out, N_DP, axis=1, tiled=True),
+        lax.all_gather(ffn_in, N_DP, axis=1, tiled=True),
+        lax.all_gather(ffn_out, N_DP, axis=2, tiled=True),
+        lax.all_gather(vectors, N_DP, axis=1, tiled=True),
     )
     qkv_w, proj_w, cq_w, ckv_w, cproj_w, up_w, down_w, vector_low = gathered
     vecs = vector_low.astype(jnp.float32)
@@ -1560,14 +1591,14 @@
     )
     out_low = round_low(after_ffn)
     regathered = (
-        lax.all_gather(self_qkv, "dp", axis=1, tiled=True),
-        lax.all_gather(self_out, "dp", axis=1, tiled=True),
-        lax.all_gather(cross_q, "dp", axis=0, tiled=True),
-        lax.all_gather(cross_kv, "dp", axis=1, tiled=True),
-        lax.all_gather(cross_out, "dp", axis=1, tiled=True),
-        lax.all_gather(ffn_in, "dp", axis=1, tiled=True),
-        lax.all_gather(ffn_out, "dp", axis=2, tiled=True),
-        lax.all_gather(vectors, "dp", axis=1, tiled=True),
+        lax.all_gather(self_qkv, N_DP, axis=1, tiled=True),
+        lax.all_gather(self_out, N_DP, axis=1, tiled=True),
+        lax.all_gather(cross_q, N_DP, axis=0, tiled=True),
+        lax.all_gather(cross_kv, N_DP, axis=1, tiled=True),
+        lax.all_gather(cross_out, N_DP, axis=1, tiled=True),
+        lax.all_gather(ffn_in, N_DP, axis=1, tiled=True),
+        lax.all_gather(ffn_out, N_DP, axis=2, tiled=True),
+        lax.all_gather(vectors, N_DP, axis=1, tiled=True),
     )
     qkv_w, proj_w, cq_w, ckv_w, cproj_w, up_w, down_w, vector_low = regathered
     vecs = vector_low.astype(jnp.float32)
@@ -1673,14 +1704,14 @@
     grad_up = jnp.stack([in_query, in_text])
     grad_down = jnp.stack([down_query, down_text])
     owned = (
-        lax.psum_scatter(grad_qkv, "dp", scatter_dimension=1, tiled=True),
-        lax.psum_scatter(grad_proj, "dp", scatter_dimension=1, tiled=True),
-        lax.psum_scatter(grad_cq, "dp", scatter_dimension=0, tiled=True),
-        lax.psum_scatter(grad_ckv, "dp", scatter_dimension=1, tiled=True),
-        lax.psum_scatter(grad_cproj, "dp", scatter_dimension=1, tiled=True),
-        lax.psum_scatter(grad_up, "dp", scatter_dimension=1, tiled=True),
-        lax.psum_scatter(grad_down, "dp", scatter_dimension=2, tiled=True),
-        lax.psum_scatter(grad_vectors, "dp", scatter_dimension=1, tiled=True),
+        lax.psum_scatter(grad_qkv, N_DP, scatter_dimension=1, tiled=True),
+        lax.psum_scatter(grad_proj, N_DP, scatter_dimension=1, tiled=True),
+        lax.psum_scatter(grad_cq, N_DP, scatter_dimension=0, tiled=True),
+        lax.psum_scatter(grad_ckv, N_DP, scatter_dimension=1, tiled=True),
+        lax.psum_scatter(grad_cproj, N_DP, scatter_dimension=1, tiled=True),
+        lax.psum_scatter(grad_up, N_DP, scatter_dimension=1, tiled=True),
+        lax.psum_scatter(grad_down, N_DP, scatter_dimension=2, tiled=True),
+        lax.psum_scatter(grad_vectors, N_DP, scatter_dimension=1, tiled=True),
     )
     grad_heads = jnp.stack(
         [
@@ -1692,7 +1723,7 @@
     )
     grad_hidden_bias = jnp.stack([hidden_bias_query, hidden_bias_text])
     grad_heads, grad_hidden_bias, stream_stats = lax.psum(
-        (grad_heads, grad_hidden_bias, stream_stats), "dp"
+        (grad_heads, grad_hidden_bias, stream_stats), N_DP
     )
     stream_rms = jnp.sqrt(stream_stats[:4] / (stream_stats[4] * model_width))
     return (
@@ -1714,43 +1745,43 @@
 
 def solution(mesh):
     in_specs = (
-        P("dp", None),
-        P("dp", None, None),
-        P("dp", None),
-        P("dp", None),
-        P("dp", None),
-        P(None, "dp", "mp"),
-        P("mp", "dp"),
-        P("dp", "mp"),
-        P(None, "dp", "mp"),
-        P("mp", "dp"),
-        P(None, "dp", "mp"),
-        P(None, "mp", "dp"),
-        P(None, "dp"),
-        P(None, "mp"),
-        P(None, "mp"),
-        P("dp", None),
+        P(N_DP, None),
+        P(N_DP, None, None),
+        P(N_DP, None),
+        P(N_DP, None),
+        P(N_DP, None),
+        P(None, N_DP, N_MP),
+        P(N_MP, N_DP),
+        P(N_DP, N_MP),
+        P(None, N_DP, N_MP),
+        P(N_MP, N_DP),
+        P(None, N_DP, N_MP),
+        P(None, N_MP, N_DP),
+        P(None, N_DP),
+        P(None, N_MP),
+        P(None, N_MP),
+        P(N_DP, None),
     )
     out_specs = (
-        P("dp", None),
-        P("dp", None),
-        P(None, "dp", "mp"),
-        P("mp", "dp"),
-        P("dp", "mp"),
-        P(None, "dp", "mp"),
-        P("mp", "dp"),
-        P(None, "dp", "mp"),
-        P(None, "mp", "dp"),
-        P(None, "dp"),
-        P(None, "mp"),
-        P(None, "mp"),
+        P(N_DP, None),
+        P(N_DP, None),
+        P(None, N_DP, N_MP),
+        P(N_MP, N_DP),
+        P(N_DP, N_MP),
+        P(None, N_DP, N_MP),
+        P(N_MP, N_DP),
+        P(None, N_DP, N_MP),
+        P(None, N_MP, N_DP),
+        P(None, N_DP),
+        P(None, N_MP),
+        P(None, N_MP),
         P(),
     )
 
     def apply(*args):
-        fan = args[5].shape[1] // mesh.shape["dp"]
-        whole_tiles = fan % 16 == 0 and fan <= 128 and mesh.shape["dp"] % 2 == 0
-        run = layer if whole_tiles and mesh.shape["mp"] == 4 else body
+        fan = args[5].shape[1] // mesh.shape[N_DP]
+        whole_tiles = fan % 16 == 0 and fan <= 128 and mesh.shape[N_DP] % 2 == 0
+        run = layer if whole_tiles and mesh.shape[N_MP] == 4 else body
         return jax.shard_map(
             run, mesh=mesh, in_specs=in_specs, out_specs=out_specs, check_vma=False
         )(*args)

time: 205 us -> 205 us (level)
  no operation moved by 1% of the time
where the time goes in v5:
time: 205 us; the launch traced here: 204 us
  Pallas kernels  203 us (99%)
    pallas_call x1, Pallas kernels, layer(): pl.pallas_call(functools.partial(layer_kernel, names, z), out_shape=[jax....  198 us
    pallas_call x1, Pallas kernels, layer(): pl.pallas_call(finish_kernel, out_shape=[jax.ShapeDtypeStruct(*item) for...  5.7 us

profile of v5, /device:TPU:0, one launch (start us, length us, event | category | flops | bytes accessed | tf_op | source)
XLA Modules:
  0.0 204.2 jit_solution(2955684064155526768)
XLA Ops:
  0.7 197.7 %shard_map.255 = (bf16[4,256,768]{2,1,0:T(8,128)(2,1)}, bf16[4,256,768]{2,1,0:T(8,128)(2,1)}, f32[96,768]{1,0:T(8,128)}, f32[176,384]{1,0:T(8,128)}, f32[96,384]...) custom-call(s32[16]{0:T(128)} %bitcast.15, bf16[10,96]{1,0:T(8,128)(2,1)} %refs_1_.1, bf16[3,96,192]{2,1,0:T(8,128)(2,1)} %refs_2_.1, ...), custom_call_target="tpu_custom_call" | custom-call | tf_op jit(solution)/shard_map/pallas_call | solution.py:1319
  198.4 5.7 %shard_map.256 = (bf16[4,256,768]{2,1,0:T(8,128)(2,1)}, f32[4,256,768]{2,1,0:T(8,128)}, f32[3,96,192]{2,1,0:T(8,128)}, f32[192,96]{1,0:T(8,128)}, f32[96,192]{1,...) custom-call(bf16[4,256,768]{2,1,0:T(8,128)(2,1)} %get-tuple-element., ...), custom_call_target="tpu_custom_call" | custom-call | tf_op jit(solution)/shard_map/pallas_call | solution.py:1348
